TPU v7x, 32 devices: a whole 2x2x4 slice. The times are simulated.
32 devices in a mesh: tm: 16 (over z, y, x), det: 2 (over core).
Axes of the slice: x: 2, y: 2, z: 4, core: 2. Of those that a mesh axis runs over, the one named last changes fastest.
Arguments:
- offset_coeffs: float32 [16, 32], P('det', 'tm'), may hold values from -6 to 6
- leftover_error: float32 [16, 32], P('det', 'tm'), may hold values from -22 to 22
- search_vector: float32 [16, 32], P('det', 'tm'), may hold values from -22 to 22
- node_lattice_offset: int32 [16], P('det'), may hold values from 0 to 1023
- sky_cell_in_patch: int32 [16, 32768], P('det', 'tm'), may hold values from 0 to 127
- analyser_reading_phase: float32 [16, 32768], P('det', 'tm'), may hold values from -3.140625 to 3.140625
- segment_sky_patch: int32 [16, 256], P('det', 'tm'), may hold values from 0 to 16383, as said below
Outputs:
- fresh_offset_coeffs: float32 [16, 32], P('det', 'tm')
- fresh_leftover_error: float32 [16, 32], P('det', 'tm')
- fresh_search_vector: float32 [16, 32], P('det', 'tm')
Inputs may be any that keep to these rules, and one draw needn't show every extreme that they name: `segment_sky_patch`: tile t belongs to owner t // 1024. Among the blocks of one device (8 detectors, one time span), at most 16 lie in tiles of one owner, and on every device some owner holds exactly 16 of them.
All inputs are finite; a program needn't handle non-finite values.
Results may differ from a plain program's by a relative error of at most 0.0001.
Values sent between devices are 32-bit elements; how exact they have to be, the bound alone decides.
No kernel may reach another device: no remote copies, remote signals or barrier semaphores. Data moves between devices by JAX's collectives and lax.ppermute only.
A program may use at most 64 MiB of HBM per device.

v0:
```python
import math

import jax
import jax.numpy as jnp
from jax import lax
from jax.sharding import PartitionSpec as P

PIX_OWN = 131072


MAP_PRIOR = 1.0
BASE_PRIOR = 0.1
LANES = 128


def padded_2(cells, sides, width):
    for axis, dim in sides:
        count = lax.axis_size(axis)
        head = lax.slice_in_dim(cells, 0, width, axis=dim)
        tail = lax.slice_in_dim(cells, cells.shape[dim] - width, cells.shape[dim], axis=dim)
        cells = jnp.concatenate(
            [
                lax.ppermute(tail, axis, [(i, (i + 1) % count) for i in range(count)]),
                cells,
                lax.ppermute(head, axis, [((i + 1) % count, i) for i in range(count)]),
            ],
            axis=dim,
        )
    return cells


def spline_weights(fraction):
    square = fraction * fraction
    cube = square * fraction
    first = (1.0 - fraction) * (1.0 - fraction) * (1.0 - fraction) / 6.0
    second = (3.0 * cube - 6.0 * square + 4.0) / 6.0
    third = (-3.0 * cube + 3.0 * square + 3.0 * fraction + 1.0) / 6.0
    fourth = cube / 6.0
    return (first, second, third, fourth)


def solve_pixels(sums):
    total_signal, signal_cos, signal_sin, hit_count, cos_sum, sin_sum, cos_cos, cos_sin, sin_sin = (
        sums
    )
    stokes_i = hit_count + MAP_PRIOR
    stokes_q = cos_cos + MAP_PRIOR
    stokes_u = sin_sin + MAP_PRIOR
    minor_one = stokes_q * stokes_u - cos_sin * cos_sin
    minor_two = sin_sum * cos_sin - cos_sum * stokes_u
    minor_three = cos_sum * cos_sin - sin_sum * stokes_q
    minor_four = stokes_i * stokes_u - sin_sum * sin_sum
    minor_five = cos_sum * sin_sum - stokes_i * cos_sin
    minor_six = stokes_i * stokes_q - cos_sum * cos_sum
    determinant = stokes_i * minor_one + cos_sum * minor_two + sin_sum * minor_three
    intensity = (
        minor_one * total_signal + minor_two * signal_cos + minor_three * signal_sin
    ) / determinant
    polar_q = (
        minor_two * total_signal + minor_four * signal_cos + minor_five * signal_sin
    ) / determinant
    polar_u = (
        minor_three * total_signal + minor_five * signal_cos + minor_six * signal_sin
    ) / determinant
    return (intensity, polar_q, polar_u)


def solve_tiles(sums):
    parts = tuple((sums[:, column] for column in range(9)))
    return jnp.stack(solve_pixels(parts), axis=1)


def place_rows(rows, labels, owner_tiles):
    targets = labels.astype(jnp.int32)
    targets = jnp.where(targets < 0, owner_tiles, targets)
    return jnp.zeros((owner_tiles + 1, 9, LANES), jnp.float32).at[targets].add(rows)[:owner_tiles]


def combine_maps(rows, labels, owner_tiles):
    partial_value = place_rows(rows, labels, owner_tiles)
    totals = lax.psum(partial_value, "det")
    return solve_tiles(totals)


def block_groups(block_count):
    return math.gcd(block_count, 64)


def bin_blocks(entries, offsets):
    block_count, channels = (entries.shape[0], entries.shape[1])
    group_width = block_groups(block_count)
    lane_ids = jnp.arange(LANES, dtype=jnp.int32)

    def bin_one_group(input_arrays):
        indicator_matrix = (input_arrays[1][:, :, None] == lane_ids[None, None, :]).astype(
            jnp.float32
        )
        return jnp.einsum(
            "zte,zeh->zth", input_arrays[0], indicator_matrix, precision=lax.Precision.HIGHEST
        )

    binned = lax.map(
        bin_one_group,
        (
            entries.reshape(block_count // group_width, group_width, channels, LANES),
            offsets.reshape(block_count // group_width, group_width, LANES),
        ),
    )
    return binned.reshape(block_count, channels, LANES)


def read_blocks(tile_maps, offsets):
    block_count, channels = (tile_maps.shape[0], tile_maps.shape[1])
    group_width = block_groups(block_count)
    lane_ids = jnp.arange(LANES, dtype=jnp.int32)

    def read_one_group(input_arrays):
        indicator_matrix = (input_arrays[1][:, :, None] == lane_ids[None, None, :]).astype(
            jnp.float32
        )
        return jnp.einsum(
            "rhe,roe->rho", input_arrays[0], indicator_matrix, precision=lax.Precision.HIGHEST
        )

    values_read = lax.map(
        read_one_group,
        (
            tile_maps.reshape(block_count // group_width, group_width, channels, LANES),
            offsets.reshape(block_count // group_width, group_width, LANES),
        ),
    )
    return values_read.reshape(block_count, channels, LANES)


def pixel_sums(stream_blocks, cos_blocks, sin_blocks):
    ones = jnp.ones_like(cos_blocks)
    return jnp.stack(
        [
            stream_blocks,
            stream_blocks * cos_blocks,
            stream_blocks * sin_blocks,
            ones,
            cos_blocks,
            sin_blocks,
            cos_blocks * cos_blocks,
            cos_blocks * sin_blocks,
            sin_blocks * sin_blocks,
        ],
        axis=1,
    )


def body(
    offset_coeffs,
    leftover_error,
    search_vector,
    node_lattice_offset,
    sky_cell_in_patch,
    analyser_reading_phase,
    segment_sky_patch,
):
    ranks = lax.axis_size("tm")
    tm_index = lax.axis_index("tm")
    det_count, samples = analyser_reading_phase.shape
    node_portion = offset_coeffs.shape[1]
    spacing = samples // node_portion
    width_ext = node_portion + 4
    times = tm_index * samples + jnp.arange(samples, dtype=jnp.int32)
    shifted = times[None, :] - node_lattice_offset[:, None]
    interval = jnp.floor_divide(shifted, spacing)
    fraction = (shifted - interval * spacing).astype(jnp.float32) / spacing
    weights = spline_weights(fraction)
    local_knot = interval - tm_index * node_portion
    columns = []
    for column in range(width_ext):
        weight_col = jnp.zeros_like(fraction)
        for term in range(4):
            weight_col = weight_col + jnp.where(local_knot + term + 1 == column, weights[term], 0.0)
        columns.append(weight_col)
    extended = padded_2(search_vector, (("tm", 1),), 2)
    stream = jnp.zeros_like(fraction)
    for column in range(width_ext):
        stream = stream + columns[column] * extended[:, column : column + 1]
    cosine = jnp.cos(2.0 * analyser_reading_phase)
    sine = jnp.sin(2.0 * analyser_reading_phase)
    block_count = segment_sky_patch.size
    offsets = sky_cell_in_patch.reshape(block_count, LANES)
    stream_blocks = stream.reshape(block_count, LANES)
    cos_blocks = cosine.reshape(block_count, LANES)
    sin_blocks = sine.reshape(block_count, LANES)
    tiles = segment_sky_patch.reshape(block_count)
    owner_tiles = PIX_OWN // LANES
    owners = tiles // owner_tiles
    local_tiles = tiles - owners * owner_tiles
    capacity = max(2, 2 * block_count // ranks)
    slot_total = ranks * capacity
    member = (owners[:, None] == jnp.arange(ranks, dtype=jnp.int32)[None, :]).astype(jnp.int32)
    earlier = jnp.cumsum(member, axis=0) - member
    slots = owners * capacity + jnp.sum(earlier * member, axis=1)
    labels = (
        jnp.full((slot_total,), -1.0, jnp.float32).at[slots].set(local_tiles.astype(jnp.float32))
    )
    labels = labels.reshape(ranks, capacity)
    binned = bin_blocks(pixel_sums(stream_blocks, cos_blocks, sin_blocks), offsets)
    outgoing = jnp.zeros((slot_total, 9, LANES), jnp.float32).at[slots].set(binned)
    arrived, arrived_labels = (
        lax.all_to_all(
            outgoing.reshape(ranks, capacity, 9, LANES),
            "tm",
            split_axis=0,
            concat_axis=0,
            tiled=True,
        ),
        lax.all_to_all(labels, "tm", split_axis=0, concat_axis=0, tiled=True),
    )
    flat_labels = arrived_labels.reshape(-1)
    targets = flat_labels.astype(jnp.int32)
    targets = jnp.where(targets < 0, owner_tiles, targets)
    solved = combine_maps(arrived.reshape(slot_total, 9, LANES), flat_labels, owner_tiles)
    padded = jnp.concatenate([solved, jnp.zeros((1, 3, LANES), jnp.float32)], axis=0)
    returned = padded[targets].reshape(ranks, capacity, 3, LANES)
    received = lax.all_to_all(returned, "tm", split_axis=0, concat_axis=0, tiled=True)
    own_maps = received.reshape(slot_total, 3, LANES)[slots]
    values_read = read_blocks(own_maps, offsets)
    projected = values_read[:, 0] + cos_blocks * values_read[:, 1] + sin_blocks * values_read[:, 2]
    cleaned = stream - projected.reshape(det_count, samples)
    gathered = jnp.stack(
        [jnp.sum(columns[column] * cleaned, axis=1) for column in range(width_ext)], axis=1
    )
    rims = jnp.concatenate([gathered[:, :2], gathered[:, width_ext - 2 :]], axis=1)
    neighbours = padded_2(rims, (("tm", 1),), 2)
    owned = gathered[:, 2 : width_ext - 2]
    owned = owned.at[:, :2].add(neighbours[:, :2])
    owned = owned.at[:, node_portion - 2 :].add(neighbours[:, 6:])
    image = owned / spacing + BASE_PRIOR * search_vector
    norm_old, curvature, cross_term, image_square = lax.psum(
        (
            jnp.sum(leftover_error * leftover_error),
            jnp.sum(search_vector * image),
            jnp.sum(leftover_error * image),
            jnp.sum(image * image),
        ),
        ("tm", "det"),
    )
    stride_factor = norm_old / curvature
    fresh_leftover_error = leftover_error - stride_factor * image
    norm_new = (
        norm_old - 2.0 * stride_factor * cross_term + stride_factor * stride_factor * image_square
    )
    fresh_offset_coeffs = offset_coeffs + stride_factor * search_vector
    fresh_search_vector = fresh_leftover_error + norm_new / norm_old * search_vector
    return (fresh_offset_coeffs, fresh_leftover_error, fresh_search_vector)


def solution(mesh):
    return jax.shard_map(
        body,
        mesh=mesh,
        in_specs=(
            P("det", "tm"),
            P("det", "tm"),
            P("det", "tm"),
            P("det"),
            P("det", "tm"),
            P("det", "tm"),
            P("det", "tm"),
        ),
        out_specs=(P("det", "tm"), P("det", "tm"), P("det", "tm")),
        check_vma=False,
    )
```

profile of v0, /device:TPU:0, one launch (start us, length us, event | category | flops | bytes accessed | tf_op | source)
XLA Modules:
  0.0 247.7 jit_solution(8191328043365047832)
XLA Ops:
  7.2 3.0 %collective-permute-start = (f32[8,2]{0,1:T(2,128)}, f32[8,2]{0,1:T(2,128)S(1)}, u32[]{:S(2)}, u32[]{:S(2)}) collective-permute-start(f32[8,2]{0,1:T(2,128)} %param.21), channel_id=1, source_target_pairs={{0,2},{2,4},{4,6},{6,8},{8,10},{10,12},{12,14},{14,16},{16,18},{18... | collective-permute-start | bytes 200 | tf_op jit(solution)/shard_map/ppermute | solution.py:23
  10.2 4.1 %collective-permute-start.1 = (f32[8,2]{0,1:T(2,128)}, f32[8,2]{0,1:T(2,128)S(1)}, u32[]{:S(2)}, u32[]{:S(2)}) collective-permute-start(f32[8,2]{0,1:T(2,128)} %param.21), channel_id=1, source_target_pairs={{2,0},{4,2},{6,4},{8,6},{10,8},{12,10},{14,12},{16,14},{18,16},{20... | collective-permute-start | bytes 200 | tf_op jit(solution)/shard_map/ppermute | solution.py:25
  14.2 0.8 reshape.984
  15.0 0.8 reshape.983
  15.9 0.2 reduce_window_sum.11
  16.0 0.2 select_reduce_fusion
  16.2 1.0 scatter_custom_fusion
  17.2 0.7 all_to_all.12
  17.9 3.5 %all-to-all-start = ((f32[16,1,16]{2,1,0:T(1,128)}), f32[16,1,16]{2,1,0:T(1,128)S(1)}, u32[]{:S(2)}, u32[]{:S(2)}) async-start(f32[16,1,16]{2,1,0:T(1,128)} %all_to_all.12), calls=%async_computation | async-start | bytes 16384 | tf_op jit(solution)/shard_map/all_to_all | solution.py:214
  21.4 0.8 slice_reduce_fusion.6
  22.2 1.1 multiply_cosine_fusion
  23.2 0.1 reshape.985
  23.5 0.1 mul.831
  23.7 0.1 mul.836
  23.8 0.1 reshape.986
  23.9 0.7 sub.231
  24.8 0.1 sub.233
  24.8 0.9 reshape_reshape.4
  25.7 0.1 mul.819
  25.9 0.1 mul.821
  26.1 0.1 mul.826
  26.2 0.1 mul.839
  26.4 0.1 mul.841
  26.6 0.1 mul.846
  26.7 2.9 %fusion.62 = (f32[2,64,1,128]{3,2,1,0:T(1,128)S(1)}, f32[2,64,1,128]{3,2,1,0:T(1,128)S(1)}, f32[2,64,1,128]{3,2,1,0:T(1,128)S(1)}, f32[2,64,1,128]{3,2,1,0:T(1,128)S(1)}) fusion(f32[2,64,1,128]{3,2,1,0:T(1,128)S(1)} %reshape.985, f32[2,64,1,128]{3,2,1,0:T(1,128)S(1)} %reshape.986, f32[2,64]{1,0:T(2,128)S(1)} %mul.846, f32[2,64]{1,0:T(2,128)S(1)} %mul.841, ...), kind=kLoop, calls=%fused_computation.190 | loop fusion | flops 2031616 | bytes 462340 | tf_op jit(solution)/shard_map/mul | solution.py:146
  29.8 1.0 stack.39
  30.7 7.4 %while.26 = (s32[]{:T(128)}, f32[2,64,9,128]{3,2,1,0:T(8,128)S(1)}, f32[2,64,9,128]{3,2,1,0:T(8,128)S(1)}, s32[2,64,128]{2,1,0:T(8,128)S(1)}, s32[]{:T(128)}) while((s32[]{:T(128)}, f32[2,64,9,128]{3,2,1,0:T(8,128)S(1)}, f32[2,64,9,128]{3,2,1,0:T(8,128)S(1)}, s32[2,64,128]{2,1,0:T(8,128)S(1)}, s32[]{:T(128)}) %tuple.90), condition=%wide.region_6.7_spmd.clone, body=%wide.region_5.6_spmd.clone.sunk | while | flops 114294784 | bytes 1147969 | solution.py:102
  30.8 3.7 %fusion.69 = f32[2,64,9,128]{3,2,1,0:T(8,128)S(1)} fusion(f32[2,64,9,128]{3,2,1,0:T(8,128)S(1)} %get-tuple-element.248, s32[]{:T(128)} %get-tuple-element.247, s32[64,128]{1,0:T(8,128)S(1)} %dynamic-slice_bitcast_fusion.4, f32[2,64,9,128]{3,2,1,0:T(8,128)S(1)} %get-tuple-element.254), kind=kOutput, calls=%fused_computation.11.clone.1 | convolution fusion | flops 114294784 | bytes 1082368 | tf_op jit(solution)/shard_map/while/body/eval_jaxpr/zte,zeh->zth/dot_general | solution.py:98
  34.5 3.7 %fusion.69 = f32[2,64,9,128]{3,2,1,0:T(8,128)S(1)} fusion(f32[2,64,9,128]{3,2,1,0:T(8,128)S(1)} %get-tuple-element.248, s32[]{:T(128)} %get-tuple-element.247, s32[64,128]{1,0:T(8,128)S(1)} %dynamic-slice_bitcast_fusion.4, f32[2,64,9,128]{3,2,1,0:T(8,128)S(1)} %get-tuple-element.254), kind=kOutput, calls=%fused_computation.11.clone.1 | convolution fusion | flops 114294784 | bytes 1082368 | tf_op jit(solution)/shard_map/while/body/eval_jaxpr/zte,zeh->zth/dot_general | solution.py:98
  38.2 0.1 broadcast_in_dim.76
  38.3 4.3 %scatter_fusion = f32[256,9,128]{2,1,0:T(8,128)S(1)} fusion(f32[256,9,128]{2,1,0:T(8,128)S(1)} %broadcast_in_dim.76, s32[128]{0:T(128)S(1)} %fusion.57, f32[128,9,128]{2,1,0:T(8,128)S(1)} %bitcast.71), kind=kCustom, calls=%fused_computation.3 | custom fusion | bytes 1769984 | tf_op jit(solution)/shard_map/scatter | solution.py:205
  42.7 1.4 copy.25
  44.0 6.9 %all-to-all-start.1 = ((f32[16,16,9,128]{3,1,2,0:T(8,128)}), f32[16,16,9,128]{3,1,2,0:T(8,128)S(1)}, u32[]{:S(2)}, u32[]{:S(2)}) async-start(f32[16,16,9,128]{3,1,2,0:T(8,128)} %copy.25), calls=%async_computation.1 | async-start | bytes 2359296 | tf_op jit(solution)/shard_map/all_to_all | solution.py:207
  51.1 26.2 %all-to-all-done.1 = f32[16,16,9,128]{3,1,2,0:T(8,128)S(1)} async-done(((f32[16,16,9,128]{3,1,2,0:T(8,128)}), f32[16,16,9,128]{3,1,2,0:T(8,128)S(1)}, u32[]{:S(2)}, u32[]{:S(2)}) %all-to-all-start.1) | async-done | bytes 1179680 | tf_op jit(solution)/shard_map/all_to_all | solution.py:207
  77.4 0.1 copy.26
  77.5 0.7 copy.27
  78.2 3.5 %broadcast_in_dim.73 = f32[1025,9,128]{2,1,0:T(8,128)} broadcast(f32[]{:T(128)} %constant.165.clone.1), dimensions={} | broadcast | bytes 4723204 | tf_op jit(solution)/shard_map/broadcast_in_dim | solution.py:76
  81.7 30.0 %scatter_fusion.1 = f32[1025,9,128]{2,1,0:T(8,128)} fusion(f32[1025,9,128]{2,1,0:T(8,128)} %broadcast_in_dim.73, s32[256]{0:T(256)S(1)} %bitcast.79, f32[256,9,128]{2,1,0:T(8,128)S(1)} %copy.27), kind=kCustom, calls=%fused_computation.4 | custom fusion | flops 294912 | bytes 3539968 | tf_op jit(solution)/shard_map/scatter-add | solution.py:76
  111.7 3.9 %slice.114 = f32[1024,9,128]{2,1,0:T(8,128)S(1)} slice(f32[1025,9,128]{2,1,0:T(8,128)} %scatter_fusion.1), slice={[0:1024], [0:9], [0:128]} | slice | bytes 9437184 | tf_op jit(solution)/shard_map/slice | solution.py:76
  115.6 3.6 %copy.38 = f32[1024,9,128]{2,0,1:T(8,128)} copy(f32[1024,9,128]{2,1,0:T(8,128)S(1)} %slice.114) | data formatting | bytes 9437184
  119.3 30.4 %all-reduce.4.cloned.1.call-done = f32[1024,9,128]{2,0,1:T(8,128)} async-done(((f32[1024,9,128]{2,0,1:T(8,128)}), f32[1024,9,128]{2,0,1:T(8,128)}) %all-reduce.4.cloned.1.call-update) | async-done | bytes 4718608 | tf_op jit(solution)/shard_map/psum | solution.py:81
  149.7 2.9 %add_divide_fusion.2 = (f32[1024,1,128]{2,0,1:T(8,128)S(1)}, f32[1024,1,128]{2,0,1:T(8,128)S(1)}, f32[1024,1,128]{2,0,1:T(8,128)S(1)}, f32[1024,1,128]{2,0,1:T(8,128)S(1)}) fusion(f32[1024,9,128]{2,0,1:T(8,128)} %all-reduce.4.cloned.1.call-done), kind=kLoop, calls=%fused_computation.33 | loop fusion | flops 3014656 | bytes 6815744 | tf_op jit(solution)/shard_map/div | solution.py:56
  152.6 0.9 copy-done
  153.5 0.5 add_divide_fusion.1
  154.0 0.1 pad_maximum_fusion
  154.1 1.1 copy.39
  155.2 0.4 concatenate.13.clone
  155.6 1.0 gather_fusion
  156.6 0.8 copy.31
  157.4 7.0 %all-to-all-start.2 = ((f32[16,16,3,128]{3,1,2,0:T(8,128)}), f32[16,16,3,128]{3,1,2,0:T(8,128)S(1)}, u32[]{:S(2)}, u32[]{:S(2)}) async-start(f32[16,16,3,128]{3,1,2,0:T(8,128)} %copy.31), calls=%async_computation.2 | async-start | bytes 786432 | tf_op jit(solution)/shard_map/all_to_all | solution.py:222
  164.4 13.0 %all-to-all-done.2 = f32[16,16,3,128]{3,1,2,0:T(8,128)S(1)} async-done(((f32[16,16,3,128]{3,1,2,0:T(8,128)}), f32[16,16,3,128]{3,1,2,0:T(8,128)S(1)}, u32[]{:S(2)}, u32[]{:S(2)}) %all-to-all-start.2) | async-done | bytes 393248 | tf_op jit(solution)/shard_map/all_to_all | solution.py:222
  177.4 0.3 copy.33
  177.7 0.8 gather_fusion.1
  178.5 8.1 %while.27 = (s32[]{:T(128)}, f32[2,64,3,128]{3,2,1,0:T(4,128)S(1)}, f32[2,64,3,128]{3,2,1,0:T(4,128)S(1)}, s32[2,64,128]{2,1,0:T(8,128)S(1)}, s32[]{:T(128)}) while((s32[]{:T(128)}, f32[2,64,3,128]{3,2,1,0:T(4,128)S(1)}, f32[2,64,3,128]{3,2,1,0:T(4,128)S(1)}, s32[2,64,128]{2,1,0:T(8,128)S(1)}, s32[]{:T(128)}) %tuple.99), condition=%wide.region_11.12_spmd.clone, body=%wide.region_10.11_spmd.clone.sunk | while | flops 38797312 | bytes 361537 | solution.py:125
  178.6 4.0 %fusion.71 = f32[2,64,3,128]{3,2,1,0:T(4,128)S(1)} fusion(f32[2,64,3,128]{3,2,1,0:T(4,128)S(1)} %get-tuple-element.263, s32[]{:T(128)} %get-tuple-element.262, s32[64,128]{1,0:T(8,128)S(1)} %dynamic-slice_bitcast_fusion.5, f32[2,64,3,128]{3,2,1,0:T(4,128)S(1)} %get-tuple-element.269), kind=kOutput, calls=%fused_computation.20.clone.1 | convolution fusion | flops 38797312 | bytes 295936 | tf_op jit(solution)/shard_map/while/body/eval_jaxpr/rhe,roe->rho/dot_general | solution.py:121
  182.6 4.0 %fusion.71 = f32[2,64,3,128]{3,2,1,0:T(4,128)S(1)} fusion(f32[2,64,3,128]{3,2,1,0:T(4,128)S(1)} %get-tuple-element.263, s32[]{:T(128)} %get-tuple-element.262, s32[64,128]{1,0:T(8,128)S(1)} %dynamic-slice_bitcast_fusion.5, f32[2,64,3,128]{3,2,1,0:T(4,128)S(1)} %get-tuple-element.269), kind=kOutput, calls=%fused_computation.20.clone.1 | convolution fusion | flops 38797312 | bytes 295936 | tf_op jit(solution)/shard_map/while/body/eval_jaxpr/rhe,roe->rho/dot_general | solution.py:121
  186.7 0.5 slice_reduce_fusion.1
  187.3 0.8 multiply_reduce_fusion.5
  188.1 0.6 collective-permute-start.2
  188.7 5.1 %collective-permute-start.3 = (f32[8,2]{0,1:T(2,128)S(1)}, f32[8,2]{0,1:T(2,128)S(1)}, u32[]{:S(2)}, u32[]{:S(2)}) collective-permute-start(f32[8,2]{0,1:T(2,128)S(1)} %pad_maximum_fusion.2), channel_id=1, source_target_pairs={{2,0},{4,2},{6,4},{8,6},{10,8},{12,10},{14,12},{16,14},{18,16},{20... | collective-permute-start | bytes 200 | tf_op jit(solution)/shard_map/ppermute | solution.py:25
  193.8 1.5 collective-permute-done.2
  195.3 0.7 multiply_reduce_fusion.6
  196.0 40.4 %all-reduce.1 = (f32[]{:T(128)}, f32[]{:T(128)}, f32[]{:T(128)}, f32[]{:T(128)}) all-reduce(f32[]{:T(128)} %get-tuple-element.134, f32[]{:T(128)} %get-tuple-element.135, f32[]{:T(128)} %get-tuple-element.133, f32[]{:T(128)} %get-tuple-element.132), channel_id=1, replica_groups=mesh['tm'=16,'det'=2] {'tm','det'}, use_global_device_ids=true, to_apply=%region_1.2 | all-reduce | flops 4 | bytes 32 | tf_op jit(solution)/shard_map/psum | solution.py:236
  240.3 0.6 multiply_add_fusion.2
  (55 shorter events, 1.4 us)
Async XLA Ops:
  7.2 18.5 %collective-permute-start = (f32[8,2]{0,1:T(2,128)}, f32[8,2]{0,1:T(2,128)S(1)}, u32[]{:S(2)}, u32[]{:S(2)}) collective-permute-start(f32[8,2]{0,1:T(2,128)} %param.21), channel_id=1, source_target_pairs={{0,2},{2,4},{4,6},{6,8},{8,10},{10,12},{12,14},{14,16},{16,18},{18... | collective-permute-start | bytes 200 | tf_op jit(solution)/shard_map/ppermute | solution.py:23
  10.2 16.1 %collective-permute-start.1 = (f32[8,2]{0,1:T(2,128)}, f32[8,2]{0,1:T(2,128)S(1)}, u32[]{:S(2)}, u32[]{:S(2)}) collective-permute-start(f32[8,2]{0,1:T(2,128)} %param.21), channel_id=1, source_target_pairs={{2,0},{4,2},{6,4},{8,6},{10,8},{12,10},{14,12},{16,14},{18,16},{20... | collective-permute-start | bytes 200 | tf_op jit(solution)/shard_map/ppermute | solution.py:25
  17.9 26.2 %all-to-all-start = ((f32[16,1,16]{2,1,0:T(1,128)}), f32[16,1,16]{2,1,0:T(1,128)S(1)}, u32[]{:S(2)}, u32[]{:S(2)}) async-start(f32[16,1,16]{2,1,0:T(1,128)} %all_to_all.12), calls=%async_computation | async-start | bytes 16384 | tf_op jit(solution)/shard_map/all_to_all | solution.py:214
  44.0 33.3 %all-to-all-start.1 = ((f32[16,16,9,128]{3,1,2,0:T(8,128)}), f32[16,16,9,128]{3,1,2,0:T(8,128)S(1)}, u32[]{:S(2)}, u32[]{:S(2)}) async-start(f32[16,16,9,128]{3,1,2,0:T(8,128)} %copy.25), calls=%async_computation.1 | async-start | bytes 2359296 | tf_op jit(solution)/shard_map/all_to_all | solution.py:207
  50.9 98.8 %all-reduce.4.cloned.1.call-start = ((), (), s32[]{:S(2)}) async-start(), calls=%async_computation.3 | async-start | bytes 9437184 | tf_op jit(solution)/shard_map/psum | solution.py:81
  149.7 3.8 %copy-start = (f32[1024,9,128]{2,0,1:T(8,128)S(1)}, f32[1024,9,128]{2,0,1:T(8,128)}, u32[]{:S(2)}) copy-start(f32[1024,9,128]{2,0,1:T(8,128)} %all-reduce.4.cloned.1.call-done) | copy-start | bytes 14155780
  157.4 20.0 %all-to-all-start.2 = ((f32[16,16,3,128]{3,1,2,0:T(8,128)}), f32[16,16,3,128]{3,1,2,0:T(8,128)S(1)}, u32[]{:S(2)}, u32[]{:S(2)}) async-start(f32[16,16,3,128]{3,1,2,0:T(8,128)} %copy.31), calls=%async_computation.2 | async-start | bytes 786432 | tf_op jit(solution)/shard_map/all_to_all | solution.py:222
  178.5 8.8 %copy-start.1 = (f32[8,2048]{1,0:T(8,128)S(1)}, f32[8,2048]{1,0:T(8,128)}, u32[]{:S(2)}) copy-start(f32[8,2048]{1,0:T(8,128)} %param.24) | copy-start | bytes 196612
  178.5 8.8 %copy-start.5 = (s32[8]{0:T(128)S(1)}, s32[8]{0:T(128)}, u32[]{:S(2)}) copy-start(s32[8]{0:T(128)} %param.22) | copy-start | bytes 100
  178.5 16.8 %copy-start.2 = (f32[8,2]{0,1:T(2,128)S(1)}, f32[8,2]{0,1:T(2,128)}, u32[]{:S(2)}) copy-start(f32[8,2]{0,1:T(2,128)} %param.21) | copy-start | bytes 196
  178.5 16.8 %copy-start.3 = (f32[8,2]{0,1:T(2,128)S(1)}, f32[8,2]{0,1:T(2,128)}, u32[]{:S(2)}) copy-start(f32[8,2]{0,1:T(2,128)} %param.20) | copy-start | bytes 196
  178.5 61.8 %copy-start.4 = (f32[8,2]{0,1:T(2,128)S(1)}, f32[8,2]{0,1:T(2,128)}, u32[]{:S(2)}) copy-start(f32[8,2]{0,1:T(2,128)} %param.19) | copy-start | bytes 196
  188.1 7.2 %collective-permute-start.2 = (f32[8,2]{0,1:T(2,128)S(1)}, f32[8,2]{0,1:T(2,128)S(1)}, u32[]{:S(2)}, u32[]{:S(2)}) collective-permute-start(f32[8,2]{0,1:T(2,128)S(1)} %pad_maximum_fusion.1), channel_id=1, source_target_pairs={{0,2},{2,4},{4,6},{6,8},{8,10},{10,12},{12,14},{14,16},{16,18},{18... | collective-permute-start | bytes 200 | tf_op jit(solution)/shard_map/ppermute | solution.py:23
  188.7 6.6 %collective-permute-start.3 = (f32[8,2]{0,1:T(2,128)S(1)}, f32[8,2]{0,1:T(2,128)S(1)}, u32[]{:S(2)}, u32[]{:S(2)}) collective-permute-start(f32[8,2]{0,1:T(2,128)S(1)} %pad_maximum_fusion.2), channel_id=1, source_target_pairs={{2,0},{4,2},{6,4},{8,6},{10,8},{12,10},{14,12},{16,14},{18,16},{20... | collective-permute-start | bytes 200 | tf_op jit(solution)/shard_map/ppermute | solution.py:25
Sparse Core Ops, SparseCore 0:
  119.4 30.2 all-reduce.3
where the time goes:
time: 249 us; the launch traced here: 248 us
  waiting for transfers between devices  71.2 us (29%)
  blocking collectives  40.4 us (16%)
  other arithmetic  40.1 us (16%)
  local copies, waits for them, and re-layouts  32 us (13%)
  starting transfers between devices  30.1 us (12%)
  between operations  18.3 us (7%)
  matrix products  15.4 us (6%)
    psum x1, blocking collectives, body(): lax.psum((jnp.sum(leftover_error * leftover_error), jnp.sum(search_vector...  40.4 us
    psum x1, waiting for transfers between devices, combine_maps(): totals = lax.psum(partial_value, 'det')  30.4 us
    scatter-add x1, other arithmetic, place_rows(): jnp.zeros((owner_tiles + 1, 9, LANES), jnp.float32).at[targets].add(rows)  30 us
    all_to_all x1, waiting for transfers between devices, body(): lax.all_to_all(outgoing.reshape(ranks, capacity, 9, LANES), 'tm', split_a...  26.2 us
    all_to_all x1, waiting for transfers between devices, body(): lax.all_to_all(returned, 'tm', split_axis=0, concat_axis=0, tiled=True)  13 us
    ppermute x2, starting transfers between devices, padded_2(): lax.ppermute(head, axis, [((i + 1) % count, i) for i in range(count)])  9.12 us
    dot_general x2, matrix products, read_one_group(): jnp.einsum('rhe,roe->rho', input_arrays[0], indicator_matrix, precision=l...  8.09 us
    dot_general x2, matrix products, bin_one_group(): jnp.einsum('zte,zeh->zth', input_arrays[0], indicator_matrix, precision=l...  7.36 us
  transfers between devices with their start and end apart: 8, of which 4 were waited for; matrix products, arithmetic and copies ran while one was open for 10% of the time, Pallas kernels for 0%

commit v1 on v0

v1 whole, which is shorter than its diff:
```python
import functools

import jax
import jax.numpy as jnp
from jax import lax
from jax.experimental import pallas as pl
from jax.experimental.pallas import tpu as pltpu
from jax.sharding import PartitionSpec as P

PIX_OWN = 131072
MAP_PRIOR = 1.0
BASE_PRIOR = 0.1
LANES = 128
OWNER_TILES = PIX_OWN // LANES
CHANNELS = 8
VMEM_BYTES = 32 * 1024 * 1024

SIN_TERMS = (1.0, -1.0 / 6, 1.0 / 120, -1.0 / 5040, 1.0 / 362880, -1.0 / 39916800, 1.0 / 6227020800)
COS_TERMS = (1.0, -0.5, 1.0 / 24, -1.0 / 720, 1.0 / 40320, -1.0 / 3628800, 1.0 / 479001600, -1.0 / 87178291200)
PI_PARTS = (3.140625, 0.0009670257568359375, 6.2771141529083252e-07)


def iota(shape, dim):
    return lax.broadcasted_iota(jnp.int32, shape, dim)


def log2(number):
    assert number & (number - 1) == 0
    return number.bit_length() - 1


def split3(x):
    high = x.astype(jnp.bfloat16)
    rest = x - high.astype(jnp.float32)
    middle = rest.astype(jnp.bfloat16)
    low = (rest - middle.astype(jnp.float32)).astype(jnp.bfloat16)
    return high, middle, low


def dot(a, b):
    return jnp.dot(a, b, preferred_element_type=jnp.float32)


def exact_dot(selector, x):
    high, middle, low = split3(x)
    return (dot(selector, high) + dot(selector, middle)) + dot(selector, low)


def horner(x, terms):
    total = jnp.full_like(x, terms[-1])
    for term in terms[-2::-1]:
        total = total * x + term
    return total


def cos_sin(angle):
    turns = jnp.round(angle * (1.0 / 3.14159265358979))
    rest = angle - turns * PI_PARTS[0]
    rest = rest - turns * PI_PARTS[1]
    rest = rest - turns * PI_PARTS[2]
    half = turns * 0.5
    sign = 1.0 - 4.0 * (half - jnp.floor(half))
    square = rest * rest
    cosine = sign * horner(square, COS_TERMS)
    sine = sign * rest * horner(square, SIN_TERMS)
    return cosine, sine


def spline_weights(fraction):
    square = fraction * fraction
    cube = square * fraction
    rest = 1.0 - fraction
    first = rest * rest * rest * (1.0 / 6.0)
    second = (3.0 * cube - 6.0 * square + 4.0) * (1.0 / 6.0)
    third = (-3.0 * cube + 3.0 * square + 3.0 * fraction + 1.0) * (1.0 / 6.0)
    fourth = cube * (1.0 / 6.0)
    return (first, second, third, fourth)


def lane_gather(table, index):
    return jnp.take_along_axis(table, index, axis=1, mode="promise_in_bounds")


def send_kernel(ranks, cap, offset_ref, patch_ref, cell_ref, phase_ref, search_ref, left_ref, out_ref):
    dets, columns = patch_ref.shape
    blocks = dets * columns
    samples = phase_ref.shape[1]
    nodes = search_ref.shape[1]
    span = lax.axis_index("tm")
    rows = 2 * cap + 1
    square = (blocks, blocks)
    tiles = jnp.concatenate(
        [jnp.broadcast_to(patch_ref[:, c : c + 1], (dets, LANES)) for c in range(columns)], axis=0
    )
    cells = jnp.concatenate([cell_ref[:, c * LANES : (c + 1) * LANES] for c in range(columns)], axis=0)
    phases = jnp.concatenate([phase_ref[:, c * LANES : (c + 1) * LANES] for c in range(columns)], axis=0)
    pixels = (tiles * LANES + cells + 1).astype(jnp.float32)
    owner = (tiles >> log2(OWNER_TILES)).astype(jnp.float32)
    owner_t = owner.T
    same = owner == owner_t
    here, there = iota(square, 0), iota(square, 1)
    rank_row = jnp.sum(jnp.where(same & (here < there), 1.0, 0.0), axis=0, keepdims=True)
    rank_col = jnp.sum(jnp.where(same & (there < here), 1.0, 0.0), axis=1, keepdims=True)
    slot_row = (owner_t[0:1, :] * cap + rank_row).astype(jnp.int32)
    place = (iota((ranks * cap, blocks), 0) == slot_row).astype(jnp.bfloat16)
    slot_phase = exact_dot(place, phases)
    slot_pixel = exact_dot(place, pixels) - 1.0
    lane = iota(square, 1)
    det_lane = iota((dets, LANES), 0)
    shift = jnp.zeros((dets, LANES), jnp.int32)
    for d in range(dets):
        shift = jnp.where(det_lane == d, offset_ref[d], shift)
    start = jnp.concatenate([c * LANES - shift for c in range(columns)], axis=0) + span * samples
    which = (iota(square, 0) & (dets - 1)) + 1
    rank = rank_col.astype(jnp.int32)
    listing = jnp.where(lane == rank, start, 0) + jnp.where(lane == rank + cap, which, 0)
    chosen = (iota((ranks, blocks), 0).astype(jnp.float32) == owner_t[0:1, :]).astype(jnp.bfloat16)
    info = exact_dot(chosen, listing.astype(jnp.float32))
    knots = jnp.zeros((dets, LANES), jnp.float32)
    small = iota((dets, LANES), 1)
    for n in range(nodes):
        base = 2 * cap + det_lane * nodes + n
        knots = knots + jnp.where(small == base, search_ref[:, n : n + 1], 0.0)
        knots = knots + jnp.where(small == base + dets * nodes, left_ref[:, n : n + 1], 0.0)
    info = info + jnp.sum(knots, axis=0, keepdims=True)
    for o in range(ranks):
        out_ref[o * rows : o * rows + cap, :] = slot_phase[o * cap : (o + 1) * cap, :]
        out_ref[o * rows + cap : o * rows + 2 * cap, :] = slot_pixel[o * cap : (o + 1) * cap, :]
        out_ref[o * rows + 2 * cap : (o + 1) * rows, :] = info[o : o + 1, :]


def main_kernel(
    ranks, cap, dets, nodes, spacing, own_ref, other_ref, out_ref, packs_ref,
    phase_ref, cell_ref, label_ref, info_ref, meta_ref, flip_ref, table_ref,
    wave_ref, stream_ref, entry_ref, bin_ref,
):
    slots = ranks * cap
    rows = 2 * cap + 1
    knots = ranks * nodes
    pages = max(1, knots // LANES)
    group = lax.axis_index("det")
    packed = knots * dets // LANES
    chunk = 32

    meta_ref[...] = jnp.zeros_like(meta_ref)
    for half, ref in enumerate((own_ref, other_ref)):
        for o in range(ranks):
            here = half * slots + o * cap
            phase_ref[here : here + cap, :] = ref[o * rows : o * rows + cap, :]
            pixel = ref[o * rows + cap : o * rows + 2 * cap, :]
            label = jnp.floor(pixel * (1.0 / LANES))
            label_ref[here : here + cap, :] = label
            cell_ref[here : here + cap, :] = pixel - label * LANES
            info = ref[o * rows + 2 * cap : (o + 1) * rows, :]
            info_ref[here : here + cap, :] = jnp.broadcast_to(info, (cap, LANES))
            meta_ref[half, o : o + 1, :] = info

    small = iota((dets, LANES), 1)
    per_row = LANES // (dets * nodes)
    for half in range(2):
        flip_ref[...] = meta_ref[half].T
        for page in range(pages):
            table = jnp.zeros((dets, LANES), jnp.float32)
            place = small + page * LANES
            for n in range(nodes):
                column = flip_ref[pl.ds(2 * cap + n, dets, stride=nodes), :]
                values = lane_gather(column, (place >> log2(nodes)) & (LANES - 1))
                table = jnp.where((place & (nodes - 1)) == n, values, table)
            table = jnp.concatenate([table, jnp.zeros((LANES - dets, LANES), jnp.float32)], axis=0)
            at = half * slots
            index = (iota((slots, LANES), 0) & (cap - 1)) + cap
            which = lane_gather(info_ref[at : at + slots, :], index)
            chosen = (which == (iota((slots, LANES), 1) + 1).astype(jnp.float32)).astype(jnp.bfloat16)
            table_ref[page, at : at + slots, :] = exact_dot(chosen, table)
        side = group if half == 0 else 1 - group
        for kind in range(2):
            for p in range(packed):
                spans = meta_ref[half, p * per_row : (p + 1) * per_row, :]
                lane = iota((per_row, LANES), 1)
                first = 2 * cap + kind * dets * nodes
                spread = lane_gather(spans, first + (lane & (dets * nodes - 1)))
                mine = (lane >> log2(dets * nodes)) == iota((per_row, LANES), 0)
                line = jnp.sum(jnp.where(mine, spread, 0.0), axis=0, keepdims=True)
                packs_ref[kind, pl.ds(side * packed + p, 1), :] = line

    def spline(at, count):
        info = info_ref[pl.ds(at, count), :]
        slot = (iota((count, LANES), 0) + at) & (cap - 1)
        start = lane_gather(info, slot).astype(jnp.int32)
        time = start + iota((count, LANES), 1)
        interval = time >> log2(spacing)
        fraction = (time & (spacing - 1)).astype(jnp.float32) * (1.0 / spacing)
        return start >> log2(spacing), interval, spline_weights(fraction)

    def prepare(step, carry):
        at = pl.multiple_of(step * chunk, chunk)
        cosine, sine = cos_sin(2.0 * phase_ref[pl.ds(at, chunk), :])
        _, interval, weights = spline(at, chunk)
        stream = jnp.zeros((chunk, LANES), jnp.float32)
        for term in range(4):
            knot = (interval + (term - 1)) & (knots - 1)
            value = lane_gather(table_ref[0, pl.ds(at, chunk), :], knot & (LANES - 1))
            for page in range(1, pages):
                more = lane_gather(table_ref[page, pl.ds(at, chunk), :], knot & (LANES - 1))
                value = jnp.where((knot >> log2(LANES)) == page, more, value)
            stream = stream + weights[term] * value
        wave_ref[0, pl.ds(at, chunk), :] = cosine
        wave_ref[1, pl.ds(at, chunk), :] = sine
        stream_ref[pl.ds(at, chunk), :] = stream
        entries = (
            stream, stream * cosine, stream * sine, jnp.ones_like(cosine), cosine, sine,
            cosine * cosine, cosine * sine,
        )
        for channel, entry in enumerate(entries):
            entry_ref[pl.ds(at * CHANNELS + channel, chunk, stride=CHANNELS), :] = entry
        return carry

    lax.fori_loop(0, 2 * slots // chunk, prepare, 0)

    lanes_down = iota((LANES, LANES), 0).astype(jnp.float32)

    def collect(slot, carry):
        at = pl.multiple_of(slot * CHANNELS, CHANNELS)
        entry = jnp.concatenate(split3(entry_ref[pl.ds(at, CHANNELS), :]), axis=0)
        cell = cell_ref[pl.ds(slot, 1), :]
        hits = (lanes_down == cell).astype(jnp.bfloat16)
        sums = lax.dot_general(
            entry, hits, (((1,), (1,)), ((), ())), preferred_element_type=jnp.float32
        )
        bin_ref[pl.ds(at, CHANNELS), :] = (
            sums[:CHANNELS] + sums[CHANNELS : 2 * CHANNELS]
        ) + sums[2 * CHANNELS :]
        return carry

    lax.fori_loop(0, 2 * slots, collect, 0, unroll=8)

    labels = label_ref[...]
    across = jnp.concatenate(
        [labels[k * LANES : (k + 1) * LANES, :].T[0:1, :] for k in range(2 * slots // LANES)], axis=1
    )
    same = (labels[:slots, 0:1] == across).astype(jnp.bfloat16)
    totals = []
    for channel in range(CHANNELS):
        binned = bin_ref[pl.ds(channel, 2 * slots, stride=CHANNELS), :]
        totals.append(exact_dot(same, binned))
    signal, signal_cos, signal_sin, count, cos_sum, sin_sum, cos_cos, cos_sin_sum = totals
    sin_sin = count - cos_cos
    stokes_i = count + MAP_PRIOR
    stokes_q = cos_cos + MAP_PRIOR
    stokes_u = sin_sin + MAP_PRIOR
    minor_one = stokes_q * stokes_u - cos_sin_sum * cos_sin_sum
    minor_two = sin_sum * cos_sin_sum - cos_sum * stokes_u
    minor_three = cos_sum * cos_sin_sum - sin_sum * stokes_q
    minor_four = stokes_i * stokes_u - sin_sum * sin_sum
    minor_five = cos_sum * sin_sum - stokes_i * cos_sin_sum
    minor_six = stokes_i * stokes_q - cos_sum * cos_sum
    determinant = stokes_i * minor_one + cos_sum * minor_two + sin_sum * minor_three
    scale = 1.0 / determinant
    map_i = (minor_one * signal + minor_two * signal_cos + minor_three * signal_sin) * scale
    map_q = (minor_two * signal + minor_four * signal_cos + minor_five * signal_sin) * scale
    map_u = (minor_three * signal + minor_five * signal_cos + minor_six * signal_sin) * scale

    cell = cell_ref[:slots, :].astype(jnp.int32)
    projected = (
        lane_gather(map_i, cell) + wave_ref[0, :slots, :] * lane_gather(map_q, cell)
    ) + wave_ref[1, :slots, :] * lane_gather(map_u, cell)
    which = lane_gather(info_ref[:slots, :], (iota((slots, LANES), 0) & (cap - 1)) + cap)
    cleaned = jnp.where(which > 0.5, stream_ref[:slots, :] - projected, 0.0)
    base, interval, weights = spline(0, slots)
    base = base[:, 0:1]
    early = interval == base
    det = which.astype(jnp.int32)[:, 0:1] - 1
    lines = [jnp.zeros((slots, LANES), jnp.float32) for _ in range(packed)]
    lane = iota((slots, LANES), 1)
    for term in range(5):
        low = weights[term] if term < 4 else 0.0
        high = weights[term - 1] if term > 0 else 0.0
        value = jnp.sum(jnp.where(early, low, high) * cleaned, axis=1, keepdims=True)
        knot = (base + (term - 1)) & (knots - 1)
        spot = (knot >> log2(nodes)) * (dets * nodes) + det * nodes + (knot & (nodes - 1))
        for p in range(packed):
            lines[p] = lines[p] + jnp.where(lane == spot - p * LANES, value, 0.0)
    partial = jnp.concatenate([jnp.sum(line, axis=0, keepdims=True) for line in lines], axis=0)
    for target in range(out_ref.shape[0] // packed):
        out_ref[target * packed : (target + 1) * packed, :] = partial


def finish_kernel(
    ranks, spacing, arrived_ref, packs_ref, offset_ref, left_ref, search_ref,
    new_offset_ref, new_left_ref, new_search_ref,
):
    dets, nodes = search_ref.shape
    height = packs_ref.shape[1]
    total = arrived_ref[0:height, :]
    for o in range(1, ranks):
        total = total + arrived_ref[o * height : (o + 1) * height, :]
    search, left = packs_ref[0], packs_ref[1]
    image = total * (1.0 / spacing) + BASE_PRIOR * search
    norm_old = jnp.sum(left * left, keepdims=True)
    stride_factor = norm_old / jnp.sum(search * image, keepdims=True)
    fresh = left - stride_factor * image
    beta = jnp.sum(fresh * fresh, keepdims=True) / norm_old
    span, group = lax.axis_index("tm"), lax.axis_index("det")
    per_row = LANES // (dets * nodes)
    row = group * (height // 2) + (span >> log2(per_row))
    mine = jnp.sum(jnp.where(iota((height, LANES), 0) == row, image, 0.0), axis=0, keepdims=True)
    lane = iota((dets, LANES), 1)
    first = (span & (per_row - 1)) * (dets * nodes)
    index = first + iota((dets, LANES), 0) * nodes + (lane & (nodes - 1))
    mine = lane_gather(jnp.broadcast_to(mine, (dets, LANES)), index)[:, :nodes]
    new_offset_ref[...] = offset_ref[...] + stride_factor * search_ref[...]
    new_left = left_ref[...] - stride_factor * mine
    new_left_ref[...] = new_left
    new_search_ref[...] = new_left + beta * search_ref[...]


def body(
    offset_coeffs,
    leftover_error,
    search_vector,
    node_lattice_offset,
    sky_cell_in_patch,
    analyser_reading_phase,
    segment_sky_patch,
):
    ranks, groups = lax.axis_size("tm"), lax.axis_size("det")
    dets, samples = analyser_reading_phase.shape
    nodes = search_vector.shape[1]
    spacing = samples // nodes
    blocks = segment_sky_patch.size
    cap = max(2, 2 * blocks // ranks)
    slots = ranks * cap
    rows = 2 * cap + 1
    packed = ranks * nodes * dets // LANES
    vmem = pl.BlockSpec(memory_space=pltpu.VMEM)
    smem = pl.BlockSpec(memory_space=pltpu.SMEM)
    params = pltpu.CompilerParams(vmem_limit_bytes=VMEM_BYTES)

    outgoing = pl.pallas_call(
        functools.partial(send_kernel, ranks, cap),
        out_shape=jax.ShapeDtypeStruct((ranks * rows, LANES), jnp.float32),
        in_specs=[smem] + [vmem] * 5,
        out_specs=vmem,
        compiler_params=params,
        name="send",
    )(
        node_lattice_offset, segment_sky_patch, sky_cell_in_patch, analyser_reading_phase,
        search_vector, leftover_error,
    )
    arrived = lax.all_to_all(
        outgoing.reshape(ranks, 1, rows * LANES), "tm", split_axis=0, concat_axis=0, tiled=True
    )
    swap = [(i, groups - 1 - i) for i in range(groups)]
    other = lax.ppermute(arrived, "det", swap)
    pages = max(1, ranks * nodes // LANES)
    big = pltpu.VMEM((2 * slots, LANES), jnp.float32)
    partials, packs = pl.pallas_call(
        functools.partial(main_kernel, ranks, cap, dets, nodes, spacing),
        out_shape=(
            jax.ShapeDtypeStruct((ranks * groups * packed, LANES), jnp.float32),
            jax.ShapeDtypeStruct((2, groups * packed, LANES), jnp.float32),
        ),
        in_specs=[vmem] * 2,
        out_specs=(vmem, vmem),
        scratch_shapes=[
            big, big, big, big,
            pltpu.VMEM((2, LANES, LANES), jnp.float32),
            pltpu.VMEM((LANES, LANES), jnp.float32),
            pltpu.VMEM((pages, 2 * slots, LANES), jnp.float32),
            pltpu.VMEM((2, 2 * slots, LANES), jnp.float32),
            big,
            pltpu.VMEM((2 * slots * CHANNELS, LANES), jnp.float32),
            pltpu.VMEM((2 * slots * CHANNELS, LANES), jnp.float32),
        ],
        compiler_params=params,
        name="main",
    )(arrived.reshape(ranks * rows, LANES), other.reshape(ranks * rows, LANES))
    gathered = lax.all_to_all(
        partials.reshape(ranks * groups, 1, packed * LANES),
        ("tm", "det"), split_axis=0, concat_axis=0, tiled=True,
    )
    small = jax.ShapeDtypeStruct((dets, nodes), jnp.float32)
    return pl.pallas_call(
        functools.partial(finish_kernel, ranks, spacing),
        out_shape=(small, small, small),
        in_specs=[vmem] * 5,
        out_specs=(vmem, vmem, vmem),
        compiler_params=params,
        name="finish",
    )(
        gathered.reshape(ranks * groups * packed, LANES), packs,
        offset_coeffs, leftover_error, search_vector,
    )


def solution(mesh):
    return jax.shard_map(
        body,
        mesh=mesh,
        in_specs=(
            P("det", "tm"),
            P("det", "tm"),
            P("det", "tm"),
            P("det"),
            P("det", "tm"),
            P("det", "tm"),
            P("det", "tm"),
        ),
        out_specs=(P("det", "tm"), P("det", "tm"), P("det", "tm")),
        check_vma=False,
    )
```

time: 249 us -> 60.2 us (0.24)
  waiting for transfers between devices: 71.2 us -> 8.7 us
  other arithmetic: 40.1 us -> 0 us
  starting transfers between devices: 30.1 us -> 2.66 us
  local copies, waits for them, and re-layouts: 32 us -> 5.1 us
  Pallas kernels: 0 us -> 24.6 us
  blocking collectives: 40.4 us -> 18.1 us
  between operations: 18.3 us -> 0.68 us
  matrix products: 15.4 us -> 0 us
    psum x1 -> x0, blocking collectives: 40.4 us -> none  [body(): lax.psum((jnp.sum(leftover_error * leftover_error), jnp.sum(search_vector...]
    all_to_all x3 -> x1, waiting for transfers between devices: 39.3 us -> 7.16 us  [body(): lax.all_to_all(partials.reshape(ranks * groups, 1, packed * LANES), ('tm'...]
    psum x1 -> x0, waiting for transfers between devices: 30.4 us -> none  [combine_maps(): totals = lax.psum(partial_value, 'det')]
    scatter-add x1 -> x0, other arithmetic: 30 us -> none  [place_rows(): jnp.zeros((owner_tiles + 1, 9, LANES), jnp.float32).at[targets].add(rows)]
    pallas_call x0 -> x3, Pallas kernels: none -> 24.6 us  [the longest x1 23.4 us: body(): pl.pallas_call(functools.partial(main_kernel, ranks, cap, dets, nodes, sp...]
    all_to_all x0 -> x1, blocking collectives: none -> 18.1 us  [body(): lax.all_to_all(outgoing.reshape(ranks, 1, rows * LANES), 'tm', split_axis...]
    dot_general x4 -> x0, matrix products: 15.4 us -> none  [the longest x2 8.09 us: read_one_group(): jnp.einsum('rhe,roe->rho', input_arrays[0], indicator_matrix, precision=l...]
    all_to_all x3 -> x1, starting transfers between devices: 17.3 us -> 2.65 us  [body(): lax.all_to_all(partials.reshape(ranks * groups, 1, packed * LANES), ('tm'...]
  transfers between devices with their start and end apart: 8 -> 2, of which waited for: 4 -> 2; matrix products, arithmetic and copies ran while one was open for 10% -> 0% of each run, Pallas kernels for 0% -> 0%
where the time goes in v1:
time: 60.2 us; the launch traced here: 59.9 us
  Pallas kernels  24.6 us (41%)
  blocking collectives  18.1 us (30%)
  waiting for transfers between devices  8.7 us (14%)
  local copies, waits for them, and re-layouts  5.1 us (8%)
  starting transfers between devices  2.66 us (4%)
  between operations  0.68 us (1%)
    pallas_call x1, Pallas kernels, body(): pl.pallas_call(functools.partial(main_kernel, ranks, cap, dets, nodes, sp...  23.4 us
    all_to_all x1, blocking collectives, body(): lax.all_to_all(outgoing.reshape(ranks, 1, rows * LANES), 'tm', split_axis...  18.1 us
    all_to_all x1, waiting for transfers between devices, body(): lax.all_to_all(partials.reshape(ranks * groups, 1, packed * LANES), ('tm'...  7.16 us
    unnamed x15, local copies, waits for them, and re-layouts  3.19 us
    all_to_all x1, starting transfers between devices, body(): lax.all_to_all(partials.reshape(ranks * groups, 1, packed * LANES), ('tm'...  2.65 us
    pallas_call x3, local copies, waits for them, and re-layouts, body(): pl.pallas_call(functools.partial(finish_kernel, ranks, spacing), out_shap...  1.91 us
    ppermute x1, waiting for transfers between devices, body(): other = lax.ppermute(arrived, 'det', swap)  1.54 us
  transfers between devices with their start and end apart: 2, of which 2 were waited for; matrix products, arithmetic and copies ran while one was open for 0% of the time, Pallas kernels for 0%

profile of v1, /device:TPU:0, one launch (start us, length us, event | category | flops | bytes accessed | tf_op | source)
XLA Modules:
  0.0 59.9 jit_solution(9127439971284360544)
XLA Ops:
  0.6 0.0 copy-start.4
  0.6 0.0 copy-start.2
  0.7 0.8 %copy.18.search_ref = f32[8,2]{1,0:T(8,128)S(1)} copy(f32[8,2]{0,1:T(2,128)} %param.9) | data formatting | bytes 128 | tf_op args[2]
  1.4 0.0 copy-done.4
  1.4 0.0 copy-start.3
  1.4 0.1 copy.19.left_ref
  1.5 0.0 copy-done.2
  1.5 0.6 copy-done.3
  2.1 0.0 copy-start
  2.1 0.8 %copy-done = s32[8,2048]{1,0:T(8,128)S(1)} copy-done((s32[8,2048]{1,0:T(8,128)S(1)}, s32[8,2048]{1,0:T(8,128)}, u32[]{:S(2)}) %copy-start) | copy-done | bytes 65560
  2.9 0.0 copy-start.1
  2.9 0.8 %copy-done.1 = f32[8,2048]{1,0:T(8,128)S(1)} copy-done((f32[8,2048]{1,0:T(8,128)S(1)}, f32[8,2048]{1,0:T(8,128)}, u32[]{:S(2)}) %copy-start.1) | copy-done | bytes 65560
  3.8 1.0 %send.1 = f32[528,128]{1,0:T(8,128)S(1)} custom-call(s32[8]{0:T(128)S(1)} %copy-done.3, s32[8,16]{1,0:T(8,128)S(1)} %copy-done.2, s32[8,2048]{1,0:T(8,128)S(1)} %copy-done, f32[8,2048]{1,0:T(8,128)S(1)} %copy-done.1, f32[8,2]{1,0:T(8,128)S(1)} %copy.18.search_ref, f32[8,2]{1,0:T(8,128)S(1)} %copy.19.left_ref), custom_call_target="tpu_custom_call" | custom-call | tf_op jit(solution)/shard_map/send/pallas_call | solution.py:339
  4.7 18.1 %all_to_all.10 = f32[16,1,4224]{2,1,0:T(1,128)S(1)} all-to-all(f32[16,1,4224]{2,1,0:T(1,128)S(1)} %bitcast.6), channel_id=1, replica_groups=mesh['tm'=16,'det'=2] {'tm'}, dimensions={0} | all-to-all | bytes 540672 | tf_op jit(solution)/shard_map/all_to_all | solution.py:350
  22.9 0.0 collective-permute-start
  22.9 1.5 %collective-permute-done = f32[16,1,4224]{2,1,0:T(1,128)S(1)} collective-permute-done((f32[16,1,4224]{2,1,0:T(1,128)S(1)}, f32[16,1,4224]{2,1,0:T(1,128)S(1)}, u32[]{:S(2)}, u32[]{:S(2)}) %collective-permute-start) | collective-permute-done | bytes 270368 | tf_op jit(solution)/shard_map/ppermute | solution.py:354
  24.4 23.4 %main.1 = (f32[64,128]{1,0:T(8,128)}, f32[2,4,128]{2,1,0:T(4,128)S(1)}) custom-call(f32[528,128]{1,0:T(8,128)S(1)} %bitcast.5, f32[528,128]{1,0:T(8,128)S(1)} %bitcast.7), custom_call_target="tpu_custom_call" | custom-call | tf_op jit(solution)/shard_map/main/pallas_call | solution.py:357
  47.8 0.0 copy-start.5
  47.8 2.7 %all-to-all-start.1 = ((f32[32,1,256]{2,1,0:T(1,128)}), f32[32,1,256]{2,1,0:T(1,128)S(1)}, u32[]{:S(2)}, u32[]{:S(2)}) async-start(f32[32,1,256]{2,1,0:T(1,128)} %bitcast.3), calls=%async_computation.1 | async-start | bytes 65536 | tf_op jit(solution)/shard_map/all_to_all | solution.py:378
  50.5 0.0 copy-done.5
  50.5 0.1 copy.22.offset_ref
  50.5 7.2 %all-to-all-done.1 = f32[32,1,256]{2,1,0:T(1,128)S(1)} async-done(((f32[32,1,256]{2,1,0:T(1,128)}), f32[32,1,256]{2,1,0:T(1,128)S(1)}, u32[]{:S(2)}, u32[]{:S(2)}) %all-to-all-start.1) | async-done | bytes 32800 | tf_op jit(solution)/shard_map/all_to_all | solution.py:378
  57.7 0.3 finish.1
  58.0 0.6 %copy.25 = f32[8,2]{0,1:T(2,128)} copy(f32[8,2]{1,0:T(8,128)S(1)} %get-tuple-element.10) | data formatting | bytes 128 | tf_op jit(solution)/shard_map/finish/pallas_call | solution.py:383
  58.6 0.6 %copy.26 = f32[8,2]{0,1:T(2,128)} copy(f32[8,2]{1,0:T(8,128)S(1)} %get-tuple-element.11) | data formatting | bytes 128 | tf_op jit(solution)/shard_map/finish/pallas_call | solution.py:383
  59.3 0.6 %copy.27 = f32[8,2]{0,1:T(2,128)} copy(f32[8,2]{1,0:T(8,128)S(1)} %get-tuple-element.12) | data formatting | bytes 128 | tf_op jit(solution)/shard_map/finish/pallas_call | solution.py:383
Async XLA Ops:
  0.6 0.8 %copy-start.4 = (f32[8,2]{0,1:T(2,128)S(1)}, f32[8,2]{0,1:T(2,128)}, u32[]{:S(2)}) copy-start(f32[8,2]{0,1:T(2,128)} %param.8) | copy-start | bytes 196
  0.6 0.9 %copy-start.2 = (s32[8,16]{1,0:T(8,128)S(1)}, s32[8,16]{1,0:T(8,128)}, u32[]{:S(2)}) copy-start(s32[8,16]{1,0:T(8,128)} %patch_ref.1) | copy-start | bytes 1540
  1.4 0.7 %copy-start.3 = (s32[8]{0:T(128)S(1)}, s32[8]{0:T(128)}, u32[]{:S(2)}) copy-start(s32[8]{0:T(128)} %offset_ref.2) | copy-start | bytes 100
  2.1 0.8 %copy-start = (s32[8,2048]{1,0:T(8,128)S(1)}, s32[8,2048]{1,0:T(8,128)}, u32[]{:S(2)}) copy-start(s32[8,2048]{1,0:T(8,128)} %cell_ref.1) | copy-start | bytes 196612
  2.9 0.8 %copy-start.1 = (f32[8,2048]{1,0:T(8,128)S(1)}, f32[8,2048]{1,0:T(8,128)}, u32[]{:S(2)}) copy-start(f32[8,2048]{1,0:T(8,128)} %phase_ref.1) | copy-start | bytes 196612
  22.9 1.5 %collective-permute-start = (f32[16,1,4224]{2,1,0:T(1,128)S(1)}, f32[16,1,4224]{2,1,0:T(1,128)S(1)}, u32[]{:S(2)}, u32[]{:S(2)}) collective-permute-start(f32[16,1,4224]{2,1,0:T(1,128)S(1)} %all_to_all.10), channel_id=1, source_target_pairs={{0,1},{1,0},{2,3},{3,2},{4,5},{5,4},{6,7},{7,6},{8,9},{9,8},{10,11... | collective-permute-start | bytes 811016 | tf_op jit(solution)/shard_map/ppermute | solution.py:354
  47.8 2.7 %copy-start.5 = (f32[8,2]{0,1:T(2,128)S(1)}, f32[8,2]{0,1:T(2,128)}, u32[]{:S(2)}) copy-start(f32[8,2]{0,1:T(2,128)} %param.7) | copy-start | bytes 196
  47.8 9.9 %all-to-all-start.1 = ((f32[32,1,256]{2,1,0:T(1,128)}), f32[32,1,256]{2,1,0:T(1,128)S(1)}, u32[]{:S(2)}, u32[]{:S(2)}) async-start(f32[32,1,256]{2,1,0:T(1,128)} %bitcast.3), calls=%async_computation.1 | async-start | bytes 65536 | tf_op jit(solution)/shard_map/all_to_all | solution.py:378

commit v2 on v1

v2 whole, which is shorter than its diff:
```python
import functools

import jax
import jax.numpy as jnp
from jax import lax
from jax.experimental import pallas as pl
from jax.experimental.pallas import tpu as pltpu
from jax.sharding import PartitionSpec as P

PIX_OWN = 131072
MAP_PRIOR = 1.0
BASE_PRIOR = 0.1
LANES = 128
OWNER_TILES = PIX_OWN // LANES
CHANNELS = 8
BLOCK = 256
CHUNK = 32
VMEM_BYTES = 32 * 1024 * 1024

SIN_TERMS = (1.0, -1.0 / 6, 1.0 / 120, -1.0 / 5040, 1.0 / 362880, -1.0 / 39916800, 1.0 / 6227020800)
COS_TERMS = (1.0, -0.5, 1.0 / 24, -1.0 / 720, 1.0 / 40320, -1.0 / 3628800, 1.0 / 479001600, -1.0 / 87178291200)
PI_PARTS = (3.140625, 0.0009670257568359375, 6.2771141529083252e-07)


def iota(shape, dim):
    return lax.broadcasted_iota(jnp.int32, shape, dim)


def log2(number):
    assert number & (number - 1) == 0
    return number.bit_length() - 1


def split3(x):
    high = x.astype(jnp.bfloat16)
    rest = x - high.astype(jnp.float32)
    middle = rest.astype(jnp.bfloat16)
    low = (rest - middle.astype(jnp.float32)).astype(jnp.bfloat16)
    return high, middle, low


def dot(a, b):
    return jnp.dot(a, b, preferred_element_type=jnp.float32)


def exact_dot(selector, x):
    high, middle, low = split3(x)
    return (dot(selector, high) + dot(selector, middle)) + dot(selector, low)


def horner(x, terms):
    total = jnp.full_like(x, terms[-1])
    for term in terms[-2::-1]:
        total = total * x + term
    return total


def cos_sin(angle):
    turns = jnp.round(angle * (1.0 / 3.14159265358979))
    rest = angle - turns * PI_PARTS[0]
    rest = rest - turns * PI_PARTS[1]
    rest = rest - turns * PI_PARTS[2]
    half = turns * 0.5
    sign = 1.0 - 4.0 * (half - jnp.floor(half))
    square = rest * rest
    cosine = sign * horner(square, COS_TERMS)
    sine = sign * rest * horner(square, SIN_TERMS)
    return cosine, sine


def spline_weights(fraction):
    square = fraction * fraction
    cube = square * fraction
    rest = 1.0 - fraction
    first = rest * rest * rest * (1.0 / 6.0)
    second = (3.0 * cube - 6.0 * square + 4.0) * (1.0 / 6.0)
    third = (-3.0 * cube + 3.0 * square + 3.0 * fraction + 1.0) * (1.0 / 6.0)
    fourth = cube * (1.0 / 6.0)
    return (first, second, third, fourth)


def lane_gather(table, index):
    return jnp.take_along_axis(table, index, axis=1, mode="promise_in_bounds")


def send_kernel(
    ranks, cap, offset_ref, patch_ref, cell_hbm, phase_hbm, search_ref, left_ref, out_ref,
    cell_ref, phase_ref, sems,
):
    big_copies = (
        pltpu.make_async_copy(cell_hbm, cell_ref, sems.at[0]),
        pltpu.make_async_copy(phase_hbm, phase_ref, sems.at[1]),
    )
    for copy in big_copies:
        copy.start()
    dets, columns = patch_ref.shape
    blocks = dets * columns
    samples = phase_ref.shape[1]
    nodes = search_ref.shape[0]
    span = lax.axis_index("tm")
    rows = 2 * cap + 1
    square = (blocks, blocks)
    tiles = jnp.concatenate(
        [jnp.broadcast_to(patch_ref[:, c : c + 1], (dets, LANES)) for c in range(columns)], axis=0
    )
    owner = (tiles >> log2(OWNER_TILES)).astype(jnp.float32)
    owner_t = owner.T
    same = owner == owner_t
    here, there = iota(square, 0), iota(square, 1)
    rank_row = jnp.sum(jnp.where(same & (here < there), 1.0, 0.0), axis=0, keepdims=True)
    rank_col = jnp.sum(jnp.where(same & (there < here), 1.0, 0.0), axis=1, keepdims=True)
    slot_row = (owner_t[0:1, :] * cap + rank_row).astype(jnp.int32)
    place = (iota((ranks * cap, blocks), 0) == slot_row).astype(jnp.bfloat16)
    lane = iota(square, 1)
    small = iota((dets, LANES), 1)
    det_lane = iota((dets, LANES), 0)
    offsets = jnp.broadcast_to(offset_ref[...], (dets, dets))
    diagonal = iota((dets, dets), 0) == iota((dets, dets), 1)
    shift = jnp.sum(jnp.where(diagonal, offsets, 0).astype(jnp.float32), axis=1, keepdims=True)
    shift = jnp.broadcast_to(shift.astype(jnp.int32), (dets, LANES))
    start = jnp.concatenate([c * LANES - shift for c in range(columns)], axis=0) + span * samples
    which = (iota(square, 0) & (dets - 1)) + 1
    rank = rank_col.astype(jnp.int32)
    listing = jnp.where(lane == rank, start, 0) + jnp.where(lane == rank + cap, which, 0)
    listing = listing + jnp.where(lane == rank + 2 * cap, tiles + 1, 0)
    chosen = (iota((ranks, blocks), 0).astype(jnp.float32) == owner_t[0:1, :]).astype(jnp.bfloat16)
    info = exact_dot(chosen, listing.astype(jnp.float32))
    knots = jnp.zeros((1, LANES), jnp.float32)
    for kind, ref in enumerate((search_ref, left_ref)):
        for n in range(nodes):
            column = jnp.broadcast_to(ref[n : n + 1, :], (dets, dets))
            column = jnp.sum(jnp.where(diagonal, column, 0.0), axis=1, keepdims=True)
            at = (3 * cap + kind * dets * nodes + n) + det_lane * nodes
            knots = knots + jnp.sum(jnp.where(small == at, column, 0.0), axis=0, keepdims=True)
    info = info + knots
    big_copies[0].wait()
    cells = jnp.concatenate([cell_ref[:, c * LANES : (c + 1) * LANES] for c in range(columns)], axis=0)
    slot_pixel = exact_dot(place, (tiles * LANES + cells).astype(jnp.float32))
    big_copies[1].wait()
    phases = jnp.concatenate([phase_ref[:, c * LANES : (c + 1) * LANES] for c in range(columns)], axis=0)
    slot_phase = exact_dot(place, phases)
    for o in range(ranks):
        out_ref[o * rows : o * rows + cap, :] = slot_phase[o * cap : (o + 1) * cap, :]
        out_ref[o * rows + cap : o * rows + 2 * cap, :] = slot_pixel[o * cap : (o + 1) * cap, :]
        out_ref[o * rows + 2 * cap : (o + 1) * rows, :] = info[o : o + 1, :]


def main_kernel(
    ranks, cap, dets, nodes, spacing, own_ref, other_ref, out_ref, packs_ref,
    phase_ref, cell_ref, info_ref, meta_ref, few_phase, few_cell, few_info, table_ref,
    cos_ref, sin_ref, stream_ref, bin_ref, total_ref, turned_ref,
):
    slots = ranks * cap
    rows = 2 * cap + 1
    knots = ranks * nodes
    width = dets * nodes
    pages = max(1, knots // LANES)
    group = lax.axis_index("det")
    packed = knots * dets // LANES
    per_row = LANES // width
    row_count = 2 * slots // LANES

    for half, ref in enumerate((own_ref, other_ref)):
        for o in range(ranks):
            here = half * slots + o * cap
            phase_ref[here : here + cap, :] = ref[o * rows : o * rows + cap, :]
            cell_ref[here : here + cap, :] = ref[o * rows + cap : o * rows + 2 * cap, :]
            info = ref[o * rows + 2 * cap : (o + 1) * rows, :]
            info_ref[here : here + cap, :] = jnp.broadcast_to(info, (cap, LANES))
            meta_ref[half, o : o + 1, :] = info

    lists = []
    spans = LANES // cap
    for half in range(2):
        for k in range(slots // LANES):
            names = meta_ref[half, k * spans : (k + 1) * spans, :]
            lane = iota((spans, LANES), 1)
            spread = lane_gather(names, 2 * cap + (lane & (cap - 1)))
            mine = (lane >> log2(cap)) == iota((spans, LANES), 0)
            lists.append(jnp.sum(jnp.where(mine, spread, 0.0), axis=0, keepdims=True))
    names = jnp.concatenate(lists, axis=0).astype(jnp.int32)
    mine = (names > 0) & (((names - 1) & 1) == group)
    ones = jnp.where(mine, 1.0, 0.0)
    earlier = (iota((LANES, LANES), 0) < iota((LANES, LANES), 1)).astype(jnp.bfloat16)
    rank = dot(ones.astype(jnp.bfloat16), earlier)
    sums = jnp.sum(ones, axis=1, keepdims=True)
    before = [jnp.zeros((1, 1), jnp.float32)]
    for k in range(row_count):
        before.append(before[-1] + sums[k : k + 1, :])
    rank = rank + jnp.concatenate(before[:-1], axis=0)
    rank = jnp.where(mine, rank, -1.0).astype(jnp.int32)
    number = jnp.sum(ones).astype(jnp.int32)
    blocks = (number + (BLOCK - 1)) >> log2(BLOCK)
    chunks = (number + (CHUNK - 1)) >> log2(CHUNK)

    tables = [[], []]
    for half in range(2):
        side = group if half == 0 else 1 - group
        packs = []
        for kind in range(2):
            for p in range(packed):
                names = meta_ref[half, p * per_row : (p + 1) * per_row, :]
                lane = iota((per_row, LANES), 1)
                spread = lane_gather(names, (3 * cap + kind * width) + (lane & (width - 1)))
                here = (lane >> log2(width)) == iota((per_row, LANES), 0)
                line = jnp.sum(jnp.where(here, spread, 0.0), axis=0, keepdims=True)
                packs_ref[kind, pl.ds(side * packed + p, 1), :] = line
                packs.append(line)
        lane = iota((dets, LANES), 1)
        for page in range(pages):
            knot = lane + page * LANES
            index = ((knot >> log2(nodes)) & (per_row - 1)) * width
            index = index + iota((dets, LANES), 0) * nodes + (knot & (nodes - 1))
            table = jnp.zeros((dets, LANES), jnp.float32)
            for p in range(packed):
                values = lane_gather(jnp.broadcast_to(packs[p], (dets, LANES)), index)
                table = jnp.where((knot >> log2(per_row * nodes)) == p, values, table)
            tables[half].append(table)

    slot = iota((slots, LANES), 0) & (cap - 1)
    lane = iota((slots, LANES), 1)
    listed = []
    for half in range(2):
        side = group if half == 0 else 1 - group
        found = lane_gather(info_ref[half * slots : (half + 1) * slots, :], jnp.minimum(lane, 2) * cap + slot)
        listed.append(found + jnp.where(lane == 1, (side * dets).astype(jnp.float32), 0.0))
    listed = jnp.concatenate(listed, axis=0)
    pixel = cell_ref[...]
    cell = (pixel - jnp.floor(pixel * (1.0 / LANES)) * LANES).astype(jnp.bfloat16)
    source = jnp.concatenate(split3(phase_ref[...]) + split3(listed) + (cell,), axis=1)

    def gather_block(block, carry):
        at = pl.multiple_of(block * BLOCK, BLOCK)
        down = iota((BLOCK, LANES), 0) + at
        place = jnp.concatenate(
            [(down == rank[k : k + 1, :]).astype(jnp.bfloat16) for k in range(row_count)], axis=1
        )
        taken = dot(place, source)
        parts = [taken[:, k * LANES : (k + 1) * LANES] for k in range(7)]
        few_phase[pl.ds(at, BLOCK), :] = (parts[0] + parts[1]) + parts[2]
        info = (parts[3] + parts[4]) + parts[5]
        few_info[pl.ds(at, BLOCK), :] = info
        few_cell[pl.ds(at, BLOCK), :] = parts[6]
        for k in range(BLOCK // LANES):
            turned_ref[pl.ds(block * (BLOCK // LANES) + k, 1), :] = info[k * LANES : (k + 1) * LANES, :].T[2:3, :]
        chosen = (info[:, 1:2] == (iota((BLOCK, LANES), 1) + 1).astype(jnp.float32)).astype(jnp.bfloat16)
        for page in range(pages):
            first, second = tables[0][page], tables[1][page]
            low = jnp.where(group == 0, first, second)
            high = jnp.where(group == 0, second, first)
            table = jnp.concatenate(
                [low, high, jnp.zeros((LANES - 2 * dets, LANES), jnp.float32)], axis=0
            )
            table_ref[page, pl.ds(at, BLOCK), :] = exact_dot(chosen, table)
        bin_ref[pl.ds(at * CHANNELS, BLOCK * CHANNELS), :] = jnp.zeros((BLOCK * CHANNELS, LANES), jnp.float32)
        return carry

    lax.fori_loop(0, blocks, gather_block, 0)

    def spline(at):
        start = jnp.broadcast_to(few_info[pl.ds(at, CHUNK), 0:1], (CHUNK, LANES)).astype(jnp.int32)
        time = start + iota((CHUNK, LANES), 1)
        interval = time >> log2(spacing)
        fraction = (time & (spacing - 1)).astype(jnp.float32) * (1.0 / spacing)
        return start >> log2(spacing), interval, spline_weights(fraction)

    def prepare(step, carry):
        at = pl.multiple_of(step * CHUNK, CHUNK)
        cosine, sine = cos_sin(2.0 * few_phase[pl.ds(at, CHUNK), :])
        _, interval, weights = spline(at)
        stream = jnp.zeros((CHUNK, LANES), jnp.float32)
        for term in range(4):
            knot = (interval + (term - 1)) & (knots - 1)
            value = lane_gather(table_ref[0, pl.ds(at, CHUNK), :], knot & (LANES - 1))
            for page in range(1, pages):
                more = lane_gather(table_ref[page, pl.ds(at, CHUNK), :], knot & (LANES - 1))
                value = jnp.where((knot >> log2(LANES)) == page, more, value)
            stream = stream + weights[term] * value
        cos_ref[pl.ds(at, CHUNK), :] = cosine
        sin_ref[pl.ds(at, CHUNK), :] = sine
        stream_ref[pl.ds(at, CHUNK), :] = stream
        return carry

    lax.fori_loop(0, chunks, prepare, 0)

    down = iota((LANES, 2 * LANES), 0).astype(jnp.float32).astype(jnp.bfloat16)
    channel = iota((CHANNELS, LANES), 0)
    zeros = jnp.zeros((4 * CHANNELS, LANES), jnp.bfloat16)

    def collect(step, carry):
        for k in range(CHUNK // 2):
            at = step * CHUNK + 2 * k
            pieces, cells = [], []
            for slot in (at, at + 1):
                stream = jnp.broadcast_to(stream_ref[pl.ds(slot, 1), :], (CHANNELS, LANES))
                cosine = jnp.broadcast_to(cos_ref[pl.ds(slot, 1), :], (CHANNELS, LANES))
                sine = jnp.broadcast_to(sin_ref[pl.ds(slot, 1), :], (CHANNELS, LANES))
                left = jnp.where(channel < 3, stream, jnp.where(channel < 6, 1.0, cosine))
                is_one = (channel == 0) | (channel == 3)
                is_sine = (channel == 2) | (channel == 5) | (channel == 7)
                right = jnp.where(is_one, 1.0, jnp.where(is_sine, sine, cosine))
                entry = left * right
                high = entry.astype(jnp.bfloat16).astype(jnp.float32)
                rest = entry - high
                middle = rest.astype(jnp.bfloat16).astype(jnp.float32)
                low = rest - middle
                stack = jnp.concatenate([high, middle, low, jnp.zeros_like(low)], axis=0)
                pieces.append(stack.astype(jnp.bfloat16))
                cells.append(jnp.broadcast_to(few_cell[pl.ds(slot, 1), :].astype(jnp.bfloat16), (LANES, LANES)))
            entry = jnp.concatenate(
                [
                    jnp.concatenate([pieces[0], zeros], axis=1),
                    jnp.concatenate([zeros, pieces[1]], axis=1),
                ],
                axis=0,
            )
            hits = jnp.where(jnp.concatenate(cells, axis=1) == down, jnp.bfloat16(1), jnp.bfloat16(0))
            sums = lax.dot_general(
                entry, hits, (((1,), (1,)), ((), ())), preferred_element_type=jnp.float32
            )
            for m in range(2):
                base = 4 * CHANNELS * m
                bin_ref[pl.ds((at + m) * CHANNELS, CHANNELS), :] = (
                    sums[base : base + CHANNELS] + sums[base + CHANNELS : base + 2 * CHANNELS]
                ) + sums[base + 2 * CHANNELS : base + 3 * CHANNELS]
        return carry

    lax.fori_loop(0, chunks, collect, 0)

    def merge(block, carry):
        at = pl.multiple_of(block * BLOCK, BLOCK)
        names = few_info[pl.ds(at, BLOCK), 2:3]

        def add(other, carry):
            there = pl.multiple_of(other * BLOCK, BLOCK)
            across = [
                turned_ref[pl.ds(other * (BLOCK // LANES) + k, 1), :] for k in range(BLOCK // LANES)
            ]
            same = (names == jnp.concatenate(across, axis=1)).astype(jnp.bfloat16)
            for c in range(CHANNELS):
                binned = bin_ref[pl.ds(there * CHANNELS + c, BLOCK, stride=CHANNELS), :]
                share = exact_dot(same, binned)
                before = total_ref[c, pl.ds(at, BLOCK), :]
                total_ref[c, pl.ds(at, BLOCK), :] = jnp.where(other == 0, share, before + share)
            return carry

        lax.fori_loop(0, blocks, add, 0)
        return carry

    lax.fori_loop(0, blocks, merge, 0)

    def project(step, lines):
        at = pl.multiple_of(step * CHUNK, CHUNK)
        here = pl.ds(at, CHUNK)
        signal, signal_cos, signal_sin, count, cos_sum, sin_sum, cos_cos, cos_sin_sum = (
            total_ref[c, here, :] for c in range(CHANNELS)
        )
        sin_sin = count - cos_cos
        stokes_i = count + MAP_PRIOR
        stokes_q = cos_cos + MAP_PRIOR
        stokes_u = sin_sin + MAP_PRIOR
        minor_one = stokes_q * stokes_u - cos_sin_sum * cos_sin_sum
        minor_two = sin_sum * cos_sin_sum - cos_sum * stokes_u
        minor_three = cos_sum * cos_sin_sum - sin_sum * stokes_q
        minor_four = stokes_i * stokes_u - sin_sum * sin_sum
        minor_five = cos_sum * sin_sum - stokes_i * cos_sin_sum
        minor_six = stokes_i * stokes_q - cos_sum * cos_sum
        determinant = stokes_i * minor_one + cos_sum * minor_two + sin_sum * minor_three
        scale = 1.0 / determinant
        map_i = (minor_one * signal + minor_two * signal_cos + minor_three * signal_sin) * scale
        map_q = (minor_two * signal + minor_four * signal_cos + minor_five * signal_sin) * scale
        map_u = (minor_three * signal + minor_five * signal_cos + minor_six * signal_sin) * scale
        cell = few_cell[here, :].astype(jnp.int32)
        projected = (
            lane_gather(map_i, cell) + cos_ref[here, :] * lane_gather(map_q, cell)
        ) + sin_ref[here, :] * lane_gather(map_u, cell)
        which = few_info[here, 1:2].astype(jnp.int32) - 1
        cleaned = jnp.where(which >= 0, stream_ref[here, :] - projected, 0.0)
        base, interval, weights = spline(at)
        early = interval == base
        lane = iota((CHUNK, LANES), 1)
        side = which >> log2(dets)
        det = which & (dets - 1)
        lines = list(lines)
        for term in range(5):
            low = weights[term] if term < 4 else 0.0
            high = weights[term - 1] if term > 0 else 0.0
            value = jnp.sum(jnp.where(early, low, high) * cleaned, axis=1, keepdims=True)
            knot = (base + (term - 1)) & (knots - 1)
            spot = side * (knots * dets) + (knot >> log2(nodes)) * width + det * nodes
            spot = spot + (knot & (nodes - 1))
            for p in range(2 * packed):
                part = jnp.where(lane + p * LANES == spot, value, 0.0)
                for q in range(CHUNK // 8):
                    lines[p] = lines[p] + part[q * 8 : (q + 1) * 8, :]
        return tuple(lines)

    lines = tuple(jnp.zeros((8, LANES), jnp.float32) for _ in range(2 * packed))
    lines = lax.fori_loop(0, chunks, project, lines)
    partial = jnp.concatenate([jnp.sum(line, axis=0, keepdims=True) for line in lines], axis=0)
    for target in range(out_ref.shape[0] // (2 * packed)):
        out_ref[target * 2 * packed : (target + 1) * 2 * packed, :] = partial


def finish_kernel(
    ranks, spacing, arrived_ref, packs_ref, offset_ref, left_ref, search_ref,
    new_offset_ref, new_left_ref, new_search_ref,
):
    nodes, dets = search_ref.shape
    height = packs_ref.shape[1]
    total = arrived_ref[0:height, :]
    for o in range(1, arrived_ref.shape[0] // height):
        total = total + arrived_ref[o * height : (o + 1) * height, :]
    search, left = packs_ref[0], packs_ref[1]
    image = total * (1.0 / spacing) + BASE_PRIOR * search
    norm_old = jnp.sum(left * left, keepdims=True)
    stride_factor = norm_old / jnp.sum(search * image, keepdims=True)
    fresh = left - stride_factor * image
    beta = jnp.sum(fresh * fresh, keepdims=True) / norm_old
    span, group = lax.axis_index("tm"), lax.axis_index("det")
    per_row = LANES // (dets * nodes)
    row = group * (height // 2) + (span >> log2(per_row))
    mine = jnp.sum(jnp.where(iota((height, LANES), 0) == row, image, 0.0), axis=0, keepdims=True)
    lane = iota((8, LANES), 1)
    first = (span & (per_row - 1)) * (dets * nodes)
    index = first + (lane & (dets - 1)) * nodes + (iota((8, LANES), 0) & (nodes - 1))
    mine = lane_gather(jnp.broadcast_to(mine, (8, LANES)), index)[:nodes, :dets]
    new_offset_ref[...] = offset_ref[...] + stride_factor * search_ref[...]
    new_left = left_ref[...] - stride_factor * mine
    new_left_ref[...] = new_left
    new_search_ref[...] = new_left + beta * search_ref[...]


def body(
    offset_coeffs,
    leftover_error,
    search_vector,
    node_lattice_offset,
    sky_cell_in_patch,
    analyser_reading_phase,
    segment_sky_patch,
):
    ranks, groups = lax.axis_size("tm"), lax.axis_size("det")
    dets, samples = analyser_reading_phase.shape
    nodes = search_vector.shape[1]
    spacing = samples // nodes
    blocks = segment_sky_patch.size
    cap = max(2, 2 * blocks // ranks)
    slots = ranks * cap
    rows = 2 * cap + 1
    height = groups * ranks * nodes * dets // LANES
    vmem = pl.BlockSpec(memory_space=pltpu.VMEM)
    hbm = pl.BlockSpec(memory_space=pltpu.HBM)
    params = pltpu.CompilerParams(vmem_limit_bytes=VMEM_BYTES)
    search, left, coeffs = search_vector.T, leftover_error.T, offset_coeffs.T

    outgoing = pl.pallas_call(
        functools.partial(send_kernel, ranks, cap),
        out_shape=jax.ShapeDtypeStruct((ranks * rows, LANES), jnp.float32),
        in_specs=[vmem, vmem, hbm, hbm, vmem, vmem],
        out_specs=vmem,
        scratch_shapes=[
            pltpu.VMEM((dets, samples), jnp.int32),
            pltpu.VMEM((dets, samples), jnp.float32),
            pltpu.SemaphoreType.DMA((2,)),
        ],
        compiler_params=params,
        name="send",
    )(
        node_lattice_offset.reshape(1, dets), segment_sky_patch, sky_cell_in_patch,
        analyser_reading_phase, search, left,
    )
    arrived = lax.all_to_all(
        outgoing.reshape(ranks, 1, rows * LANES), "tm", split_axis=0, concat_axis=0, tiled=True
    )
    swap = [(i, groups - 1 - i) for i in range(groups)]
    other = lax.ppermute(arrived, "det", swap)
    pages = max(1, ranks * nodes // LANES)
    big = pltpu.VMEM((2 * slots, LANES), jnp.float32)
    partials, packs = pl.pallas_call(
        functools.partial(main_kernel, ranks, cap, dets, nodes, spacing),
        out_shape=(
            jax.ShapeDtypeStruct((ranks * groups * height, LANES), jnp.float32),
            jax.ShapeDtypeStruct((2, height, LANES), jnp.float32),
        ),
        in_specs=[vmem] * 2,
        out_specs=(vmem, vmem),
        scratch_shapes=[
            big, big, big,
            pltpu.VMEM((2, ranks, LANES), jnp.float32),
            big, big, big,
            pltpu.VMEM((pages, 2 * slots, LANES), jnp.float32),
            big, big, big,
            pltpu.VMEM((2 * slots * CHANNELS, LANES), jnp.float32),
            pltpu.VMEM((CHANNELS, 2 * slots, LANES), jnp.float32),
            pltpu.VMEM((max(8, 2 * slots // LANES), LANES), jnp.float32),
        ],
        compiler_params=params,
        name="main",
    )(arrived.reshape(ranks * rows, LANES), other.reshape(ranks * rows, LANES))
    gathered = lax.all_to_all(
        partials.reshape(ranks * groups, 1, height * LANES),
        ("tm", "det"), split_axis=0, concat_axis=0, tiled=True,
    )
    small = jax.ShapeDtypeStruct((nodes, dets), jnp.float32)
    results = pl.pallas_call(
        functools.partial(finish_kernel, ranks, spacing),
        out_shape=(small, small, small),
        in_specs=[vmem] * 5,
        out_specs=(vmem, vmem, vmem),
        compiler_params=params,
        name="finish",
    )(gathered.reshape(ranks * groups * height, LANES), packs, coeffs, left, search)
    return tuple(result.T for result in results)


def solution(mesh):
    return jax.shard_map(
        body,
        mesh=mesh,
        in_specs=(
            P("det", "tm"),
            P("det", "tm"),
            P("det", "tm"),
            P("det"),
            P("det", "tm"),
            P("det", "tm"),
            P("det", "tm"),
        ),
        out_specs=(P("det", "tm"), P("det", "tm"), P("det", "tm")),
        check_vma=False,
    )
```

time: 60.2 us -> 42.7 us (0.71)
  Pallas kernels: 24.6 us -> 8.56 us
  blocking collectives: 18.1 us -> 27.9 us
  waiting for transfers between devices: 8.7 us -> 1.54 us
  starting transfers between devices: 2.66 us -> 0.01 us
  local copies, waits for them, and re-layouts: 5.1 us -> 3.71 us
    pallas_call x1, Pallas kernels: 23.4 us -> 6.68 us  [body(): pl.pallas_call(functools.partial(main_kernel, ranks, cap, dets, nodes, sp...]
    all_to_all x0 -> x1, blocking collectives: none -> 9.77 us  [body(): lax.all_to_all(partials.reshape(ranks * groups, 1, height * LANES), ('tm'...]
    all_to_all x1 -> x0, waiting for transfers between devices: 7.16 us -> none  [body(): lax.all_to_all(partials.reshape(ranks * groups, 1, packed * LANES), ('tm'...]
    all_to_all x1 -> x0, starting transfers between devices: 2.65 us -> none  [body(): lax.all_to_all(partials.reshape(ranks * groups, 1, packed * LANES), ('tm'...]
    pallas_call x3 -> x0, local copies, waits for them, and re-layouts: 1.91 us -> none  [body(): pl.pallas_call(functools.partial(finish_kernel, ranks, spacing), out_shap...]
    unnamed x15 -> x16, local copies, waits for them, and re-layouts: 3.19 us -> 3.71 us
  transfers between devices with their start and end apart: 2 -> 1, of which waited for: 2 -> 1; matrix products, arithmetic and copies ran while one was open for 0% -> 0% of each run, Pallas kernels for 0% -> 0%
where the time goes in v2:
time: 42.7 us; the launch traced here: 42.4 us
  blocking collectives  27.9 us (65%)
  Pallas kernels  8.56 us (20%)
  local copies, waits for them, and re-layouts  3.71 us (9%)
  waiting for transfers between devices  1.54 us (4%)
  between operations  0.69 us (2%)
    all_to_all x1, blocking collectives, body(): lax.all_to_all(outgoing.reshape(ranks, 1, rows * LANES), 'tm', split_axis...  18.1 us
    all_to_all x1, blocking collectives, body(): lax.all_to_all(partials.reshape(ranks * groups, 1, height * LANES), ('tm'...  9.77 us
    pallas_call x1, Pallas kernels, body(): pl.pallas_call(functools.partial(main_kernel, ranks, cap, dets, nodes, sp...  6.68 us
    unnamed x16, local copies, waits for them, and re-layouts  3.71 us
    ppermute x1, waiting for transfers between devices, body(): other = lax.ppermute(arrived, 'det', swap)  1.54 us
    pallas_call x1, Pallas kernels, body(): pl.pallas_call(functools.partial(send_kernel, ranks, cap), out_shape=jax....  1.03 us
  transfers between devices with their start and end apart: 1, of which 1 were waited for; matrix products, arithmetic and copies ran while one was open for 0% of the time, Pallas kernels for 0%

profile of v2, /device:TPU:0, one launch (start us, length us, event | category | flops | bytes accessed | tf_op | source)
XLA Modules:
  0.0 42.4 jit_solution(16057037059406960099)
XLA Ops:
  0.6 0.0 copy-start.2
  0.6 0.0 copy-start.3
  0.7 0.0 copy-start.7
  0.7 0.7 %copy-done.2 = s32[8,16]{1,0:T(8,128)S(1)} copy-done((s32[8,16]{1,0:T(8,128)S(1)}, s32[8,16]{1,0:T(8,128)}, u32[]{:S(2)}) %copy-start.2) | copy-done | bytes 536
  1.3 0.0 copy-done.3
  1.3 0.0 copy-done.7
  1.3 0.0 copy-start
  1.3 0.8 %copy-done = s32[8,2048]{1,0:T(8,128)S(1)} copy-done((s32[8,2048]{1,0:T(8,128)S(1)}, s32[8,2048]{1,0:T(8,128)}, u32[]{:S(2)}) %copy-start) | copy-done | bytes 65560
  2.2 0.0 copy-start.1
  2.2 0.8 %copy-done.1 = f32[8,2048]{1,0:T(8,128)S(1)} copy-done((f32[8,2048]{1,0:T(8,128)S(1)}, f32[8,2048]{1,0:T(8,128)}, u32[]{:S(2)}) %copy-start.1) | copy-done | bytes 65560
  3.0 0.0 copy-start.4
  3.0 0.7 %copy-done.4 = f32[8,2]{0,1:T(2,128)S(1)} copy-done((f32[8,2]{0,1:T(2,128)S(1)}, f32[8,2]{0,1:T(2,128)}, u32[]{:S(2)}) %copy-start.4) | copy-done | bytes 88
  3.7 1.0 %send.1 = f32[528,128]{1,0:T(8,128)S(1)} custom-call(s32[1,8]{1,0:T(1,128)S(1)} %bitcast.22, s32[8,16]{1,0:T(8,128)S(1)} %copy-done.2, s32[8,2048]{1,0:T(8,128)S(1)} %copy-done, f32[8,2048]{1,0:T(8,128)S(1)} %copy-done.1, f32[2,8]{1,0:T(2,128)S(1)} %bitcast.17, f32[2,8]{1,0:T(2,128)S(1)} %bitcast.19), custom_call_target="tpu_custom_call" | custom-call | tf_op jit(solution)/shard_map/send/pallas_call | solution.py:457
  4.7 18.1 %all_to_all.10 = f32[16,1,4224]{2,1,0:T(1,128)S(1)} all-to-all(f32[16,1,4224]{2,1,0:T(1,128)S(1)} %bitcast.13), channel_id=1, replica_groups=mesh['tm'=16,'det'=2] {'tm'}, dimensions={0} | all-to-all | bytes 540672 | tf_op jit(solution)/shard_map/all_to_all | solution.py:473
  22.9 0.0 collective-permute-start
  22.9 1.5 %collective-permute-done = f32[16,1,4224]{2,1,0:T(1,128)S(1)} collective-permute-done((f32[16,1,4224]{2,1,0:T(1,128)S(1)}, f32[16,1,4224]{2,1,0:T(1,128)S(1)}, u32[]{:S(2)}, u32[]{:S(2)}) %collective-permute-start) | collective-permute-done | bytes 270368 | tf_op jit(solution)/shard_map/ppermute | solution.py:477
  24.4 6.7 %main.1 = (f32[128,128]{1,0:T(8,128)S(1)}, f32[2,4,128]{2,1,0:T(4,128)S(1)}) custom-call(f32[528,128]{1,0:T(8,128)S(1)} %bitcast.12, f32[528,128]{1,0:T(8,128)S(1)} %bitcast.14), custom_call_target="tpu_custom_call" | custom-call | tf_op jit(solution)/shard_map/main/pallas_call | solution.py:480
  31.1 0.0 copy-start.6
  31.1 9.8 %all_to_all.11 = f32[32,1,512]{2,1,0:T(1,128)S(1)} all-to-all(f32[32,1,512]{2,1,0:T(1,128)S(1)} %bitcast.16), channel_id=1, replica_groups=mesh['tm'=16,'det'=2] {'tm','det'}, dimensions={0} | all-to-all | bytes 131072 | tf_op jit(solution)/shard_map/all_to_all | solution.py:501
  40.9 0.0 copy-start.5
  40.9 0.0 copy-done.6
  40.9 0.7 %copy-done.5 = f32[8,2]{0,1:T(2,128)S(1)} copy-done((f32[8,2]{0,1:T(2,128)S(1)}, f32[8,2]{0,1:T(2,128)}, u32[]{:S(2)}) %copy-start.5) | copy-done | bytes 88
  41.6 0.8 %finish.1 = (f32[2,8]{1,0:T(2,128)}, f32[2,8]{1,0:T(2,128)}, f32[2,8]{1,0:T(2,128)}) custom-call(f32[128,128]{1,0:T(8,128)S(1)} %bitcast.15, f32[2,4,128]{2,1,0:T(4,128)S(1)} %get-tuple-element.9.packs_ref, f32[2,8]{1,0:T(2,128)S(1)} %bitcast.21, f32[2,8]{1,0:T(2,128)S(1)} %bitcast.20, f32[2,8]{1,0:T(2,128)S(1)} %bitcast.18), custom_call_target="tpu_custom_call" | custom-call | tf_op jit(solution)/shard_map/finish/pallas_call | solution.py:506
Async XLA Ops:
  0.6 0.7 %copy-start.2 = (s32[8,16]{1,0:T(8,128)S(1)}, s32[8,16]{1,0:T(8,128)}, u32[]{:S(2)}) copy-start(s32[8,16]{1,0:T(8,128)} %patch_ref.1) | copy-start | bytes 1540
  0.6 0.7 %copy-start.3 = (f32[8,2]{0,1:T(2,128)S(1)}, f32[8,2]{0,1:T(2,128)}, u32[]{:S(2)}) copy-start(f32[8,2]{0,1:T(2,128)} %param.9) | copy-start | bytes 196
  0.7 0.7 %copy-start.7 = (s32[8]{0:T(128)S(1)}, s32[8]{0:T(128)}, u32[]{:S(2)}) copy-start(s32[8]{0:T(128)} %param.10) | copy-start | bytes 100
  1.3 0.8 %copy-start = (s32[8,2048]{1,0:T(8,128)S(1)}, s32[8,2048]{1,0:T(8,128)}, u32[]{:S(2)}) copy-start(s32[8,2048]{1,0:T(8,128)} %cell_hbm.1) | copy-start | bytes 196612
  2.2 0.8 %copy-start.1 = (f32[8,2048]{1,0:T(8,128)S(1)}, f32[8,2048]{1,0:T(8,128)}, u32[]{:S(2)}) copy-start(f32[8,2048]{1,0:T(8,128)} %phase_hbm.1) | copy-start | bytes 196612
  3.0 0.7 %copy-start.4 = (f32[8,2]{0,1:T(2,128)S(1)}, f32[8,2]{0,1:T(2,128)}, u32[]{:S(2)}) copy-start(f32[8,2]{0,1:T(2,128)} %param.8) | copy-start | bytes 196
  22.9 1.5 %collective-permute-start = (f32[16,1,4224]{2,1,0:T(1,128)S(1)}, f32[16,1,4224]{2,1,0:T(1,128)S(1)}, u32[]{:S(2)}, u32[]{:S(2)}) collective-permute-start(f32[16,1,4224]{2,1,0:T(1,128)S(1)} %all_to_all.10), channel_id=1, source_target_pairs={{0,1},{1,0},{2,3},{3,2},{4,5},{5,4},{6,7},{7,6},{8,9},{9,8},{10,11... | collective-permute-start | bytes 811016 | tf_op jit(solution)/shard_map/ppermute | solution.py:477
  31.1 9.8 %copy-start.6 = (f32[8,2]{0,1:T(2,128)S(1)}, f32[8,2]{0,1:T(2,128)}, u32[]{:S(2)}) copy-start(f32[8,2]{0,1:T(2,128)} %param.7) | copy-start | bytes 196
  40.9 0.7 %copy-start.5 = (f32[8,2]{0,1:T(2,128)S(1)}, f32[8,2]{0,1:T(2,128)}, u32[]{:S(2)}) copy-start(f32[8,2]{0,1:T(2,128)} %param.8) | copy-start | bytes 196

commit v3 on v2

--- a/solution.py
+++ b/solution.py
@@ -84,15 +84,17 @@
 
 
 def send_kernel(
-    ranks, cap, offset_ref, patch_ref, cell_hbm, phase_hbm, search_ref, left_ref, out_ref,
-    cell_ref, phase_ref, sems,
+    ranks, cap, patch_hbm, offset_hbm, search_hbm, left_hbm, cell_hbm, phase_hbm, out_ref,
+    patch_ref, offset_ref, search_ref, left_ref, cell_ref, phase_ref, sems,
 ):
-    big_copies = (
-        pltpu.make_async_copy(cell_hbm, cell_ref, sems.at[0]),
-        pltpu.make_async_copy(phase_hbm, phase_ref, sems.at[1]),
+    pairs = (
+        (patch_hbm, patch_ref), (offset_hbm, offset_ref), (search_hbm, search_ref),
+        (left_hbm, left_ref), (cell_hbm, cell_ref), (phase_hbm, phase_ref),
     )
-    for copy in big_copies:
+    copies = [pltpu.make_async_copy(src, dst, sems.at[k]) for k, (src, dst) in enumerate(pairs)]
+    for copy in copies:
         copy.start()
+    copies[0].wait()
     dets, columns = patch_ref.shape
     blocks = dets * columns
     samples = phase_ref.shape[1]
@@ -114,6 +116,8 @@
     lane = iota(square, 1)
     small = iota((dets, LANES), 1)
     det_lane = iota((dets, LANES), 0)
+    for copy in copies[1:4]:
+        copy.wait()
     offsets = jnp.broadcast_to(offset_ref[...], (dets, dets))
     diagonal = iota((dets, dets), 0) == iota((dets, dets), 1)
     shift = jnp.sum(jnp.where(diagonal, offsets, 0).astype(jnp.float32), axis=1, keepdims=True)
@@ -133,10 +137,10 @@
             at = (3 * cap + kind * dets * nodes + n) + det_lane * nodes
             knots = knots + jnp.sum(jnp.where(small == at, column, 0.0), axis=0, keepdims=True)
     info = info + knots
-    big_copies[0].wait()
+    copies[4].wait()
     cells = jnp.concatenate([cell_ref[:, c * LANES : (c + 1) * LANES] for c in range(columns)], axis=0)
     slot_pixel = exact_dot(place, (tiles * LANES + cells).astype(jnp.float32))
-    big_copies[1].wait()
+    copies[5].wait()
     phases = jnp.concatenate([phase_ref[:, c * LANES : (c + 1) * LANES] for c in range(columns)], axis=0)
     slot_phase = exact_dot(place, phases)
     for o in range(ranks):
@@ -146,10 +150,12 @@
 
 
 def main_kernel(
-    ranks, cap, dets, nodes, spacing, own_ref, other_ref, out_ref, packs_ref,
+    ranks, cap, dets, nodes, spacing, own_ref, other_ref, coeffs_hbm, out_ref, packs_ref, coeffs_ref,
     phase_ref, cell_ref, info_ref, meta_ref, few_phase, few_cell, few_info, table_ref,
-    cos_ref, sin_ref, stream_ref, bin_ref, total_ref, turned_ref,
+    cos_ref, sin_ref, stream_ref, bin_ref, total_ref, turned_ref, sems,
 ):
+    coeffs_copy = pltpu.make_async_copy(coeffs_hbm, coeffs_ref, sems.at[0])
+    coeffs_copy.start()
     slots = ranks * cap
     rows = 2 * cap + 1
     knots = ranks * nodes
@@ -400,13 +406,13 @@
     partial = jnp.concatenate([jnp.sum(line, axis=0, keepdims=True) for line in lines], axis=0)
     for target in range(out_ref.shape[0] // (2 * packed)):
         out_ref[target * 2 * packed : (target + 1) * 2 * packed, :] = partial
+    coeffs_copy.wait()
 
 
 def finish_kernel(
-    ranks, spacing, arrived_ref, packs_ref, offset_ref, left_ref, search_ref,
-    new_offset_ref, new_left_ref, new_search_ref,
+    ranks, spacing, arrived_ref, packs_ref, coeffs_ref, new_offset_ref, new_left_ref, new_search_ref,
 ):
-    nodes, dets = search_ref.shape
+    nodes, dets = coeffs_ref.shape
     height = packs_ref.shape[1]
     total = arrived_ref[0:height, :]
     for o in range(1, arrived_ref.shape[0] // height):
@@ -420,15 +426,20 @@
     span, group = lax.axis_index("tm"), lax.axis_index("det")
     per_row = LANES // (dets * nodes)
     row = group * (height // 2) + (span >> log2(per_row))
-    mine = jnp.sum(jnp.where(iota((height, LANES), 0) == row, image, 0.0), axis=0, keepdims=True)
     lane = iota((8, LANES), 1)
     first = (span & (per_row - 1)) * (dets * nodes)
     index = first + (lane & (dets - 1)) * nodes + (iota((8, LANES), 0) & (nodes - 1))
-    mine = lane_gather(jnp.broadcast_to(mine, (8, LANES)), index)[:nodes, :dets]
-    new_offset_ref[...] = offset_ref[...] + stride_factor * search_ref[...]
-    new_left = left_ref[...] - stride_factor * mine
-    new_left_ref[...] = new_left
-    new_search_ref[...] = new_left + beta * search_ref[...]
+    here = iota((height, LANES), 0) == row
+
+    def own(x):
+        line = jnp.sum(jnp.where(here, x, 0.0), axis=0, keepdims=True)
+        return lane_gather(jnp.broadcast_to(line, (8, LANES)), index)[:nodes, :dets]
+
+    my_search = own(search)
+    my_left = own(fresh)
+    new_offset_ref[...] = coeffs_ref[...] + stride_factor * my_search
+    new_left_ref[...] = my_left
+    new_search_ref[...] = my_left + beta * my_search
 
 
 def body(
@@ -451,25 +462,24 @@
     height = groups * ranks * nodes * dets // LANES
     vmem = pl.BlockSpec(memory_space=pltpu.VMEM)
     hbm = pl.BlockSpec(memory_space=pltpu.HBM)
+    pin = functools.partial(pltpu.with_memory_space_constraint, memory_space=pltpu.HBM)
     params = pltpu.CompilerParams(vmem_limit_bytes=VMEM_BYTES)
-    search, left, coeffs = search_vector.T, leftover_error.T, offset_coeffs.T
+    inputs = (
+        segment_sky_patch, node_lattice_offset.reshape(1, dets), search_vector.T, leftover_error.T,
+        sky_cell_in_patch, analyser_reading_phase,
+    )
+    small = jax.ShapeDtypeStruct((nodes, dets), jnp.float32)
 
     outgoing = pl.pallas_call(
         functools.partial(send_kernel, ranks, cap),
         out_shape=jax.ShapeDtypeStruct((ranks * rows, LANES), jnp.float32),
-        in_specs=[vmem, vmem, hbm, hbm, vmem, vmem],
+        in_specs=[hbm] * len(inputs),
         out_specs=vmem,
-        scratch_shapes=[
-            pltpu.VMEM((dets, samples), jnp.int32),
-            pltpu.VMEM((dets, samples), jnp.float32),
-            pltpu.SemaphoreType.DMA((2,)),
-        ],
+        scratch_shapes=[pltpu.VMEM(x.shape, x.dtype) for x in inputs]
+        + [pltpu.SemaphoreType.DMA((len(inputs),))],
         compiler_params=params,
         name="send",
-    )(
-        node_lattice_offset.reshape(1, dets), segment_sky_patch, sky_cell_in_patch,
-        analyser_reading_phase, search, left,
-    )
+    )(*[pin(x) for x in inputs])
     arrived = lax.all_to_all(
         outgoing.reshape(ranks, 1, rows * LANES), "tm", split_axis=0, concat_axis=0, tiled=True
     )
@@ -477,14 +487,15 @@
     other = lax.ppermute(arrived, "det", swap)
     pages = max(1, ranks * nodes // LANES)
     big = pltpu.VMEM((2 * slots, LANES), jnp.float32)
-    partials, packs = pl.pallas_call(
+    partials, packs, coeffs = pl.pallas_call(
         functools.partial(main_kernel, ranks, cap, dets, nodes, spacing),
         out_shape=(
             jax.ShapeDtypeStruct((ranks * groups * height, LANES), jnp.float32),
             jax.ShapeDtypeStruct((2, height, LANES), jnp.float32),
+            small,
         ),
-        in_specs=[vmem] * 2,
-        out_specs=(vmem, vmem),
+        in_specs=[vmem, vmem, hbm],
+        out_specs=(vmem, vmem, vmem),
         scratch_shapes=[
             big, big, big,
             pltpu.VMEM((2, ranks, LANES), jnp.float32),
@@ -494,23 +505,23 @@
             pltpu.VMEM((2 * slots * CHANNELS, LANES), jnp.float32),
             pltpu.VMEM((CHANNELS, 2 * slots, LANES), jnp.float32),
             pltpu.VMEM((max(8, 2 * slots // LANES), LANES), jnp.float32),
+            pltpu.SemaphoreType.DMA((1,)),
         ],
         compiler_params=params,
         name="main",
-    )(arrived.reshape(ranks * rows, LANES), other.reshape(ranks * rows, LANES))
+    )(arrived.reshape(ranks * rows, LANES), other.reshape(ranks * rows, LANES), pin(offset_coeffs.T))
     gathered = lax.all_to_all(
         partials.reshape(ranks * groups, 1, height * LANES),
         ("tm", "det"), split_axis=0, concat_axis=0, tiled=True,
     )
-    small = jax.ShapeDtypeStruct((nodes, dets), jnp.float32)
     results = pl.pallas_call(
         functools.partial(finish_kernel, ranks, spacing),
         out_shape=(small, small, small),
-        in_specs=[vmem] * 5,
+        in_specs=[vmem] * 3,
         out_specs=(vmem, vmem, vmem),
         compiler_params=params,
         name="finish",
-    )(gathered.reshape(ranks * groups * height, LANES), packs, coeffs, left, search)
+    )(gathered.reshape(ranks * groups * height, LANES), packs, coeffs)
     return tuple(result.T for result in results)
 
 

time: 42.7 us -> 39.4 us (0.923)
  local copies, waits for them, and re-layouts: 3.71 us -> 0 us
  Pallas kernels: 8.56 us -> 9.27 us
    unnamed x16 -> x0, local copies, waits for them, and re-layouts: 3.71 us -> none
    pallas_call x1, Pallas kernels: 1.03 us -> 1.72 us  [body(): pl.pallas_call(functools.partial(send_kernel, ranks, cap), out_shape=jax....]
where the time goes in v3:
time: 39.4 us; the launch traced here: 39.1 us
  blocking collectives  27.6 us (70%)
  Pallas kernels  9.27 us (24%)
  waiting for transfers between devices  1.54 us (4%)
  between operations  0.65 us (2%)
    all_to_all x1, blocking collectives, body(): lax.all_to_all(outgoing.reshape(ranks, 1, rows * LANES), 'tm', split_axis...  18.1 us
    all_to_all x1, blocking collectives, body(): lax.all_to_all(partials.reshape(ranks * groups, 1, height * LANES), ('tm'...  9.5 us
    pallas_call x1, Pallas kernels, body(): pl.pallas_call(functools.partial(main_kernel, ranks, cap, dets, nodes, sp...  6.69 us
    pallas_call x1, Pallas kernels, body(): pl.pallas_call(functools.partial(send_kernel, ranks, cap), out_shape=jax....  1.72 us
    ppermute x1, waiting for transfers between devices, body(): other = lax.ppermute(arrived, 'det', swap)  1.54 us
    pallas_call x1, Pallas kernels, body(): pl.pallas_call(functools.partial(finish_kernel, ranks, spacing), out_shap...  0.85 us
  transfers between devices with their start and end apart: 1, of which 1 were waited for; matrix products, arithmetic and copies ran while one was open for 0% of the time, Pallas kernels for 0%

profile of v3, /device:TPU:0, one launch (start us, length us, event | category | flops | bytes accessed | tf_op | source)
XLA Modules:
  0.0 39.1 jit_solution(11180840646445402207)
XLA Ops:
  0.6 1.7 %send.1 = f32[528,128]{1,0:T(8,128)S(1)} custom-call(s32[8,16]{1,0:T(8,128)} %patch_hbm.1, s32[1,8]{1,0:T(1,128)} %bitcast.20, f32[2,8]{1,0:T(2,128)} %bitcast.17, f32[2,8]{1,0:T(2,128)} %bitcast.18, s32[8,2048]{1,0:T(8,128)} %cell_hbm.1, f32[8,2048]{1,0:T(8,128)} %phase_hbm.1), custom_call_target="tpu_custom_call" | custom-call | tf_op jit(solution)/shard_map/send/pallas_call | solution.py:473
  2.4 18.1 %all_to_all.10 = f32[16,1,4224]{2,1,0:T(1,128)S(1)} all-to-all(f32[16,1,4224]{2,1,0:T(1,128)S(1)} %bitcast.13), channel_id=1, replica_groups=mesh['tm'=16,'det'=2] {'tm'}, dimensions={0} | all-to-all | bytes 540672 | tf_op jit(solution)/shard_map/all_to_all | solution.py:483
  20.5 0.0 collective-permute-start
  20.5 1.5 %collective-permute-done = f32[16,1,4224]{2,1,0:T(1,128)S(1)} collective-permute-done((f32[16,1,4224]{2,1,0:T(1,128)S(1)}, f32[16,1,4224]{2,1,0:T(1,128)S(1)}, u32[]{:S(2)}, u32[]{:S(2)}) %collective-permute-start) | collective-permute-done | bytes 270368 | tf_op jit(solution)/shard_map/ppermute | solution.py:487
  22.0 6.7 %main.1 = (f32[128,128]{1,0:T(8,128)S(1)}, f32[2,4,128]{2,1,0:T(4,128)S(1)}, f32[2,8]{1,0:T(2,128)S(1)}) custom-call(f32[528,128]{1,0:T(8,128)S(1)} %bitcast.12, f32[528,128]{1,0:T(8,128)S(1)} %bitcast.14, f32[2,8]{1,0:T(2,128)} %bitcast.19), custom_call_target="tpu_custom_call" | custom-call | tf_op jit(solution)/shard_map/main/pallas_call | solution.py:490
  28.7 9.5 %all_to_all.11 = f32[32,1,512]{2,1,0:T(1,128)S(1)} all-to-all(f32[32,1,512]{2,1,0:T(1,128)S(1)} %bitcast.16), channel_id=1, replica_groups=mesh['tm'=16,'det'=2] {'tm','det'}, dimensions={0} | all-to-all | bytes 131072 | tf_op jit(solution)/shard_map/all_to_all | solution.py:513
  38.3 0.8 %finish.1 = (f32[2,8]{1,0:T(2,128)}, f32[2,8]{1,0:T(2,128)}, f32[2,8]{1,0:T(2,128)}) custom-call(f32[128,128]{1,0:T(8,128)S(1)} %bitcast.15, f32[2,4,128]{2,1,0:T(4,128)S(1)} %get-tuple-element.10.packs_ref, f32[2,8]{1,0:T(2,128)S(1)} %get-tuple-element.11.coeffs_ref), custom_call_target="tpu_custom_call" | custom-call | tf_op jit(solution)/shard_map/finish/pallas_call | solution.py:517
Async XLA Ops:
  20.5 1.5 %collective-permute-start = (f32[16,1,4224]{2,1,0:T(1,128)S(1)}, f32[16,1,4224]{2,1,0:T(1,128)S(1)}, u32[]{:S(2)}, u32[]{:S(2)}) collective-permute-start(f32[16,1,4224]{2,1,0:T(1,128)S(1)} %all_to_all.10), channel_id=1, source_target_pairs={{0,1},{1,0},{2,3},{3,2},{4,5},{5,4},{6,7},{7,6},{8,9},{9,8},{10,11... | collective-permute-start | bytes 811016 | tf_op jit(solution)/shard_map/ppermute | solution.py:487

commit v4 on v3

--- a/solution.py
+++ b/solution.py
@@ -13,8 +13,11 @@
 LANES = 128
 OWNER_TILES = PIX_OWN // LANES
 CHANNELS = 8
-BLOCK = 256
-CHUNK = 32
+COUNT = 3
+BLOCK = 192
+PREPARE = 32
+COLLECT = 32
+PROJECT = 64
 VMEM_BYTES = 32 * 1024 * 1024
 
 SIN_TERMS = (1.0, -1.0 / 6, 1.0 / 120, -1.0 / 5040, 1.0 / 362880, -1.0 / 39916800, 1.0 / 6227020800)
@@ -196,8 +199,12 @@
     rank = rank + jnp.concatenate(before[:-1], axis=0)
     rank = jnp.where(mine, rank, -1.0).astype(jnp.int32)
     number = jnp.sum(ones).astype(jnp.int32)
-    blocks = (number + (BLOCK - 1)) >> log2(BLOCK)
-    chunks = (number + (CHUNK - 1)) >> log2(CHUNK)
+    blocks = sum(
+        jnp.where(number > start, 1, 0) for start in range(0, 2 * slots, BLOCK)
+    )
+
+    def steps(chunk):
+        return (number + (chunk - 1)) >> log2(chunk)
 
     tables = [[], []]
     for half in range(2):
@@ -233,22 +240,24 @@
     listed = jnp.concatenate(listed, axis=0)
     pixel = cell_ref[...]
     cell = (pixel - jnp.floor(pixel * (1.0 / LANES)) * LANES).astype(jnp.bfloat16)
-    source = jnp.concatenate(split3(phase_ref[...]) + split3(listed) + (cell,), axis=1)
+    whole = split3(listed)
+    if max(ranks * nodes * spacing, ranks * OWNER_TILES) <= 65536:
+        whole = whole[:2]
+    source = jnp.concatenate(split3(phase_ref[...]) + (cell,) + whole, axis=1)
 
     def gather_block(block, carry):
-        at = pl.multiple_of(block * BLOCK, BLOCK)
+        at = pl.multiple_of(block * BLOCK, 64)
         down = iota((BLOCK, LANES), 0) + at
         place = jnp.concatenate(
             [(down == rank[k : k + 1, :]).astype(jnp.bfloat16) for k in range(row_count)], axis=1
         )
         taken = dot(place, source)
-        parts = [taken[:, k * LANES : (k + 1) * LANES] for k in range(7)]
+        parts = [taken[:, k * LANES : (k + 1) * LANES] for k in range(4 + len(whole))]
         few_phase[pl.ds(at, BLOCK), :] = (parts[0] + parts[1]) + parts[2]
-        info = (parts[3] + parts[4]) + parts[5]
+        info = sum(parts[5:], parts[4])
         few_info[pl.ds(at, BLOCK), :] = info
-        few_cell[pl.ds(at, BLOCK), :] = parts[6]
-        for k in range(BLOCK // LANES):
-            turned_ref[pl.ds(block * (BLOCK // LANES) + k, 1), :] = info[k * LANES : (k + 1) * LANES, :].T[2:3, :]
+        few_cell[pl.ds(at, BLOCK), :] = parts[3]
+        turned_ref[pl.ds(block, 1), :] = info.T[2:3, :]
         chosen = (info[:, 1:2] == (iota((BLOCK, LANES), 1) + 1).astype(jnp.float32)).astype(jnp.bfloat16)
         for page in range(pages):
             first, second = tables[0][page], tables[1][page]
@@ -263,39 +272,38 @@
 
     lax.fori_loop(0, blocks, gather_block, 0)
 
-    def spline(at):
-        start = jnp.broadcast_to(few_info[pl.ds(at, CHUNK), 0:1], (CHUNK, LANES)).astype(jnp.int32)
-        time = start + iota((CHUNK, LANES), 1)
+    def spline(at, chunk):
+        start = jnp.broadcast_to(few_info[pl.ds(at, chunk), 0:1], (chunk, LANES)).astype(jnp.int32)
+        time = start + iota((chunk, LANES), 1)
         interval = time >> log2(spacing)
         fraction = (time & (spacing - 1)).astype(jnp.float32) * (1.0 / spacing)
         return start >> log2(spacing), interval, spline_weights(fraction)
 
     def prepare(step, carry):
-        at = pl.multiple_of(step * CHUNK, CHUNK)
-        cosine, sine = cos_sin(2.0 * few_phase[pl.ds(at, CHUNK), :])
-        _, interval, weights = spline(at)
-        stream = jnp.zeros((CHUNK, LANES), jnp.float32)
+        at = pl.multiple_of(step * PREPARE, PREPARE)
+        cosine, sine = cos_sin(2.0 * few_phase[pl.ds(at, PREPARE), :])
+        _, interval, weights = spline(at, PREPARE)
+        stream = jnp.zeros((PREPARE, LANES), jnp.float32)
         for term in range(4):
             knot = (interval + (term - 1)) & (knots - 1)
-            value = lane_gather(table_ref[0, pl.ds(at, CHUNK), :], knot & (LANES - 1))
+            value = lane_gather(table_ref[0, pl.ds(at, PREPARE), :], knot & (LANES - 1))
             for page in range(1, pages):
-                more = lane_gather(table_ref[page, pl.ds(at, CHUNK), :], knot & (LANES - 1))
+                more = lane_gather(table_ref[page, pl.ds(at, PREPARE), :], knot & (LANES - 1))
                 value = jnp.where((knot >> log2(LANES)) == page, more, value)
             stream = stream + weights[term] * value
-        cos_ref[pl.ds(at, CHUNK), :] = cosine
-        sin_ref[pl.ds(at, CHUNK), :] = sine
-        stream_ref[pl.ds(at, CHUNK), :] = stream
+        cos_ref[pl.ds(at, PREPARE), :] = cosine
+        sin_ref[pl.ds(at, PREPARE), :] = sine
+        stream_ref[pl.ds(at, PREPARE), :] = stream
         return carry
 
-    lax.fori_loop(0, chunks, prepare, 0)
 
     down = iota((LANES, 2 * LANES), 0).astype(jnp.float32).astype(jnp.bfloat16)
     channel = iota((CHANNELS, LANES), 0)
-    zeros = jnp.zeros((4 * CHANNELS, LANES), jnp.bfloat16)
+    zeros = jnp.zeros((2 * CHANNELS, LANES), jnp.bfloat16)
 
     def collect(step, carry):
-        for k in range(CHUNK // 2):
-            at = step * CHUNK + 2 * k
+        for k in range(COLLECT // 2):
+            at = step * COLLECT + 2 * k
             pieces, cells = [], []
             for slot in (at, at + 1):
                 stream = jnp.broadcast_to(stream_ref[pl.ds(slot, 1), :], (CHANNELS, LANES))
@@ -308,9 +316,7 @@
                 entry = left * right
                 high = entry.astype(jnp.bfloat16).astype(jnp.float32)
                 rest = entry - high
-                middle = rest.astype(jnp.bfloat16).astype(jnp.float32)
-                low = rest - middle
-                stack = jnp.concatenate([high, middle, low, jnp.zeros_like(low)], axis=0)
+                stack = jnp.concatenate([high, rest], axis=0)
                 pieces.append(stack.astype(jnp.bfloat16))
                 cells.append(jnp.broadcast_to(few_cell[pl.ds(slot, 1), :].astype(jnp.bfloat16), (LANES, LANES)))
             entry = jnp.concatenate(
@@ -325,27 +331,28 @@
                 entry, hits, (((1,), (1,)), ((), ())), preferred_element_type=jnp.float32
             )
             for m in range(2):
-                base = 4 * CHANNELS * m
+                base = 2 * CHANNELS * m
                 bin_ref[pl.ds((at + m) * CHANNELS, CHANNELS), :] = (
                     sums[base : base + CHANNELS] + sums[base + CHANNELS : base + 2 * CHANNELS]
-                ) + sums[base + 2 * CHANNELS : base + 3 * CHANNELS]
-        return carry
-
-    lax.fori_loop(0, chunks, collect, 0)
+                )
+        return prepare(step + 1, carry)
+
+    prepare(0, 0)
+    lax.fori_loop(0, steps(COLLECT), collect, 0)
 
     def merge(block, carry):
-        at = pl.multiple_of(block * BLOCK, BLOCK)
+        at = pl.multiple_of(block * BLOCK, 64)
         names = few_info[pl.ds(at, BLOCK), 2:3]
 
         def add(other, carry):
-            there = pl.multiple_of(other * BLOCK, BLOCK)
-            across = [
-                turned_ref[pl.ds(other * (BLOCK // LANES) + k, 1), :] for k in range(BLOCK // LANES)
-            ]
-            same = (names == jnp.concatenate(across, axis=1)).astype(jnp.bfloat16)
+            there = pl.multiple_of(other * BLOCK, 64)
+            same = (names == turned_ref[pl.ds(other, 1), :]).astype(jnp.bfloat16)
             for c in range(CHANNELS):
                 binned = bin_ref[pl.ds(there * CHANNELS + c, BLOCK, stride=CHANNELS), :]
-                share = exact_dot(same, binned)
+                high = binned.astype(jnp.bfloat16)
+                share = dot(same, high)
+                if c != COUNT:
+                    share = share + dot(same, (binned - high.astype(jnp.float32)).astype(jnp.bfloat16))
                 before = total_ref[c, pl.ds(at, BLOCK), :]
                 total_ref[c, pl.ds(at, BLOCK), :] = jnp.where(other == 0, share, before + share)
             return carry
@@ -356,8 +363,8 @@
     lax.fori_loop(0, blocks, merge, 0)
 
     def project(step, lines):
-        at = pl.multiple_of(step * CHUNK, CHUNK)
-        here = pl.ds(at, CHUNK)
+        at = pl.multiple_of(step * PROJECT, PROJECT)
+        here = pl.ds(at, PROJECT)
         signal, signal_cos, signal_sin, count, cos_sum, sin_sum, cos_cos, cos_sin_sum = (
             total_ref[c, here, :] for c in range(CHANNELS)
         )
@@ -382,9 +389,9 @@
         ) + sin_ref[here, :] * lane_gather(map_u, cell)
         which = few_info[here, 1:2].astype(jnp.int32) - 1
         cleaned = jnp.where(which >= 0, stream_ref[here, :] - projected, 0.0)
-        base, interval, weights = spline(at)
+        base, interval, weights = spline(at, PROJECT)
         early = interval == base
-        lane = iota((CHUNK, LANES), 1)
+        lane = iota((PROJECT, LANES), 1)
         side = which >> log2(dets)
         det = which & (dets - 1)
         lines = list(lines)
@@ -397,12 +404,12 @@
             spot = spot + (knot & (nodes - 1))
             for p in range(2 * packed):
                 part = jnp.where(lane + p * LANES == spot, value, 0.0)
-                for q in range(CHUNK // 8):
+                for q in range(PROJECT // 8):
                     lines[p] = lines[p] + part[q * 8 : (q + 1) * 8, :]
         return tuple(lines)
 
     lines = tuple(jnp.zeros((8, LANES), jnp.float32) for _ in range(2 * packed))
-    lines = lax.fori_loop(0, chunks, project, lines)
+    lines = lax.fori_loop(0, steps(PROJECT), project, lines)
     partial = jnp.concatenate([jnp.sum(line, axis=0, keepdims=True) for line in lines], axis=0)
     for target in range(out_ref.shape[0] // (2 * packed)):
         out_ref[target * 2 * packed : (target + 1) * 2 * packed, :] = partial
@@ -487,6 +494,8 @@
     other = lax.ppermute(arrived, "det", swap)
     pages = max(1, ranks * nodes // LANES)
     big = pltpu.VMEM((2 * slots, LANES), jnp.float32)
+    room = pl.cdiv(2 * slots, BLOCK) * BLOCK + max(PREPARE, COLLECT, PROJECT)
+    few = pltpu.VMEM((room, LANES), jnp.float32)
     partials, packs, coeffs = pl.pallas_call(
         functools.partial(main_kernel, ranks, cap, dets, nodes, spacing),
         out_shape=(
@@ -499,12 +508,12 @@
         scratch_shapes=[
             big, big, big,
             pltpu.VMEM((2, ranks, LANES), jnp.float32),
-            big, big, big,
-            pltpu.VMEM((pages, 2 * slots, LANES), jnp.float32),
-            big, big, big,
-            pltpu.VMEM((2 * slots * CHANNELS, LANES), jnp.float32),
-            pltpu.VMEM((CHANNELS, 2 * slots, LANES), jnp.float32),
-            pltpu.VMEM((max(8, 2 * slots // LANES), LANES), jnp.float32),
+            few, few, few,
+            pltpu.VMEM((pages, room, LANES), jnp.float32),
+            few, few, few,
+            pltpu.VMEM((room * CHANNELS, LANES), jnp.float32),
+            pltpu.VMEM((CHANNELS, room, LANES), jnp.float32),
+            pltpu.VMEM((8, BLOCK), jnp.float32),
             pltpu.SemaphoreType.DMA((1,)),
         ],
         compiler_params=params,

time: 39.4 us -> 38.1 us (0.967)
  Pallas kernels: 9.27 us -> 7.1 us
  blocking collectives: 27.6 us -> 28.7 us
    pallas_call x1, Pallas kernels: 6.69 us -> 4.53 us  [body(): pl.pallas_call(functools.partial(main_kernel, ranks, cap, dets, nodes, sp...]
    all_to_all x1, blocking collectives: 9.5 us -> 10.6 us  [body(): lax.all_to_all(partials.reshape(ranks * groups, 1, height * LANES), ('tm'...]
where the time goes in v4:
time: 38.1 us; the launch traced here: 38 us
  blocking collectives  28.7 us (75%)
  Pallas kernels  7.1 us (19%)
  waiting for transfers between devices  1.54 us (4%)
  between operations  0.65 us (2%)
    all_to_all x1, blocking collectives, body(): lax.all_to_all(outgoing.reshape(ranks, 1, rows * LANES), 'tm', split_axis...  18.1 us
    all_to_all x1, blocking collectives, body(): lax.all_to_all(partials.reshape(ranks * groups, 1, height * LANES), ('tm'...  10.6 us
    pallas_call x1, Pallas kernels, body(): pl.pallas_call(functools.partial(main_kernel, ranks, cap, dets, nodes, sp...  4.53 us
    pallas_call x1, Pallas kernels, body(): pl.pallas_call(functools.partial(send_kernel, ranks, cap), out_shape=jax....  1.72 us
    ppermute x1, waiting for transfers between devices, body(): other = lax.ppermute(arrived, 'det', swap)  1.54 us
    pallas_call x1, Pallas kernels, body(): pl.pallas_call(functools.partial(finish_kernel, ranks, spacing), out_shap...  0.85 us
  transfers between devices with their start and end apart: 1, of which 1 were waited for; matrix products, arithmetic and copies ran while one was open for 0% of the time, Pallas kernels for 0%

profile of v4, /device:TPU:0, one launch (start us, length us, event | category | flops | bytes accessed | tf_op | source)
XLA Modules:
  0.0 38.0 jit_solution(2937225156125759594)
XLA Ops:
  0.6 1.7 %send.1 = f32[528,128]{1,0:T(8,128)S(1)} custom-call(s32[8,16]{1,0:T(8,128)} %patch_hbm.1, s32[1,8]{1,0:T(1,128)} %bitcast.20, f32[2,8]{1,0:T(2,128)} %bitcast.17, f32[2,8]{1,0:T(2,128)} %bitcast.18, s32[8,2048]{1,0:T(8,128)} %cell_hbm.1, f32[8,2048]{1,0:T(8,128)} %phase_hbm.1), custom_call_target="tpu_custom_call" | custom-call | tf_op jit(solution)/shard_map/send/pallas_call | solution.py:480
  2.4 18.1 %all_to_all.10 = f32[16,1,4224]{2,1,0:T(1,128)S(1)} all-to-all(f32[16,1,4224]{2,1,0:T(1,128)S(1)} %bitcast.13), channel_id=1, replica_groups=mesh['tm'=16,'det'=2] {'tm'}, dimensions={0} | all-to-all | bytes 540672 | tf_op jit(solution)/shard_map/all_to_all | solution.py:490
  20.5 0.0 collective-permute-start
  20.5 1.5 %collective-permute-done = f32[16,1,4224]{2,1,0:T(1,128)S(1)} collective-permute-done((f32[16,1,4224]{2,1,0:T(1,128)S(1)}, f32[16,1,4224]{2,1,0:T(1,128)S(1)}, u32[]{:S(2)}, u32[]{:S(2)}) %collective-permute-start) | collective-permute-done | bytes 270368 | tf_op jit(solution)/shard_map/ppermute | solution.py:494
  22.0 4.5 %main.1 = (f32[128,128]{1,0:T(8,128)S(1)}, f32[2,4,128]{2,1,0:T(4,128)S(1)}, f32[2,8]{1,0:T(2,128)S(1)}) custom-call(f32[528,128]{1,0:T(8,128)S(1)} %bitcast.12, f32[528,128]{1,0:T(8,128)S(1)} %bitcast.14, f32[2,8]{1,0:T(2,128)} %bitcast.19), custom_call_target="tpu_custom_call" | custom-call | tf_op jit(solution)/shard_map/main/pallas_call | solution.py:499
  26.6 10.6 %all_to_all.11 = f32[32,1,512]{2,1,0:T(1,128)S(1)} all-to-all(f32[32,1,512]{2,1,0:T(1,128)S(1)} %bitcast.16), channel_id=1, replica_groups=mesh['tm'=16,'det'=2] {'tm','det'}, dimensions={0} | all-to-all | bytes 131072 | tf_op jit(solution)/shard_map/all_to_all | solution.py:522
  37.2 0.8 %finish.1 = (f32[2,8]{1,0:T(2,128)}, f32[2,8]{1,0:T(2,128)}, f32[2,8]{1,0:T(2,128)}) custom-call(f32[128,128]{1,0:T(8,128)S(1)} %bitcast.15, f32[2,4,128]{2,1,0:T(4,128)S(1)} %get-tuple-element.10.packs_ref, f32[2,8]{1,0:T(2,128)S(1)} %get-tuple-element.11.coeffs_ref), custom_call_target="tpu_custom_call" | custom-call | tf_op jit(solution)/shard_map/finish/pallas_call | solution.py:526
Async XLA Ops:
  20.5 1.5 %collective-permute-start = (f32[16,1,4224]{2,1,0:T(1,128)S(1)}, f32[16,1,4224]{2,1,0:T(1,128)S(1)}, u32[]{:S(2)}, u32[]{:S(2)}) collective-permute-start(f32[16,1,4224]{2,1,0:T(1,128)S(1)} %all_to_all.10), channel_id=1, source_target_pairs={{0,1},{1,0},{2,3},{3,2},{4,5},{5,4},{6,7},{7,6},{8,9},{9,8},{10,11... | collective-permute-start | bytes 811016 | tf_op jit(solution)/shard_map/ppermute | solution.py:494

commit v5 on v4

--- a/solution.py
+++ b/solution.py
@@ -14,10 +14,9 @@
 OWNER_TILES = PIX_OWN // LANES
 CHANNELS = 8
 COUNT = 3
-BLOCK = 192
-PREPARE = 32
+BLOCK = 160
 COLLECT = 32
-PROJECT = 64
+PROJECT = 80
 VMEM_BYTES = 32 * 1024 * 1024
 
 SIN_TERMS = (1.0, -1.0 / 6, 1.0 / 120, -1.0 / 5040, 1.0 / 362880, -1.0 / 39916800, 1.0 / 6227020800)
@@ -142,160 +141,156 @@
     info = info + knots
     copies[4].wait()
     cells = jnp.concatenate([cell_ref[:, c * LANES : (c + 1) * LANES] for c in range(columns)], axis=0)
-    slot_pixel = exact_dot(place, (tiles * LANES + cells).astype(jnp.float32))
+    pixels = (tiles * LANES + cells).astype(jnp.float32)
     copies[5].wait()
     phases = jnp.concatenate([phase_ref[:, c * LANES : (c + 1) * LANES] for c in range(columns)], axis=0)
-    slot_phase = exact_dot(place, phases)
+    moved = exact_dot(place, jnp.concatenate([phases, pixels], axis=1))
+    slot_phase, slot_pixel = moved[:, :LANES], moved[:, LANES:]
     for o in range(ranks):
         out_ref[o * rows : o * rows + cap, :] = slot_phase[o * cap : (o + 1) * cap, :]
         out_ref[o * rows + cap : o * rows + 2 * cap, :] = slot_pixel[o * cap : (o + 1) * cap, :]
         out_ref[o * rows + 2 * cap : (o + 1) * rows, :] = info[o : o + 1, :]
 
 
-def main_kernel(
-    ranks, cap, dets, nodes, spacing, own_ref, other_ref, coeffs_hbm, out_ref, packs_ref, coeffs_ref,
-    phase_ref, cell_ref, info_ref, meta_ref, few_phase, few_cell, few_info, table_ref,
-    cos_ref, sin_ref, stream_ref, bin_ref, total_ref, turned_ref, sems,
-):
-    coeffs_copy = pltpu.make_async_copy(coeffs_hbm, coeffs_ref, sems.at[0])
-    coeffs_copy.start()
-    slots = ranks * cap
+def unpack(ranks, cap, ref, phase_ref, cell_ref, info_ref, meta_ref):
     rows = 2 * cap + 1
-    knots = ranks * nodes
-    width = dets * nodes
-    pages = max(1, knots // LANES)
-    group = lax.axis_index("det")
-    packed = knots * dets // LANES
-    per_row = LANES // width
-    row_count = 2 * slots // LANES
-
-    for half, ref in enumerate((own_ref, other_ref)):
-        for o in range(ranks):
-            here = half * slots + o * cap
-            phase_ref[here : here + cap, :] = ref[o * rows : o * rows + cap, :]
-            cell_ref[here : here + cap, :] = ref[o * rows + cap : o * rows + 2 * cap, :]
-            info = ref[o * rows + 2 * cap : (o + 1) * rows, :]
-            info_ref[here : here + cap, :] = jnp.broadcast_to(info, (cap, LANES))
-            meta_ref[half, o : o + 1, :] = info
-
+    for o in range(ranks):
+        here = o * cap
+        phase_ref[here : here + cap, :] = ref[o * rows : o * rows + cap, :]
+        cell_ref[here : here + cap, :] = ref[o * rows + cap : o * rows + 2 * cap, :]
+        info = ref[o * rows + 2 * cap : (o + 1) * rows, :]
+        info_ref[here : here + cap, :] = jnp.broadcast_to(info, (cap, LANES))
+        meta_ref[o : o + 1, :] = info
+
+
+def rank_slots(ranks, cap, meta_ref):
     lists = []
     spans = LANES // cap
-    for half in range(2):
-        for k in range(slots // LANES):
-            names = meta_ref[half, k * spans : (k + 1) * spans, :]
-            lane = iota((spans, LANES), 1)
-            spread = lane_gather(names, 2 * cap + (lane & (cap - 1)))
-            mine = (lane >> log2(cap)) == iota((spans, LANES), 0)
-            lists.append(jnp.sum(jnp.where(mine, spread, 0.0), axis=0, keepdims=True))
+    for k in range(ranks * cap // LANES):
+        names = meta_ref[k * spans : (k + 1) * spans, :]
+        lane = iota((spans, LANES), 1)
+        spread = lane_gather(names, 2 * cap + (lane & (cap - 1)))
+        mine = (lane >> log2(cap)) == iota((spans, LANES), 0)
+        lists.append(jnp.sum(jnp.where(mine, spread, 0.0), axis=0, keepdims=True))
     names = jnp.concatenate(lists, axis=0).astype(jnp.int32)
-    mine = (names > 0) & (((names - 1) & 1) == group)
+    mine = (names > 0) & (((names - 1) & 1) == lax.axis_index("det"))
     ones = jnp.where(mine, 1.0, 0.0)
     earlier = (iota((LANES, LANES), 0) < iota((LANES, LANES), 1)).astype(jnp.bfloat16)
     rank = dot(ones.astype(jnp.bfloat16), earlier)
     sums = jnp.sum(ones, axis=1, keepdims=True)
     before = [jnp.zeros((1, 1), jnp.float32)]
-    for k in range(row_count):
+    for k in range(len(lists)):
         before.append(before[-1] + sums[k : k + 1, :])
     rank = rank + jnp.concatenate(before[:-1], axis=0)
-    rank = jnp.where(mine, rank, -1.0).astype(jnp.int32)
-    number = jnp.sum(ones).astype(jnp.int32)
-    blocks = sum(
-        jnp.where(number > start, 1, 0) for start in range(0, 2 * slots, BLOCK)
-    )
-
-    def steps(chunk):
-        return (number + (chunk - 1)) >> log2(chunk)
-
-    tables = [[], []]
-    for half in range(2):
-        side = group if half == 0 else 1 - group
-        packs = []
-        for kind in range(2):
-            for p in range(packed):
-                names = meta_ref[half, p * per_row : (p + 1) * per_row, :]
-                lane = iota((per_row, LANES), 1)
-                spread = lane_gather(names, (3 * cap + kind * width) + (lane & (width - 1)))
-                here = (lane >> log2(width)) == iota((per_row, LANES), 0)
-                line = jnp.sum(jnp.where(here, spread, 0.0), axis=0, keepdims=True)
-                packs_ref[kind, pl.ds(side * packed + p, 1), :] = line
-                packs.append(line)
+    return jnp.where(mine, rank, -1.0).astype(jnp.int32), jnp.sum(ones).astype(jnp.int32)
+
+
+def flatten(pages, knots):
+    dets = pages[0].shape[0]
+    if knots >= LANES:
+        return [page[d : d + 1, :] for d in range(dets) for page in pages]
+    lane, det = iota((dets, LANES), 1), iota((dets, LANES), 0)
+    spread = lane_gather(pages[0], lane & (knots - 1))
+    per_row = LANES // knots
+    mine = (det & (per_row - 1)) == (lane >> log2(knots))
+    spread = jnp.where(mine, spread, 0.0)
+    rows = []
+    for first in range(0, dets, per_row):
+        rows.append(jnp.sum(spread[first : first + per_row, :], axis=0, keepdims=True))
+    return rows
+
+
+def read_knots(ranks, cap, dets, nodes, meta_ref):
+    width = dets * nodes
+    knots = ranks * nodes
+    per_row = LANES // width
+    kinds = []
+    for kind in range(2):
+        lines = []
+        for p in range(ranks // per_row):
+            names = meta_ref[p * per_row : (p + 1) * per_row, :]
+            lane = iota((per_row, LANES), 1)
+            spread = lane_gather(names, (3 * cap + kind * width) + (lane & (width - 1)))
+            here = (lane >> log2(width)) == iota((per_row, LANES), 0)
+            lines.append(jnp.sum(jnp.where(here, spread, 0.0), axis=0, keepdims=True))
         lane = iota((dets, LANES), 1)
-        for page in range(pages):
+        tables = []
+        for page in range(max(1, knots // LANES)):
             knot = lane + page * LANES
             index = ((knot >> log2(nodes)) & (per_row - 1)) * width
             index = index + iota((dets, LANES), 0) * nodes + (knot & (nodes - 1))
             table = jnp.zeros((dets, LANES), jnp.float32)
-            for p in range(packed):
-                values = lane_gather(jnp.broadcast_to(packs[p], (dets, LANES)), index)
+            for p, line in enumerate(lines):
+                values = lane_gather(jnp.broadcast_to(line, (dets, LANES)), index)
                 table = jnp.where((knot >> log2(per_row * nodes)) == p, values, table)
-            tables[half].append(table)
-
+            tables.append(table)
+        kinds.append(tables)
+    return kinds
+
+
+def source_of(ranks, cap, dets, total, side, phase_ref, cell_ref, info_ref):
+    slots = ranks * cap
     slot = iota((slots, LANES), 0) & (cap - 1)
     lane = iota((slots, LANES), 1)
-    listed = []
-    for half in range(2):
-        side = group if half == 0 else 1 - group
-        found = lane_gather(info_ref[half * slots : (half + 1) * slots, :], jnp.minimum(lane, 2) * cap + slot)
-        listed.append(found + jnp.where(lane == 1, (side * dets).astype(jnp.float32), 0.0))
-    listed = jnp.concatenate(listed, axis=0)
+    listed = lane_gather(info_ref[...], jnp.minimum(lane, 2) * cap + slot)
+    listed = listed + jnp.where(lane == 1, (side * dets).astype(jnp.float32), 0.0)
     pixel = cell_ref[...]
     cell = (pixel - jnp.floor(pixel * (1.0 / LANES)) * LANES).astype(jnp.bfloat16)
     whole = split3(listed)
-    if max(ranks * nodes * spacing, ranks * OWNER_TILES) <= 65536:
+    if max(total, ranks * OWNER_TILES) <= 65536:
         whole = whole[:2]
-    source = jnp.concatenate(split3(phase_ref[...]) + (cell,) + whole, axis=1)
-
-    def gather_block(block, carry):
-        at = pl.multiple_of(block * BLOCK, 64)
-        down = iota((BLOCK, LANES), 0) + at
-        place = jnp.concatenate(
-            [(down == rank[k : k + 1, :]).astype(jnp.bfloat16) for k in range(row_count)], axis=1
-        )
-        taken = dot(place, source)
-        parts = [taken[:, k * LANES : (k + 1) * LANES] for k in range(4 + len(whole))]
-        few_phase[pl.ds(at, BLOCK), :] = (parts[0] + parts[1]) + parts[2]
-        info = sum(parts[5:], parts[4])
-        few_info[pl.ds(at, BLOCK), :] = info
-        few_cell[pl.ds(at, BLOCK), :] = parts[3]
-        turned_ref[pl.ds(block, 1), :] = info.T[2:3, :]
-        chosen = (info[:, 1:2] == (iota((BLOCK, LANES), 1) + 1).astype(jnp.float32)).astype(jnp.bfloat16)
-        for page in range(pages):
-            first, second = tables[0][page], tables[1][page]
-            low = jnp.where(group == 0, first, second)
-            high = jnp.where(group == 0, second, first)
-            table = jnp.concatenate(
-                [low, high, jnp.zeros((LANES - 2 * dets, LANES), jnp.float32)], axis=0
-            )
-            table_ref[page, pl.ds(at, BLOCK), :] = exact_dot(chosen, table)
-        bin_ref[pl.ds(at * CHANNELS, BLOCK * CHANNELS), :] = jnp.zeros((BLOCK * CHANNELS, LANES), jnp.float32)
-        return carry
-
-    lax.fori_loop(0, blocks, gather_block, 0)
-
-    def spline(at, chunk):
-        start = jnp.broadcast_to(few_info[pl.ds(at, chunk), 0:1], (chunk, LANES)).astype(jnp.int32)
-        time = start + iota((chunk, LANES), 1)
-        interval = time >> log2(spacing)
-        fraction = (time & (spacing - 1)).astype(jnp.float32) * (1.0 / spacing)
-        return start >> log2(spacing), interval, spline_weights(fraction)
-
-    def prepare(step, carry):
-        at = pl.multiple_of(step * PREPARE, PREPARE)
-        cosine, sine = cos_sin(2.0 * few_phase[pl.ds(at, PREPARE), :])
-        _, interval, weights = spline(at, PREPARE)
-        stream = jnp.zeros((PREPARE, LANES), jnp.float32)
+    return jnp.concatenate(split3(phase_ref[...]) + (cell,) + whole, axis=1)
+
+
+def take_slots(at, rank, source, dets, side, tables):
+    down = iota((BLOCK, LANES), 0) + at
+    place = jnp.concatenate(
+        [(down == rank[k : k + 1, :]).astype(jnp.bfloat16) for k in range(rank.shape[0])], axis=1
+    )
+    taken = dot(place, source)
+    parts = [taken[:, k * LANES : (k + 1) * LANES] for k in range(taken.shape[1] // LANES)]
+    phase = (parts[0] + parts[1]) + parts[2]
+    info = sum(parts[5:], parts[4])
+    lane = iota((BLOCK, LANES), 1) + (1 + side * dets)
+    chosen = ((info[:, 1:2] == lane.astype(jnp.float32)) & (iota((BLOCK, LANES), 1) < dets)).astype(jnp.bfloat16)
+    empty = jnp.zeros((LANES - dets, LANES), jnp.float32)
+    knots = [exact_dot(chosen, jnp.concatenate([table, empty], axis=0)) for table in tables]
+    return phase, parts[3], info, knots
+
+
+def spline(info_ref, spacing, at, chunk):
+    start = jnp.broadcast_to(info_ref[pl.ds(at, chunk), 0:1], (chunk, LANES)).astype(jnp.int32)
+    time = start + iota((chunk, LANES), 1)
+    interval = time >> log2(spacing)
+    fraction = (time & (spacing - 1)).astype(jnp.float32) * (1.0 / spacing)
+    return start >> log2(spacing), interval, spline_weights(fraction)
+
+
+def five_weights(early, weights):
+    padded = (0.0,) + weights + (0.0,)
+    return [jnp.where(early, padded[term + 1], padded[term]) for term in range(5)]
+
+
+def bin_chunks(first, last, knots, spacing, few_phase, few_cell, few_info, table_ref, cos_ref, sin_ref, stream_ref, basis_ref, bin_ref):
+    pages = table_ref.shape[0]
+
+    def prepare(step):
+        at = pl.multiple_of(step * COLLECT, COLLECT)
+        cosine, sine = cos_sin(2.0 * few_phase[pl.ds(at, COLLECT), :])
+        base, interval, weights = spline(few_info, spacing, at, COLLECT)
+        for term, weight in enumerate(five_weights(interval == base, weights)):
+            basis_ref[term, pl.ds(at, COLLECT), :] = weight
+        stream = jnp.zeros((COLLECT, LANES), jnp.float32)
         for term in range(4):
             knot = (interval + (term - 1)) & (knots - 1)
-            value = lane_gather(table_ref[0, pl.ds(at, PREPARE), :], knot & (LANES - 1))
+            value = lane_gather(table_ref[0, pl.ds(at, COLLECT), :], knot & (LANES - 1))
             for page in range(1, pages):
-                more = lane_gather(table_ref[page, pl.ds(at, PREPARE), :], knot & (LANES - 1))
+                more = lane_gather(table_ref[page, pl.ds(at, COLLECT), :], knot & (LANES - 1))
                 value = jnp.where((knot >> log2(LANES)) == page, more, value)
             stream = stream + weights[term] * value
-        cos_ref[pl.ds(at, PREPARE), :] = cosine
-        sin_ref[pl.ds(at, PREPARE), :] = sine
-        stream_ref[pl.ds(at, PREPARE), :] = stream
-        return carry
-
+        cos_ref[pl.ds(at, COLLECT), :] = cosine
+        sin_ref[pl.ds(at, COLLECT), :] = sine
+        stream_ref[pl.ds(at, COLLECT), :] = stream
 
     down = iota((LANES, 2 * LANES), 0).astype(jnp.float32).astype(jnp.bfloat16)
     channel = iota((CHANNELS, LANES), 0)
@@ -335,18 +330,114 @@
                 bin_ref[pl.ds((at + m) * CHANNELS, CHANNELS), :] = (
                     sums[base : base + CHANNELS] + sums[base + CHANNELS : base + 2 * CHANNELS]
                 )
-        return prepare(step + 1, carry)
-
-    prepare(0, 0)
-    lax.fori_loop(0, steps(COLLECT), collect, 0)
+        prepare(step + 1)
+        return carry
+
+    prepare(first)
+    lax.fori_loop(first, last, collect, 0)
+
+
+def own_kernel(
+    ranks, cap, dets, nodes, spacing, own_ref,
+    few_phase, few_cell, few_info, table_ref, cos_ref, sin_ref, stream_ref, basis_ref, bin_ref, packs_ref, count_ref,
+    phase_ref, cell_ref, info_ref, meta_ref,
+):
+    knots = ranks * nodes
+    side = lax.axis_index("det")
+    unpack(ranks, cap, own_ref, phase_ref, cell_ref, info_ref, meta_ref)
+    rank, number = rank_slots(ranks, cap, meta_ref)
+    count_ref[...] = jnp.full((8, LANES), number, jnp.int32)
+    tables, left = read_knots(ranks, cap, dets, nodes, meta_ref)
+    packs_ref[...] = jnp.concatenate(flatten(tables, knots) + flatten(left, knots), axis=0)
+    source = source_of(ranks, cap, dets, knots * spacing, side, phase_ref, cell_ref, info_ref)
+
+    def gather_block(block, carry):
+        here = pl.ds(pl.multiple_of(block * BLOCK, 32), BLOCK)
+        few_phase[here, :], few_cell[here, :], few_info[here, :], found = take_slots(
+            block * BLOCK, rank, source, dets, side, tables
+        )
+        for page, rows in enumerate(found):
+            table_ref[page, here, :] = rows
+        return carry
+
+    lax.fori_loop(0, block_count(number, ranks * cap), gather_block, 0)
+    bin_chunks(
+        0, number >> log2(COLLECT), knots, spacing, few_phase, few_cell, few_info, table_ref,
+        cos_ref, sin_ref, stream_ref, basis_ref, bin_ref,
+    )
+
+
+def block_count(number, most):
+    return sum(jnp.where(number > start, 1, 0) for start in range(0, most, BLOCK))
+
+
+def main_kernel(
+    ranks, cap, dets, nodes, spacing, other_ref, coeffs_hbm, packs_own, count_ref, *refs,
+):
+    few_phase, few_cell, few_info, table_ref, cos_ref, sin_ref, stream_ref, basis_ref, bin_ref = refs[9:18]
+    out_ref, packs_ref, coeffs_ref = refs[18:21]
+    phase_ref, cell_ref, info_ref, meta_ref, total_ref, turned_ref, knots_ref, sems = refs[21:]
+    coeffs_copy = pltpu.make_async_copy(coeffs_hbm, coeffs_ref, sems.at[0])
+    coeffs_copy.start()
+    slots = ranks * cap
+    knots = ranks * nodes
+    packed = knots * dets // LANES
+    group = lax.axis_index("det")
+    side = 1 - group
+
+    unpack(ranks, cap, other_ref, phase_ref, cell_ref, info_ref, meta_ref)
+    rank, more = rank_slots(ranks, cap, meta_ref)
+    ready = jnp.max(count_ref[...])
+    rank = jnp.where(rank >= 0, rank + ready, -1)
+    number = ready + more
+    tables, left = read_knots(ranks, cap, dets, nodes, meta_ref)
+    for kind, pages in enumerate((tables, left)):
+        here = slice(kind * packed, (kind + 1) * packed)
+        packs_ref[kind, pl.ds(group * packed, packed), :] = packs_own[here, :]
+        packs_ref[kind, pl.ds(side * packed, packed), :] = jnp.concatenate(flatten(pages, knots), axis=0)
+    source = source_of(ranks, cap, dets, knots * spacing, side, phase_ref, cell_ref, info_ref)
+    blocks = block_count(number, 2 * slots)
+    ready_blocks = block_count(ready, slots)
+
+    def gather_block(block, carry):
+        here = pl.ds(pl.multiple_of(block * BLOCK, 32), BLOCK)
+        started = block < ready_blocks
+        phase, cell, info, found = take_slots(block * BLOCK, rank, source, dets, side, tables)
+        few_phase[here, :] = jnp.where(started, few_phase[here, :], 0.0) + phase
+        few_cell[here, :] = jnp.where(started, few_cell[here, :], 0.0) + cell
+        info = jnp.where(started, few_info[here, :], 0.0) + info
+        few_info[here, :] = info
+        turned = info.T
+        turned_ref[0, pl.ds(block, 1), :] = turned[1:2, :]
+        turned_ref[1, pl.ds(block, 1), :] = turned[2:3, :]
+        for page, rows in enumerate(found):
+            table_ref[page, here, :] = jnp.where(started, table_ref[page, here, :], 0.0) + rows
+        return carry
+
+    lax.fori_loop(0, blocks, gather_block, 0)
+
+    def steps(chunk):
+        return (number + (chunk - 1)) >> log2(chunk)
+
+    bin_chunks(
+        ready >> log2(COLLECT), steps(COLLECT), knots, spacing, few_phase, few_cell, few_info, table_ref,
+        cos_ref, sin_ref, stream_ref, basis_ref, bin_ref,
+    )
+
+    def clear(step, carry):
+        at = pl.multiple_of(step * COLLECT * CHANNELS, COLLECT * CHANNELS)
+        bin_ref[pl.ds(at, COLLECT * CHANNELS), :] = jnp.zeros((COLLECT * CHANNELS, LANES), jnp.float32)
+        return carry
+
+    lax.fori_loop(steps(COLLECT), blocks * (BLOCK // COLLECT), clear, 0)
 
     def merge(block, carry):
-        at = pl.multiple_of(block * BLOCK, 64)
+        at = pl.multiple_of(block * BLOCK, 32)
         names = few_info[pl.ds(at, BLOCK), 2:3]
 
         def add(other, carry):
-            there = pl.multiple_of(other * BLOCK, 64)
-            same = (names == turned_ref[pl.ds(other, 1), :]).astype(jnp.bfloat16)
+            there = pl.multiple_of(other * BLOCK, 32)
+            same = (names == turned_ref[1, pl.ds(other, 1), :]).astype(jnp.bfloat16)
             for c in range(CHANNELS):
                 binned = bin_ref[pl.ds(there * CHANNELS + c, BLOCK, stride=CHANNELS), :]
                 high = binned.astype(jnp.bfloat16)
@@ -362,9 +453,8 @@
 
     lax.fori_loop(0, blocks, merge, 0)
 
-    def project(step, lines):
-        at = pl.multiple_of(step * PROJECT, PROJECT)
-        here = pl.ds(at, PROJECT)
+    def project(at):
+        here = pl.ds(pl.multiple_of(at, 16), PROJECT)
         signal, signal_cos, signal_sin, count, cos_sum, sin_sum, cos_cos, cos_sin_sum = (
             total_ref[c, here, :] for c in range(CHANNELS)
         )
@@ -387,30 +477,32 @@
         projected = (
             lane_gather(map_i, cell) + cos_ref[here, :] * lane_gather(map_q, cell)
         ) + sin_ref[here, :] * lane_gather(map_u, cell)
-        which = few_info[here, 1:2].astype(jnp.int32) - 1
-        cleaned = jnp.where(which >= 0, stream_ref[here, :] - projected, 0.0)
-        base, interval, weights = spline(at, PROJECT)
-        early = interval == base
+        cleaned = stream_ref[here, :] - projected
+        valid = few_info[here, 1:2] > 0.5
+        base = few_info[here, 0:1].astype(jnp.int32) >> log2(spacing)
         lane = iota((PROJECT, LANES), 1)
-        side = which >> log2(dets)
-        det = which & (dets - 1)
-        lines = list(lines)
+        pages = [jnp.zeros((PROJECT, LANES), jnp.float32) for _ in range(knots_ref.shape[0])]
         for term in range(5):
-            low = weights[term] if term < 4 else 0.0
-            high = weights[term - 1] if term > 0 else 0.0
-            value = jnp.sum(jnp.where(early, low, high) * cleaned, axis=1, keepdims=True)
+            value = jnp.sum(basis_ref[term, here, :] * cleaned, axis=1, keepdims=True)
             knot = (base + (term - 1)) & (knots - 1)
-            spot = side * (knots * dets) + (knot >> log2(nodes)) * width + det * nodes
-            spot = spot + (knot & (nodes - 1))
-            for p in range(2 * packed):
-                part = jnp.where(lane + p * LANES == spot, value, 0.0)
-                for q in range(PROJECT // 8):
-                    lines[p] = lines[p] + part[q * 8 : (q + 1) * 8, :]
-        return tuple(lines)
-
-    lines = tuple(jnp.zeros((8, LANES), jnp.float32) for _ in range(2 * packed))
-    lines = lax.fori_loop(0, steps(PROJECT), project, lines)
-    partial = jnp.concatenate([jnp.sum(line, axis=0, keepdims=True) for line in lines], axis=0)
+            for page in range(len(pages)):
+                pages[page] = pages[page] + jnp.where(lane + page * LANES == knot, value, 0.0)
+        for page, sums in enumerate(pages):
+            knots_ref[page, here, :] = jnp.where(valid, sums, 0.0)
+
+    def image_of(block, sums):
+        at = pl.multiple_of(block * BLOCK, 32)
+        for first in range(0, BLOCK, PROJECT):
+            project(at + first)
+        det = (iota((2 * dets, BLOCK), 0) + 1).astype(jnp.float32)
+        chosen = (turned_ref[0, pl.ds(block, 1), :] == det).astype(jnp.bfloat16)
+        return tuple(
+            total + exact_dot(chosen, knots_ref[page, pl.ds(at, BLOCK), :]) for page, total in enumerate(sums)
+        )
+
+    image = tuple(jnp.zeros((2 * dets, LANES), jnp.float32) for _ in range(knots_ref.shape[0]))
+    image = lax.fori_loop(0, blocks, image_of, image)
+    partial = jnp.concatenate(flatten(image, knots), axis=0)
     for target in range(out_ref.shape[0] // (2 * packed)):
         out_ref[target * 2 * packed : (target + 1) * 2 * packed, :] = partial
     coeffs_copy.wait()
@@ -431,16 +523,17 @@
     fresh = left - stride_factor * image
     beta = jnp.sum(fresh * fresh, keepdims=True) / norm_old
     span, group = lax.axis_index("tm"), lax.axis_index("det")
-    per_row = LANES // (dets * nodes)
-    row = group * (height // 2) + (span >> log2(per_row))
-    lane = iota((8, LANES), 1)
-    first = (span & (per_row - 1)) * (dets * nodes)
-    index = first + (lane & (dets - 1)) * nodes + (iota((8, LANES), 0) & (nodes - 1))
-    here = iota((height, LANES), 0) == row
+    lines = height // 2
+    knots = lines * LANES // dets
+    place = (iota((8, LANES), 1) & (dets - 1)) * knots + span * nodes + (iota((8, LANES), 0) & (nodes - 1))
 
     def own(x):
-        line = jnp.sum(jnp.where(here, x, 0.0), axis=0, keepdims=True)
-        return lane_gather(jnp.broadcast_to(line, (8, LANES)), index)[:nodes, :dets]
+        x = jnp.where(group == 0, x[:lines, :], x[lines:, :])
+        found = jnp.zeros((8, LANES), jnp.float32)
+        for p in range(lines):
+            values = lane_gather(jnp.broadcast_to(x[p : p + 1, :], (8, LANES)), place & (LANES - 1))
+            found = jnp.where((place >> log2(LANES)) == p, values, found)
+        return found[:nodes, :dets]
 
     my_search = own(search)
     my_left = own(fresh)
@@ -493,32 +586,48 @@
     swap = [(i, groups - 1 - i) for i in range(groups)]
     other = lax.ppermute(arrived, "det", swap)
     pages = max(1, ranks * nodes // LANES)
-    big = pltpu.VMEM((2 * slots, LANES), jnp.float32)
-    room = pl.cdiv(2 * slots, BLOCK) * BLOCK + max(PREPARE, COLLECT, PROJECT)
-    few = pltpu.VMEM((room, LANES), jnp.float32)
-    partials, packs, coeffs = pl.pallas_call(
-        functools.partial(main_kernel, ranks, cap, dets, nodes, spacing),
-        out_shape=(
-            jax.ShapeDtypeStruct((ranks * groups * height, LANES), jnp.float32),
-            jax.ShapeDtypeStruct((2, height, LANES), jnp.float32),
+    f32 = jnp.float32
+    room = pl.cdiv(2 * slots, BLOCK) * BLOCK + max(COLLECT, PROJECT)
+    few = jax.ShapeDtypeStruct((room, LANES), f32)
+    shared = (
+        few, few, few, jax.ShapeDtypeStruct((pages, room, LANES), f32), few, few, few,
+        jax.ShapeDtypeStruct((5, room, LANES), f32),
+        jax.ShapeDtypeStruct((room * CHANNELS, LANES), f32),
+    )
+    arrival = [pltpu.VMEM((slots, LANES), f32)] * 3 + [pltpu.VMEM((ranks, LANES), f32)]
+    sizes = (ranks, cap, dets, nodes, spacing)
+    *state, packs, count = pl.pallas_call(
+        functools.partial(own_kernel, *sizes),
+        out_shape=shared + (
+            jax.ShapeDtypeStruct((2 * height // groups, LANES), f32),
+            jax.ShapeDtypeStruct((8, LANES), jnp.int32),
+        ),
+        in_specs=[vmem],
+        out_specs=(vmem,) * 11,
+        scratch_shapes=arrival,
+        compiler_params=params,
+        cost_estimate=pl.CostEstimate(flops=4_000_000_000, bytes_accessed=4_000_000, transcendentals=0),
+        name="own",
+    )(arrived.reshape(ranks * rows, LANES))
+    *_, partials, packs, coeffs = pl.pallas_call(
+        functools.partial(main_kernel, *sizes),
+        out_shape=shared + (
+            jax.ShapeDtypeStruct((ranks * groups * height, LANES), f32),
+            jax.ShapeDtypeStruct((2, height, LANES), f32),
             small,
         ),
-        in_specs=[vmem, vmem, hbm],
-        out_specs=(vmem, vmem, vmem),
-        scratch_shapes=[
-            big, big, big,
-            pltpu.VMEM((2, ranks, LANES), jnp.float32),
-            few, few, few,
-            pltpu.VMEM((pages, room, LANES), jnp.float32),
-            few, few, few,
-            pltpu.VMEM((room * CHANNELS, LANES), jnp.float32),
-            pltpu.VMEM((CHANNELS, room, LANES), jnp.float32),
-            pltpu.VMEM((8, BLOCK), jnp.float32),
+        in_specs=[vmem, hbm] + [vmem] * 11,
+        out_specs=(vmem,) * 12,
+        scratch_shapes=arrival + [
+            pltpu.VMEM((CHANNELS, room, LANES), f32),
+            pltpu.VMEM((2, 8, BLOCK), f32),
+            pltpu.VMEM((pages, room, LANES), f32),
             pltpu.SemaphoreType.DMA((1,)),
         ],
+        input_output_aliases={4 + k: k for k in range(9)},
         compiler_params=params,
         name="main",
-    )(arrived.reshape(ranks * rows, LANES), other.reshape(ranks * rows, LANES), pin(offset_coeffs.T))
+    )(other.reshape(ranks * rows, LANES), pin(offset_coeffs.T), packs, count, *state)
     gathered = lax.all_to_all(
         partials.reshape(ranks * groups, 1, height * LANES),
         ("tm", "det"), split_axis=0, concat_axis=0, tiled=True,

time: 38.1 us -> 37.2 us (0.976)
  waiting for transfers between devices: 1.54 us -> 0.12 us
  Pallas kernels: 7.1 us -> 8.28 us
  blocking collectives: 28.7 us -> 27.9 us
    ppermute x1, waiting for transfers between devices: 1.54 us -> 0.12 us  [body(): other = lax.ppermute(arrived, 'det', swap)]
    pallas_call x1 -> x2, Pallas kernels: 4.53 us -> 5.93 us  [the longest x1 4.51 us: body(): pl.pallas_call(functools.partial(main_kernel, *sizes), out_shape=shared +...]
    all_to_all x1, blocking collectives: 10.6 us -> 9.77 us  [body(): lax.all_to_all(partials.reshape(ranks * groups, 1, height * LANES), ('tm'...]
  transfers between devices with their start and end apart: 1 -> 1, of which waited for: 1 -> 1; matrix products, arithmetic and copies ran while one was open for 0% -> 0% of each run, Pallas kernels for 0% -> 4%
where the time goes in v5:
time: 37.2 us; the launch traced here: 37 us
  blocking collectives  27.9 us (75%)
  Pallas kernels  8.28 us (22%)
  between operations  0.65 us (2%)
    all_to_all x1, blocking collectives, body(): lax.all_to_all(outgoing.reshape(ranks, 1, rows * LANES), 'tm', split_axis...  18.1 us
    all_to_all x1, blocking collectives, body(): lax.all_to_all(partials.reshape(ranks * groups, 1, height * LANES), ('tm'...  9.77 us
    pallas_call x1, Pallas kernels, body(): pl.pallas_call(functools.partial(main_kernel, *sizes), out_shape=shared +...  4.51 us
    pallas_call x1, Pallas kernels, body(): pl.pallas_call(functools.partial(send_kernel, ranks, cap), out_shape=jax....  1.5 us
    pallas_call x1, Pallas kernels, body(): pl.pallas_call(functools.partial(own_kernel, *sizes), out_shape=shared +...  1.42 us
    pallas_call x1, Pallas kernels, body(): pl.pallas_call(functools.partial(finish_kernel, ranks, spacing), out_shap...  0.85 us
  transfers between devices with their start and end apart: 1, of which 1 were waited for; matrix products, arithmetic and copies ran while one was open for 0% of the time, Pallas kernels for 4%

profile of v5, /device:TPU:0, one launch (start us, length us, event | category | flops | bytes accessed | tf_op | source)
XLA Modules:
  0.0 37.0 jit_solution(2818562655528961205)
XLA Ops:
  0.6 1.5 %send.1 = f32[528,128]{1,0:T(8,128)S(1)} custom-call(s32[8,16]{1,0:T(8,128)} %patch_hbm.1, s32[1,8]{1,0:T(1,128)} %bitcast.20, f32[2,8]{1,0:T(2,128)} %bitcast.17, f32[2,8]{1,0:T(2,128)} %bitcast.18, s32[8,2048]{1,0:T(8,128)} %cell_hbm.1, f32[8,2048]{1,0:T(8,128)} %phase_hbm.1), custom_call_target="tpu_custom_call" | custom-call | tf_op jit(solution)/shard_map/send/pallas_call | solution.py:573
  2.1 18.1 %all_to_all.10 = f32[16,1,4224]{2,1,0:T(1,128)S(1)} all-to-all(f32[16,1,4224]{2,1,0:T(1,128)S(1)} %bitcast.12), channel_id=1, replica_groups=mesh['tm'=16,'det'=2] {'tm'}, dimensions={0} | all-to-all | bytes 540672 | tf_op jit(solution)/shard_map/all_to_all | solution.py:583
  20.3 0.0 collective-permute-start
  20.3 1.4 %own.1 = (f32[720,128]{1,0:T(8,128)S(1)}, f32[720,128]{1,0:T(8,128)S(1)}, f32[720,128]{1,0:T(8,128)S(1)}, f32[1,720,128]{2,1,0:T(8,128)S(1)}, f32[720,128]{1,0:T...) custom-call(f32[528,128]{1,0:T(8,128)S(1)} %bitcast.14), custom_call_target="tpu_custom_call" | custom-call | flops 4000000000 | bytes 4000000 | tf_op jit(solution)/shard_map/own/pallas_call | solution.py:599
  21.7 0.1 collective-permute-done
  21.8 4.5 %main.1 = (f32[720,128]{1,0:T(8,128)S(1)}, f32[720,128]{1,0:T(8,128)S(1)}, f32[720,128]{1,0:T(8,128)S(1)}, f32[1,720,128]{2,1,0:T(8,128)S(1)}, f32[720,128]{1,0:...) custom-call(f32[528,128]{1,0:T(8,128)S(1)} %bitcast.13, ...), custom_call_target="tpu_custom_call", output_to_operand_aliasing={{0}: (4, {}), {1}: (5, {}), {2}: (6, {}), {3}: (7, {}), {4}... | custom-call | tf_op jit(solution)/shard_map/main/pallas_call | solution.py:612
  26.3 9.8 %all_to_all.11 = f32[32,1,512]{2,1,0:T(1,128)S(1)} all-to-all(f32[32,1,512]{2,1,0:T(1,128)S(1)} %bitcast.16), channel_id=1, replica_groups=mesh['tm'=16,'det'=2] {'tm','det'}, dimensions={0} | all-to-all | bytes 131072 | tf_op jit(solution)/shard_map/all_to_all | solution.py:631
  36.1 0.8 %finish.1 = (f32[2,8]{1,0:T(2,128)}, f32[2,8]{1,0:T(2,128)}, f32[2,8]{1,0:T(2,128)}) custom-call(f32[128,128]{1,0:T(8,128)S(1)} %bitcast.15, f32[2,4,128]{2,1,0:T(4,128)S(1)} %get-tuple-element.32.packs_ref, f32[2,8]{1,0:T(2,128)S(1)} %get-tuple-element.33.coeffs_ref), custom_call_target="tpu_custom_call" | custom-call | tf_op jit(solution)/shard_map/finish/pallas_call | solution.py:635
Async XLA Ops:
  20.3 1.5 %collective-permute-start = (f32[16,1,4224]{2,1,0:T(1,128)S(1)}, f32[16,1,4224]{2,1,0:T(1,128)S(1)}, u32[]{:S(2)}, u32[]{:S(2)}) collective-permute-start(f32[16,1,4224]{2,1,0:T(1,128)S(1)} %all_to_all.10), channel_id=1, source_target_pairs={{0,1},{1,0},{2,3},{3,2},{4,5},{5,4},{6,7},{7,6},{8,9},{9,8},{10,11... | collective-permute-start | bytes 811016 | tf_op jit(solution)/shard_map/ppermute | solution.py:587

commit v6 on v5

--- a/solution.py
+++ b/solution.py
@@ -79,6 +79,10 @@
     third = (-3.0 * cube + 3.0 * square + 3.0 * fraction + 1.0) * (1.0 / 6.0)
     fourth = cube * (1.0 / 6.0)
     return (first, second, third, fourth)
+
+
+def aligned(index, unit):
+    return index if isinstance(index, int) else pl.multiple_of(index, unit)
 
 
 def lane_gather(table, index):
@@ -352,7 +356,7 @@
     source = source_of(ranks, cap, dets, knots * spacing, side, phase_ref, cell_ref, info_ref)
 
     def gather_block(block, carry):
-        here = pl.ds(pl.multiple_of(block * BLOCK, 32), BLOCK)
+        here = pl.ds(aligned(block * BLOCK, 32), BLOCK)
         few_phase[here, :], few_cell[here, :], few_info[here, :], found = take_slots(
             block * BLOCK, rank, source, dets, side, tables
         )
@@ -360,7 +364,8 @@
             table_ref[page, here, :] = rows
         return carry
 
-    lax.fori_loop(0, block_count(number, ranks * cap), gather_block, 0)
+    gather_block(0, 0)
+    lax.fori_loop(1, block_count(number, ranks * cap), gather_block, 0)
     bin_chunks(
         0, number >> log2(COLLECT), knots, spacing, few_phase, few_cell, few_info, table_ref,
         cos_ref, sin_ref, stream_ref, basis_ref, bin_ref,
@@ -400,21 +405,24 @@
     ready_blocks = block_count(ready, slots)
 
     def gather_block(block, carry):
-        here = pl.ds(pl.multiple_of(block * BLOCK, 32), BLOCK)
-        started = block < ready_blocks
+        here = pl.ds(aligned(block * BLOCK, 32), BLOCK)
+        def before(rows):
+            return rows if isinstance(block, int) else jnp.where(block < ready_blocks, rows, 0.0)
+
         phase, cell, info, found = take_slots(block * BLOCK, rank, source, dets, side, tables)
-        few_phase[here, :] = jnp.where(started, few_phase[here, :], 0.0) + phase
-        few_cell[here, :] = jnp.where(started, few_cell[here, :], 0.0) + cell
-        info = jnp.where(started, few_info[here, :], 0.0) + info
+        few_phase[here, :] = before(few_phase[here, :]) + phase
+        few_cell[here, :] = before(few_cell[here, :]) + cell
+        info = before(few_info[here, :]) + info
         few_info[here, :] = info
         turned = info.T
         turned_ref[0, pl.ds(block, 1), :] = turned[1:2, :]
         turned_ref[1, pl.ds(block, 1), :] = turned[2:3, :]
         for page, rows in enumerate(found):
-            table_ref[page, here, :] = jnp.where(started, table_ref[page, here, :], 0.0) + rows
+            table_ref[page, here, :] = before(table_ref[page, here, :]) + rows
         return carry
 
-    lax.fori_loop(0, blocks, gather_block, 0)
+    gather_block(0, 0)
+    lax.fori_loop(1, blocks, gather_block, 0)
 
     def steps(chunk):
         return (number + (chunk - 1)) >> log2(chunk)
@@ -429,14 +437,14 @@
         bin_ref[pl.ds(at, COLLECT * CHANNELS), :] = jnp.zeros((COLLECT * CHANNELS, LANES), jnp.float32)
         return carry
 
-    lax.fori_loop(steps(COLLECT), blocks * (BLOCK // COLLECT), clear, 0)
+    lax.fori_loop(steps(COLLECT), jnp.maximum(blocks, 1) * (BLOCK // COLLECT), clear, 0)
 
     def merge(block, carry):
-        at = pl.multiple_of(block * BLOCK, 32)
+        at = aligned(block * BLOCK, 32)
         names = few_info[pl.ds(at, BLOCK), 2:3]
 
         def add(other, carry):
-            there = pl.multiple_of(other * BLOCK, 32)
+            there = aligned(other * BLOCK, 32)
             same = (names == turned_ref[1, pl.ds(other, 1), :]).astype(jnp.bfloat16)
             for c in range(CHANNELS):
                 binned = bin_ref[pl.ds(there * CHANNELS + c, BLOCK, stride=CHANNELS), :]
@@ -444,17 +452,20 @@
                 share = dot(same, high)
                 if c != COUNT:
                     share = share + dot(same, (binned - high.astype(jnp.float32)).astype(jnp.bfloat16))
-                before = total_ref[c, pl.ds(at, BLOCK), :]
-                total_ref[c, pl.ds(at, BLOCK), :] = jnp.where(other == 0, share, before + share)
+                if not isinstance(other, int):
+                    share = share + total_ref[c, pl.ds(at, BLOCK), :]
+                total_ref[c, pl.ds(at, BLOCK), :] = share
             return carry
 
-        lax.fori_loop(0, blocks, add, 0)
+        add(0, 0)
+        lax.fori_loop(1, blocks, add, 0)
         return carry
 
-    lax.fori_loop(0, blocks, merge, 0)
+    merge(0, 0)
+    lax.fori_loop(1, blocks, merge, 0)
 
     def project(at):
-        here = pl.ds(pl.multiple_of(at, 16), PROJECT)
+        here = pl.ds(aligned(at, 16), PROJECT)
         signal, signal_cos, signal_sin, count, cos_sum, sin_sum, cos_cos, cos_sin_sum = (
             total_ref[c, here, :] for c in range(CHANNELS)
         )
@@ -483,7 +494,10 @@
         lane = iota((PROJECT, LANES), 1)
         pages = [jnp.zeros((PROJECT, LANES), jnp.float32) for _ in range(knots_ref.shape[0])]
         for term in range(5):
-            value = jnp.sum(basis_ref[term, here, :] * cleaned, axis=1, keepdims=True)
+            value = basis_ref[term, here, :] * cleaned
+            high = value.astype(jnp.bfloat16)
+            low = (value - high.astype(jnp.float32)).astype(jnp.bfloat16)
+            value = dot(jnp.concatenate([high, low], axis=1), jnp.ones((2 * LANES, LANES), jnp.bfloat16))
             knot = (base + (term - 1)) & (knots - 1)
             for page in range(len(pages)):
                 pages[page] = pages[page] + jnp.where(lane + page * LANES == knot, value, 0.0)
@@ -491,7 +505,7 @@
             knots_ref[page, here, :] = jnp.where(valid, sums, 0.0)
 
     def image_of(block, sums):
-        at = pl.multiple_of(block * BLOCK, 32)
+        at = aligned(block * BLOCK, 32)
         for first in range(0, BLOCK, PROJECT):
             project(at + first)
         det = (iota((2 * dets, BLOCK), 0) + 1).astype(jnp.float32)
@@ -501,7 +515,7 @@
         )
 
     image = tuple(jnp.zeros((2 * dets, LANES), jnp.float32) for _ in range(knots_ref.shape[0]))
-    image = lax.fori_loop(0, blocks, image_of, image)
+    image = lax.fori_loop(1, blocks, image_of, image_of(0, image))
     partial = jnp.concatenate(flatten(image, knots), axis=0)
     for target in range(out_ref.shape[0] // (2 * packed)):
         out_ref[target * 2 * packed : (target + 1) * 2 * packed, :] = partial

time: 37.2 us -> 36.7 us (0.987)
  Pallas kernels: 8.28 us -> 7.89 us
    pallas_call x1, Pallas kernels: 4.51 us -> 3.65 us  [body(): pl.pallas_call(functools.partial(main_kernel, *sizes), out_shape=shared +...]
    pallas_call x1, Pallas kernels: 1.42 us -> 1.89 us  [body(): pl.pallas_call(functools.partial(own_kernel, *sizes), out_shape=shared +...]
  transfers between devices with their start and end apart: 1 -> 1, of which waited for: 1 -> 0; matrix products, arithmetic and copies ran while one was open for 0% -> 0% of each run, Pallas kernels for 4% -> 5%
where the time goes in v6:
time: 36.7 us; the launch traced here: 36.6 us
  blocking collectives  28 us (76%)
  Pallas kernels  7.89 us (21%)
  between operations  0.66 us (2%)
    all_to_all x1, blocking collectives, body(): lax.all_to_all(outgoing.reshape(ranks, 1, rows * LANES), 'tm', split_axis...  18.1 us
    all_to_all x1, blocking collectives, body(): lax.all_to_all(partials.reshape(ranks * groups, 1, height * LANES), ('tm'...  9.88 us
    pallas_call x1, Pallas kernels, body(): pl.pallas_call(functools.partial(main_kernel, *sizes), out_shape=shared +...  3.65 us
    pallas_call x1, Pallas kernels, body(): pl.pallas_call(functools.partial(own_kernel, *sizes), out_shape=shared +...  1.89 us
    pallas_call x1, Pallas kernels, body(): pl.pallas_call(functools.partial(send_kernel, ranks, cap), out_shape=jax....  1.5 us
    pallas_call x1, Pallas kernels, body(): pl.pallas_call(functools.partial(finish_kernel, ranks, spacing), out_shap...  0.85 us
  transfers between devices with their start and end apart: 1, of which 0 were waited for; matrix products, arithmetic and copies ran while one was open for 0% of the time, Pallas kernels for 5%

profile of v6, /device:TPU:0, one launch (start us, length us, event | category | flops | bytes accessed | tf_op | source)
XLA Modules:
  0.0 36.6 jit_solution(9971925660759162259)
XLA Ops:
  0.6 1.5 %send.1 = f32[528,128]{1,0:T(8,128)S(1)} custom-call(s32[8,16]{1,0:T(8,128)} %patch_hbm.1, s32[1,8]{1,0:T(1,128)} %bitcast.20, f32[2,8]{1,0:T(2,128)} %bitcast.17, f32[2,8]{1,0:T(2,128)} %bitcast.18, s32[8,2048]{1,0:T(8,128)} %cell_hbm.1, f32[8,2048]{1,0:T(8,128)} %phase_hbm.1), custom_call_target="tpu_custom_call" | custom-call | tf_op jit(solution)/shard_map/send/pallas_call | solution.py:587
  2.1 18.1 %all_to_all.10 = f32[16,1,4224]{2,1,0:T(1,128)S(1)} all-to-all(f32[16,1,4224]{2,1,0:T(1,128)S(1)} %bitcast.12), channel_id=1, replica_groups=mesh['tm'=16,'det'=2] {'tm'}, dimensions={0} | all-to-all | bytes 540672 | tf_op jit(solution)/shard_map/all_to_all | solution.py:597
  20.3 0.0 collective-permute-start
  20.3 1.9 %own.1 = (f32[720,128]{1,0:T(8,128)S(1)}, f32[720,128]{1,0:T(8,128)S(1)}, f32[720,128]{1,0:T(8,128)S(1)}, f32[1,720,128]{2,1,0:T(8,128)S(1)}, f32[720,128]{1,0:T...) custom-call(f32[528,128]{1,0:T(8,128)S(1)} %bitcast.14), custom_call_target="tpu_custom_call" | custom-call | flops 4000000000 | bytes 4000000 | tf_op jit(solution)/shard_map/own/pallas_call | solution.py:613
  22.2 0.0 collective-permute-done
  22.2 3.7 %main.1 = (f32[720,128]{1,0:T(8,128)S(1)}, f32[720,128]{1,0:T(8,128)S(1)}, f32[720,128]{1,0:T(8,128)S(1)}, f32[1,720,128]{2,1,0:T(8,128)S(1)}, f32[720,128]{1,0:...) custom-call(f32[528,128]{1,0:T(8,128)S(1)} %bitcast.13, ...), custom_call_target="tpu_custom_call", output_to_operand_aliasing={{0}: (4, {}), {1}: (5, {}), {2}: (6, {}), {3}: (7, {}), {4}... | custom-call | tf_op jit(solution)/shard_map/main/pallas_call | solution.py:626
  25.8 9.9 %all_to_all.11 = f32[32,1,512]{2,1,0:T(1,128)S(1)} all-to-all(f32[32,1,512]{2,1,0:T(1,128)S(1)} %bitcast.16), channel_id=1, replica_groups=mesh['tm'=16,'det'=2] {'tm','det'}, dimensions={0} | all-to-all | bytes 131072 | tf_op jit(solution)/shard_map/all_to_all | solution.py:645
  35.7 0.8 %finish.1 = (f32[2,8]{1,0:T(2,128)}, f32[2,8]{1,0:T(2,128)}, f32[2,8]{1,0:T(2,128)}) custom-call(f32[128,128]{1,0:T(8,128)S(1)} %bitcast.15, f32[2,4,128]{2,1,0:T(4,128)S(1)} %get-tuple-element.32.packs_ref, f32[2,8]{1,0:T(2,128)S(1)} %get-tuple-element.33.coeffs_ref), custom_call_target="tpu_custom_call" | custom-call | tf_op jit(solution)/shard_map/finish/pallas_call | solution.py:649
Async XLA Ops:
  20.3 1.9 %collective-permute-start = (f32[16,1,4224]{2,1,0:T(1,128)S(1)}, f32[16,1,4224]{2,1,0:T(1,128)S(1)}, u32[]{:S(2)}, u32[]{:S(2)}) collective-permute-start(f32[16,1,4224]{2,1,0:T(1,128)S(1)} %all_to_all.10), channel_id=1, source_target_pairs={{0,1},{1,0},{2,3},{3,2},{4,5},{5,4},{6,7},{7,6},{8,9},{9,8},{10,11... | collective-permute-start | bytes 811016 | tf_op jit(solution)/shard_map/ppermute | solution.py:601

commit v7 on v6

--- a/solution.py
+++ b/solution.py
@@ -14,9 +14,9 @@
 OWNER_TILES = PIX_OWN // LANES
 CHANNELS = 8
 COUNT = 3
-BLOCK = 160
+BLOCK = 176
 COLLECT = 32
-PROJECT = 80
+PROJECT = 64
 VMEM_BYTES = 32 * 1024 * 1024
 
 SIN_TERMS = (1.0, -1.0 / 6, 1.0 / 120, -1.0 / 5040, 1.0 / 362880, -1.0 / 39916800, 1.0 / 6227020800)
@@ -279,7 +279,7 @@
     pages = table_ref.shape[0]
 
     def prepare(step):
-        at = pl.multiple_of(step * COLLECT, COLLECT)
+        at = aligned(step * COLLECT, COLLECT)
         cosine, sine = cos_sin(2.0 * few_phase[pl.ds(at, COLLECT), :])
         base, interval, weights = spline(few_info, spacing, at, COLLECT)
         for term, weight in enumerate(five_weights(interval == base, weights)):
@@ -300,7 +300,7 @@
     channel = iota((CHANNELS, LANES), 0)
     zeros = jnp.zeros((2 * CHANNELS, LANES), jnp.bfloat16)
 
-    def collect(step, carry):
+    def collect(step):
         for k in range(COLLECT // 2):
             at = step * COLLECT + 2 * k
             pieces, cells = [], []
@@ -325,20 +325,21 @@
                 ],
                 axis=0,
             )
-            hits = jnp.where(jnp.concatenate(cells, axis=1) == down, jnp.bfloat16(1), jnp.bfloat16(0))
-            sums = lax.dot_general(
-                entry, hits, (((1,), (1,)), ((), ())), preferred_element_type=jnp.float32
-            )
+            hits = jnp.where(jnp.concatenate(cells, axis=1) == down, jnp.int8(1), jnp.int8(0))
+            sums = dot(entry, hits.T.astype(jnp.bfloat16))
             for m in range(2):
                 base = 2 * CHANNELS * m
                 bin_ref[pl.ds((at + m) * CHANNELS, CHANNELS), :] = (
                     sums[base : base + CHANNELS] + sums[base + CHANNELS : base + 2 * CHANNELS]
                 )
+    def both(step, carry):
+        collect(step)
         prepare(step + 1)
         return carry
 
+
     prepare(first)
-    lax.fori_loop(first, last, collect, 0)
+    lax.fori_loop(first, last, both, 0)
 
 
 def own_kernel(
@@ -356,7 +357,7 @@
     source = source_of(ranks, cap, dets, knots * spacing, side, phase_ref, cell_ref, info_ref)
 
     def gather_block(block, carry):
-        here = pl.ds(aligned(block * BLOCK, 32), BLOCK)
+        here = pl.ds(aligned(block * BLOCK, 16), BLOCK)
         few_phase[here, :], few_cell[here, :], few_info[here, :], found = take_slots(
             block * BLOCK, rank, source, dets, side, tables
         )
@@ -405,7 +406,7 @@
     ready_blocks = block_count(ready, slots)
 
     def gather_block(block, carry):
-        here = pl.ds(aligned(block * BLOCK, 32), BLOCK)
+        here = pl.ds(aligned(block * BLOCK, 16), BLOCK)
         def before(rows):
             return rows if isinstance(block, int) else jnp.where(block < ready_blocks, rows, 0.0)
 
@@ -437,14 +438,15 @@
         bin_ref[pl.ds(at, COLLECT * CHANNELS), :] = jnp.zeros((COLLECT * CHANNELS, LANES), jnp.float32)
         return carry
 
-    lax.fori_loop(steps(COLLECT), jnp.maximum(blocks, 1) * (BLOCK // COLLECT), clear, 0)
+    end = (jnp.maximum(blocks, 1) * BLOCK + (COLLECT - 1)) >> log2(COLLECT)
+    lax.fori_loop(steps(COLLECT), end, clear, 0)
 
     def merge(block, carry):
-        at = aligned(block * BLOCK, 32)
+        at = aligned(block * BLOCK, 16)
         names = few_info[pl.ds(at, BLOCK), 2:3]
 
         def add(other, carry):
-            there = aligned(other * BLOCK, 32)
+            there = aligned(other * BLOCK, 16)
             same = (names == turned_ref[1, pl.ds(other, 1), :]).astype(jnp.bfloat16)
             for c in range(CHANNELS):
                 binned = bin_ref[pl.ds(there * CHANNELS + c, BLOCK, stride=CHANNELS), :]
@@ -464,8 +466,8 @@
     merge(0, 0)
     lax.fori_loop(1, blocks, merge, 0)
 
-    def project(at):
-        here = pl.ds(aligned(at, 16), PROJECT)
+    def project(at, size):
+        here = pl.ds(aligned(at, 16), size)
         signal, signal_cos, signal_sin, count, cos_sum, sin_sum, cos_cos, cos_sin_sum = (
             total_ref[c, here, :] for c in range(CHANNELS)
         )
@@ -491,8 +493,8 @@
         cleaned = stream_ref[here, :] - projected
         valid = few_info[here, 1:2] > 0.5
         base = few_info[here, 0:1].astype(jnp.int32) >> log2(spacing)
-        lane = iota((PROJECT, LANES), 1)
-        pages = [jnp.zeros((PROJECT, LANES), jnp.float32) for _ in range(knots_ref.shape[0])]
+        lane = iota((size, LANES), 1)
+        pages = [jnp.zeros((size, LANES), jnp.float32) for _ in range(knots_ref.shape[0])]
         for term in range(5):
             value = basis_ref[term, here, :] * cleaned
             high = value.astype(jnp.bfloat16)
@@ -505,9 +507,9 @@
             knots_ref[page, here, :] = jnp.where(valid, sums, 0.0)
 
     def image_of(block, sums):
-        at = aligned(block * BLOCK, 32)
+        at = aligned(block * BLOCK, 16)
         for first in range(0, BLOCK, PROJECT):
-            project(at + first)
+            project(at + first, min(PROJECT, BLOCK - first))
         det = (iota((2 * dets, BLOCK), 0) + 1).astype(jnp.float32)
         chosen = (turned_ref[0, pl.ds(block, 1), :] == det).astype(jnp.bfloat16)
         return tuple(

time: 36.7 us -> 36.3 us (0.989)
  Pallas kernels: 7.89 us -> 7.39 us
    pallas_call x1, Pallas kernels: 1.89 us -> 1.34 us  [body(): pl.pallas_call(functools.partial(own_kernel, *sizes), out_shape=shared +...]
  transfers between devices with their start and end apart: 1 -> 1, of which waited for: 0 -> 1; matrix products, arithmetic and copies ran while one was open for 0% -> 0% of each run, Pallas kernels for 5% -> 4%
where the time goes in v7:
time: 36.3 us; the launch traced here: 36.1 us
  blocking collectives  27.8 us (77%)
  Pallas kernels  7.39 us (20%)
  between operations  0.66 us (2%)
    all_to_all x1, blocking collectives, body(): lax.all_to_all(outgoing.reshape(ranks, 1, rows * LANES), 'tm', split_axis...  18.1 us
    all_to_all x1, blocking collectives, body(): lax.all_to_all(partials.reshape(ranks * groups, 1, height * LANES), ('tm'...  9.69 us
    pallas_call x1, Pallas kernels, body(): pl.pallas_call(functools.partial(main_kernel, *sizes), out_shape=shared +...  3.71 us
    pallas_call x1, Pallas kernels, body(): pl.pallas_call(functools.partial(send_kernel, ranks, cap), out_shape=jax....  1.5 us
    pallas_call x1, Pallas kernels, body(): pl.pallas_call(functools.partial(own_kernel, *sizes), out_shape=shared +...  1.34 us
    pallas_call x1, Pallas kernels, body(): pl.pallas_call(functools.partial(finish_kernel, ranks, spacing), out_shap...  0.85 us
  transfers between devices with their start and end apart: 1, of which 1 were waited for; matrix products, arithmetic and copies ran while one was open for 0% of the time, Pallas kernels for 4%

profile of v7, /device:TPU:0, one launch (start us, length us, event | category | flops | bytes accessed | tf_op | source)
XLA Modules:
  0.0 36.1 jit_solution(15286083648639884117)
XLA Ops:
  0.6 1.5 %send.1 = f32[528,128]{1,0:T(8,128)S(1)} custom-call(s32[8,16]{1,0:T(8,128)} %patch_hbm.1, s32[1,8]{1,0:T(1,128)} %bitcast.20, f32[2,8]{1,0:T(2,128)} %bitcast.17, f32[2,8]{1,0:T(2,128)} %bitcast.18, s32[8,2048]{1,0:T(8,128)} %cell_hbm.1, f32[8,2048]{1,0:T(8,128)} %phase_hbm.1), custom_call_target="tpu_custom_call" | custom-call | tf_op jit(solution)/shard_map/send/pallas_call | solution.py:589
  2.1 18.1 %all_to_all.10 = f32[16,1,4224]{2,1,0:T(1,128)S(1)} all-to-all(f32[16,1,4224]{2,1,0:T(1,128)S(1)} %bitcast.12), channel_id=1, replica_groups=mesh['tm'=16,'det'=2] {'tm'}, dimensions={0} | all-to-all | bytes 540672 | tf_op jit(solution)/shard_map/all_to_all | solution.py:599
  20.3 0.0 collective-permute-start
  20.3 1.3 %own.1 = (f32[592,128]{1,0:T(8,128)S(1)}, f32[592,128]{1,0:T(8,128)S(1)}, f32[592,128]{1,0:T(8,128)S(1)}, f32[1,592,128]{2,1,0:T(8,128)S(1)}, f32[592,128]{1,0:T...) custom-call(f32[528,128]{1,0:T(8,128)S(1)} %bitcast.14), custom_call_target="tpu_custom_call" | custom-call | flops 4000000000 | bytes 4000000 | tf_op jit(solution)/shard_map/own/pallas_call | solution.py:615
  21.6 0.2 collective-permute-done
  21.8 3.7 %main.1 = (f32[592,128]{1,0:T(8,128)S(1)}, f32[592,128]{1,0:T(8,128)S(1)}, f32[592,128]{1,0:T(8,128)S(1)}, f32[1,592,128]{2,1,0:T(8,128)S(1)}, f32[592,128]{1,0:...) custom-call(f32[528,128]{1,0:T(8,128)S(1)} %bitcast.13, ...), custom_call_target="tpu_custom_call", output_to_operand_aliasing={{0}: (4, {}), {1}: (5, {}), {2}: (6, {}), {3}: (7, {}), {4}... | custom-call | tf_op jit(solution)/shard_map/main/pallas_call | solution.py:628
  25.5 9.7 %all_to_all.11 = f32[32,1,512]{2,1,0:T(1,128)S(1)} all-to-all(f32[32,1,512]{2,1,0:T(1,128)S(1)} %bitcast.16), channel_id=1, replica_groups=mesh['tm'=16,'det'=2] {'tm','det'}, dimensions={0} | all-to-all | bytes 131072 | tf_op jit(solution)/shard_map/all_to_all | solution.py:647
  35.2 0.8 %finish.1 = (f32[2,8]{1,0:T(2,128)}, f32[2,8]{1,0:T(2,128)}, f32[2,8]{1,0:T(2,128)}) custom-call(f32[128,128]{1,0:T(8,128)S(1)} %bitcast.15, f32[2,4,128]{2,1,0:T(4,128)S(1)} %get-tuple-element.32.packs_ref, f32[2,8]{1,0:T(2,128)S(1)} %get-tuple-element.33.coeffs_ref), custom_call_target="tpu_custom_call" | custom-call | tf_op jit(solution)/shard_map/finish/pallas_call | solution.py:651
Async XLA Ops:
  20.3 1.5 %collective-permute-start = (f32[16,1,4224]{2,1,0:T(1,128)S(1)}, f32[16,1,4224]{2,1,0:T(1,128)S(1)}, u32[]{:S(2)}, u32[]{:S(2)}) collective-permute-start(f32[16,1,4224]{2,1,0:T(1,128)S(1)} %all_to_all.10), channel_id=1, source_target_pairs={{0,1},{1,0},{2,3},{3,2},{4,5},{5,4},{6,7},{7,6},{8,9},{9,8},{10,11... | collective-permute-start | bytes 811016 | tf_op jit(solution)/shard_map/ppermute | solution.py:603

commit v8 on v7

--- a/solution.py
+++ b/solution.py
@@ -47,7 +47,9 @@
 
 def exact_dot(selector, x):
     high, middle, low = split3(x)
-    return (dot(selector, high) + dot(selector, middle)) + dot(selector, low)
+    width = x.shape[1]
+    parts = dot(selector, jnp.concatenate([high, middle, low], axis=1))
+    return (parts[:, :width] + parts[:, width : 2 * width]) + parts[:, 2 * width :]
 
 
 def horner(x, terms):
@@ -119,11 +121,16 @@
     rank_col = jnp.sum(jnp.where(same & (there < here), 1.0, 0.0), axis=1, keepdims=True)
     slot_row = (owner_t[0:1, :] * cap + rank_row).astype(jnp.int32)
     place = (iota((ranks * cap, blocks), 0) == slot_row).astype(jnp.bfloat16)
+    for copy in copies[1:]:
+        copy.wait()
+    cells = jnp.concatenate([cell_ref[:, c * LANES : (c + 1) * LANES] for c in range(columns)], axis=0)
+    pixels = (tiles * LANES + cells).astype(jnp.float32)
+    phases = jnp.concatenate([phase_ref[:, c * LANES : (c + 1) * LANES] for c in range(columns)], axis=0)
+    moved = exact_dot(place, jnp.concatenate([phases, pixels], axis=1))
+    slot_phase, slot_pixel = moved[:, :LANES], moved[:, LANES:]
     lane = iota(square, 1)
     small = iota((dets, LANES), 1)
     det_lane = iota((dets, LANES), 0)
-    for copy in copies[1:4]:
-        copy.wait()
     offsets = jnp.broadcast_to(offset_ref[...], (dets, dets))
     diagonal = iota((dets, dets), 0) == iota((dets, dets), 1)
     shift = jnp.sum(jnp.where(diagonal, offsets, 0).astype(jnp.float32), axis=1, keepdims=True)
@@ -143,13 +150,6 @@
             at = (3 * cap + kind * dets * nodes + n) + det_lane * nodes
             knots = knots + jnp.sum(jnp.where(small == at, column, 0.0), axis=0, keepdims=True)
     info = info + knots
-    copies[4].wait()
-    cells = jnp.concatenate([cell_ref[:, c * LANES : (c + 1) * LANES] for c in range(columns)], axis=0)
-    pixels = (tiles * LANES + cells).astype(jnp.float32)
-    copies[5].wait()
-    phases = jnp.concatenate([phase_ref[:, c * LANES : (c + 1) * LANES] for c in range(columns)], axis=0)
-    moved = exact_dot(place, jnp.concatenate([phases, pixels], axis=1))
-    slot_phase, slot_pixel = moved[:, :LANES], moved[:, LANES:]
     for o in range(ranks):
         out_ref[o * rows : o * rows + cap, :] = slot_phase[o * cap : (o + 1) * cap, :]
         out_ref[o * rows + cap : o * rows + 2 * cap, :] = slot_pixel[o * cap : (o + 1) * cap, :]
@@ -451,9 +451,12 @@
             for c in range(CHANNELS):
                 binned = bin_ref[pl.ds(there * CHANNELS + c, BLOCK, stride=CHANNELS), :]
                 high = binned.astype(jnp.bfloat16)
-                share = dot(same, high)
-                if c != COUNT:
-                    share = share + dot(same, (binned - high.astype(jnp.float32)).astype(jnp.bfloat16))
+                if c == COUNT:
+                    share = dot(same, high)
+                else:
+                    low = (binned - high.astype(jnp.float32)).astype(jnp.bfloat16)
+                    share = dot(same, jnp.concatenate([high, low], axis=1))
+                    share = share[:, :LANES] + share[:, LANES:]
                 if not isinstance(other, int):
                     share = share + total_ref[c, pl.ds(at, BLOCK), :]
                 total_ref[c, pl.ds(at, BLOCK), :] = share

time: 36.3 us -> 35.9 us (0.989)
  Pallas kernels: 7.39 us -> 6.98 us
    pallas_call x1, Pallas kernels: 3.71 us -> 3.19 us  [body(): pl.pallas_call(functools.partial(main_kernel, *sizes), out_shape=shared +...]
  transfers between devices with their start and end apart: 1 -> 1, of which waited for: 1 -> 0; matrix products, arithmetic and copies ran while one was open for 0% -> 0% of each run, Pallas kernels for 4% -> 5%
where the time goes in v8:
time: 35.9 us; the launch traced here: 35.8 us
  blocking collectives  28.1 us (78%)
  Pallas kernels  6.98 us (19%)
  between operations  0.67 us (2%)
    all_to_all x1, blocking collectives, body(): lax.all_to_all(outgoing.reshape(ranks, 1, rows * LANES), 'tm', split_axis...  18.1 us
    all_to_all x1, blocking collectives, body(): lax.all_to_all(partials.reshape(ranks * groups, 1, height * LANES), ('tm'...  9.97 us
    pallas_call x1, Pallas kernels, body(): pl.pallas_call(functools.partial(main_kernel, *sizes), out_shape=shared +...  3.19 us
    pallas_call x1, Pallas kernels, body(): pl.pallas_call(functools.partial(own_kernel, *sizes), out_shape=shared +...  1.67 us
    pallas_call x1, Pallas kernels, body(): pl.pallas_call(functools.partial(send_kernel, ranks, cap), out_shape=jax....  1.27 us
    pallas_call x1, Pallas kernels, body(): pl.pallas_call(functools.partial(finish_kernel, ranks, spacing), out_shap...  0.85 us
  transfers between devices with their start and end apart: 1, of which 0 were waited for; matrix products, arithmetic and copies ran while one was open for 0% of the time, Pallas kernels for 5%

profile of v8, /device:TPU:0, one launch (start us, length us, event | category | flops | bytes accessed | tf_op | source)
XLA Modules:
  0.0 35.8 jit_solution(10410889702448699717)
XLA Ops:
  0.6 1.3 %send.1 = f32[528,128]{1,0:T(8,128)S(1)} custom-call(s32[8,16]{1,0:T(8,128)} %patch_hbm.1, s32[1,8]{1,0:T(1,128)} %bitcast.20, f32[2,8]{1,0:T(2,128)} %bitcast.17, f32[2,8]{1,0:T(2,128)} %bitcast.18, s32[8,2048]{1,0:T(8,128)} %cell_hbm.1, f32[8,2048]{1,0:T(8,128)} %phase_hbm.1), custom_call_target="tpu_custom_call" | custom-call | tf_op jit(solution)/shard_map/send/pallas_call | solution.py:592
  1.9 18.1 %all_to_all.10 = f32[16,1,4224]{2,1,0:T(1,128)S(1)} all-to-all(f32[16,1,4224]{2,1,0:T(1,128)S(1)} %bitcast.12), channel_id=1, replica_groups=mesh['tm'=16,'det'=2] {'tm'}, dimensions={0} | all-to-all | bytes 540672 | tf_op jit(solution)/shard_map/all_to_all | solution.py:602
  20.0 0.0 collective-permute-start
  20.1 1.7 %own.1 = (f32[592,128]{1,0:T(8,128)S(1)}, f32[592,128]{1,0:T(8,128)S(1)}, f32[592,128]{1,0:T(8,128)S(1)}, f32[1,592,128]{2,1,0:T(8,128)S(1)}, f32[592,128]{1,0:T...) custom-call(f32[528,128]{1,0:T(8,128)S(1)} %bitcast.14), custom_call_target="tpu_custom_call" | custom-call | flops 4000000000 | bytes 4000000 | tf_op jit(solution)/shard_map/own/pallas_call | solution.py:618
  21.7 0.0 collective-permute-done
  21.7 3.2 %main.1 = (f32[592,128]{1,0:T(8,128)S(1)}, f32[592,128]{1,0:T(8,128)S(1)}, f32[592,128]{1,0:T(8,128)S(1)}, f32[1,592,128]{2,1,0:T(8,128)S(1)}, f32[592,128]{1,0:...) custom-call(f32[528,128]{1,0:T(8,128)S(1)} %bitcast.13, ...), custom_call_target="tpu_custom_call", output_to_operand_aliasing={{0}: (4, {}), {1}: (5, {}), {2}: (6, {}), {3}: (7, {}), {4}... | custom-call | tf_op jit(solution)/shard_map/main/pallas_call | solution.py:631
  24.9 10.0 %all_to_all.11 = f32[32,1,512]{2,1,0:T(1,128)S(1)} all-to-all(f32[32,1,512]{2,1,0:T(1,128)S(1)} %bitcast.16), channel_id=1, replica_groups=mesh['tm'=16,'det'=2] {'tm','det'}, dimensions={0} | all-to-all | bytes 131072 | tf_op jit(solution)/shard_map/all_to_all | solution.py:650
  34.9 0.8 %finish.1 = (f32[2,8]{1,0:T(2,128)}, f32[2,8]{1,0:T(2,128)}, f32[2,8]{1,0:T(2,128)}) custom-call(f32[128,128]{1,0:T(8,128)S(1)} %bitcast.15, f32[2,4,128]{2,1,0:T(4,128)S(1)} %get-tuple-element.32.packs_ref, f32[2,8]{1,0:T(2,128)S(1)} %get-tuple-element.33.coeffs_ref), custom_call_target="tpu_custom_call" | custom-call | tf_op jit(solution)/shard_map/finish/pallas_call | solution.py:654
Async XLA Ops:
  20.0 1.7 %collective-permute-start = (f32[16,1,4224]{2,1,0:T(1,128)S(1)}, f32[16,1,4224]{2,1,0:T(1,128)S(1)}, u32[]{:S(2)}, u32[]{:S(2)}) collective-permute-start(f32[16,1,4224]{2,1,0:T(1,128)S(1)} %all_to_all.10), channel_id=1, source_target_pairs={{0,1},{1,0},{2,3},{3,2},{4,5},{5,4},{6,7},{7,6},{8,9},{9,8},{10,11... | collective-permute-start | bytes 811016 | tf_op jit(solution)/shard_map/ppermute | solution.py:606

commit v9 on v8

--- a/solution.py
+++ b/solution.py
@@ -275,7 +275,7 @@
     return [jnp.where(early, padded[term + 1], padded[term]) for term in range(5)]
 
 
-def bin_chunks(first, last, knots, spacing, few_phase, few_cell, few_info, table_ref, cos_ref, sin_ref, stream_ref, basis_ref, bin_ref):
+def binning(knots, spacing, few_phase, few_cell, few_info, table_ref, cos_ref, sin_ref, stream_ref, basis_ref, bin_ref):
     pages = table_ref.shape[0]
 
     def prepare(step):
@@ -332,14 +332,13 @@
                 bin_ref[pl.ds((at + m) * CHANNELS, CHANNELS), :] = (
                     sums[base : base + CHANNELS] + sums[base + CHANNELS : base + 2 * CHANNELS]
                 )
+
     def both(step, carry):
         collect(step)
         prepare(step + 1)
         return carry
 
-
-    prepare(first)
-    lax.fori_loop(first, last, both, 0)
+    return prepare, both
 
 
 def own_kernel(
@@ -365,12 +364,16 @@
             table_ref[page, here, :] = rows
         return carry
 
+    prepare, both = binning(
+        knots, spacing, few_phase, few_cell, few_info, table_ref,
+        cos_ref, sin_ref, stream_ref, basis_ref, bin_ref,
+    )
     gather_block(0, 0)
+    prepare(0)
+    room = pl.cdiv(BLOCK, COLLECT) * COLLECT * CHANNELS
+    bin_ref[0:room, :] = jnp.zeros((room, LANES), jnp.float32)
     lax.fori_loop(1, block_count(number, ranks * cap), gather_block, 0)
-    bin_chunks(
-        0, number >> log2(COLLECT), knots, spacing, few_phase, few_cell, few_info, table_ref,
-        cos_ref, sin_ref, stream_ref, basis_ref, bin_ref,
-    )
+    lax.fori_loop(0, number >> log2(COLLECT), both, 0)
 
 
 def block_count(number, most):
@@ -422,24 +425,27 @@
             table_ref[page, here, :] = before(table_ref[page, here, :]) + rows
         return carry
 
-    gather_block(0, 0)
-    lax.fori_loop(1, blocks, gather_block, 0)
-
-    def steps(chunk):
-        return (number + (chunk - 1)) >> log2(chunk)
-
-    bin_chunks(
-        ready >> log2(COLLECT), steps(COLLECT), knots, spacing, few_phase, few_cell, few_info, table_ref,
+    prepare, both = binning(
+        knots, spacing, few_phase, few_cell, few_info, table_ref,
         cos_ref, sin_ref, stream_ref, basis_ref, bin_ref,
     )
+    first, last = ready >> log2(COLLECT), (number + (COLLECT - 1)) >> log2(COLLECT)
 
     def clear(step, carry):
         at = pl.multiple_of(step * COLLECT * CHANNELS, COLLECT * CHANNELS)
         bin_ref[pl.ds(at, COLLECT * CHANNELS), :] = jnp.zeros((COLLECT * CHANNELS, LANES), jnp.float32)
         return carry
 
-    end = (jnp.maximum(blocks, 1) * BLOCK + (COLLECT - 1)) >> log2(COLLECT)
-    lax.fori_loop(steps(COLLECT), end, clear, 0)
+    gather_block(0, 0)
+    prepare(first)
+
+    @pl.when(blocks > 1)
+    def _():
+        lax.fori_loop(1, blocks, gather_block, 0)
+        lax.fori_loop(last, (blocks * BLOCK + (COLLECT - 1)) >> log2(COLLECT), clear, 0)
+        prepare(first)
+
+    lax.fori_loop(first, last, both, 0)
 
     def merge(block, carry):
         at = aligned(block * BLOCK, 16)
@@ -463,11 +469,9 @@
             return carry
 
         add(0, 0)
-        lax.fori_loop(1, blocks, add, 0)
+        if not isinstance(block, int):
+            lax.fori_loop(1, blocks, add, 0)
         return carry
-
-    merge(0, 0)
-    lax.fori_loop(1, blocks, merge, 0)
 
     def project(at, size):
         here = pl.ds(aligned(at, 16), size)
@@ -519,11 +523,20 @@
             total + exact_dot(chosen, knots_ref[page, pl.ds(at, BLOCK), :]) for page, total in enumerate(sums)
         )
 
-    image = tuple(jnp.zeros((2 * dets, LANES), jnp.float32) for _ in range(knots_ref.shape[0]))
-    image = lax.fori_loop(1, blocks, image_of, image_of(0, image))
-    partial = jnp.concatenate(flatten(image, knots), axis=0)
-    for target in range(out_ref.shape[0] // (2 * packed)):
-        out_ref[target * 2 * packed : (target + 1) * 2 * packed, :] = partial
+    def write(image):
+        partial = jnp.concatenate(flatten(image, knots), axis=0)
+        for target in range(out_ref.shape[0] // (2 * packed)):
+            out_ref[target * 2 * packed : (target + 1) * 2 * packed, :] = partial
+
+    zero = tuple(jnp.zeros((2 * dets, LANES), jnp.float32) for _ in range(knots_ref.shape[0]))
+    merge(0, 0)
+    write(image_of(0, zero))
+
+    @pl.when(blocks > 1)
+    def _():
+        lax.fori_loop(0, blocks, merge, 0)
+        write(lax.fori_loop(0, blocks, image_of, zero))
+
     coeffs_copy.wait()
 
 

time: 35.9 us -> 35.7 us (level)
  Pallas kernels: 6.98 us -> 6.38 us
    pallas_call x1, Pallas kernels: 3.19 us -> 2.66 us  [body(): pl.pallas_call(functools.partial(main_kernel, *sizes), out_shape=shared +...]
where the time goes in v9:
time: 35.7 us; the launch traced here: 35.4 us
  blocking collectives  28.4 us (80%)
  Pallas kernels  6.38 us (18%)
  between operations  0.67 us (2%)
    all_to_all x1, blocking collectives, body(): lax.all_to_all(outgoing.reshape(ranks, 1, rows * LANES), 'tm', split_axis...  18.1 us
    all_to_all x1, blocking collectives, body(): lax.all_to_all(partials.reshape(ranks * groups, 1, height * LANES), ('tm'...  10.3 us
    pallas_call x1, Pallas kernels, body(): pl.pallas_call(functools.partial(main_kernel, *sizes), out_shape=shared +...  2.66 us
    pallas_call x1, Pallas kernels, body(): pl.pallas_call(functools.partial(own_kernel, *sizes), out_shape=shared +...  1.6 us
    pallas_call x1, Pallas kernels, body(): pl.pallas_call(functools.partial(send_kernel, ranks, cap), out_shape=jax....  1.27 us
    pallas_call x1, Pallas kernels, body(): pl.pallas_call(functools.partial(finish_kernel, ranks, spacing), out_shap...  0.85 us
  transfers between devices with their start and end apart: 1, of which 0 were waited for; matrix products, arithmetic and copies ran while one was open for 0% of the time, Pallas kernels for 5%

profile of v9, /device:TPU:0, one launch (start us, length us, event | category | flops | bytes accessed | tf_op | source)
XLA Modules:
  0.0 35.4 jit_solution(18149144125701336364)
XLA Ops:
  0.6 1.3 %send.1 = f32[528,128]{1,0:T(8,128)S(1)} custom-call(s32[8,16]{1,0:T(8,128)} %patch_hbm.1, s32[1,8]{1,0:T(1,128)} %bitcast.20, f32[2,8]{1,0:T(2,128)} %bitcast.17, f32[2,8]{1,0:T(2,128)} %bitcast.18, s32[8,2048]{1,0:T(8,128)} %cell_hbm.1, f32[8,2048]{1,0:T(8,128)} %phase_hbm.1), custom_call_target="tpu_custom_call" | custom-call | tf_op jit(solution)/shard_map/send/pallas_call | solution.py:605
  1.9 18.1 %all_to_all.10 = f32[16,1,4224]{2,1,0:T(1,128)S(1)} all-to-all(f32[16,1,4224]{2,1,0:T(1,128)S(1)} %bitcast.12), channel_id=1, replica_groups=mesh['tm'=16,'det'=2] {'tm'}, dimensions={0} | all-to-all | bytes 540672 | tf_op jit(solution)/shard_map/all_to_all | solution.py:615
  20.0 0.0 collective-permute-start
  20.1 1.6 %own.1 = (f32[592,128]{1,0:T(8,128)S(1)}, f32[592,128]{1,0:T(8,128)S(1)}, f32[592,128]{1,0:T(8,128)S(1)}, f32[1,592,128]{2,1,0:T(8,128)S(1)}, f32[592,128]{1,0:T...) custom-call(f32[528,128]{1,0:T(8,128)S(1)} %bitcast.14), custom_call_target="tpu_custom_call" | custom-call | flops 4000000000 | bytes 4000000 | tf_op jit(solution)/shard_map/own/pallas_call | solution.py:631
  21.7 0.0 collective-permute-done
  21.7 2.7 %main.1 = (f32[592,128]{1,0:T(8,128)S(1)}, f32[592,128]{1,0:T(8,128)S(1)}, f32[592,128]{1,0:T(8,128)S(1)}, f32[1,592,128]{2,1,0:T(8,128)S(1)}, f32[592,128]{1,0:...) custom-call(f32[528,128]{1,0:T(8,128)S(1)} %bitcast.13, ...), custom_call_target="tpu_custom_call", output_to_operand_aliasing={{0}: (4, {}), {1}: (5, {}), {2}: (6, {}), {3}: (7, {}), {4}... | custom-call | tf_op jit(solution)/shard_map/main/pallas_call | solution.py:644
  24.3 10.3 %all_to_all.11 = f32[32,1,512]{2,1,0:T(1,128)S(1)} all-to-all(f32[32,1,512]{2,1,0:T(1,128)S(1)} %bitcast.16), channel_id=1, replica_groups=mesh['tm'=16,'det'=2] {'tm','det'}, dimensions={0} | all-to-all | bytes 131072 | tf_op jit(solution)/shard_map/all_to_all | solution.py:663
  34.6 0.8 %finish.1 = (f32[2,8]{1,0:T(2,128)}, f32[2,8]{1,0:T(2,128)}, f32[2,8]{1,0:T(2,128)}) custom-call(f32[128,128]{1,0:T(8,128)S(1)} %bitcast.15, f32[2,4,128]{2,1,0:T(4,128)S(1)} %get-tuple-element.32.packs_ref, f32[2,8]{1,0:T(2,128)S(1)} %get-tuple-element.33.coeffs_ref), custom_call_target="tpu_custom_call" | custom-call | tf_op jit(solution)/shard_map/finish/pallas_call | solution.py:667
Async XLA Ops:
  20.0 1.6 %collective-permute-start = (f32[16,1,4224]{2,1,0:T(1,128)S(1)}, f32[16,1,4224]{2,1,0:T(1,128)S(1)}, u32[]{:S(2)}, u32[]{:S(2)}) collective-permute-start(f32[16,1,4224]{2,1,0:T(1,128)S(1)} %all_to_all.10), channel_id=1, source_target_pairs={{0,1},{1,0},{2,3},{3,2},{4,5},{5,4},{6,7},{7,6},{8,9},{9,8},{10,11... | collective-permute-start | bytes 811016 | tf_op jit(solution)/shard_map/ppermute | solution.py:619

commit v10 on v9

--- a/solution.py
+++ b/solution.py
@@ -156,22 +156,21 @@
         out_ref[o * rows + 2 * cap : (o + 1) * rows, :] = info[o : o + 1, :]
 
 
-def unpack(ranks, cap, ref, phase_ref, cell_ref, info_ref, meta_ref):
+def unpack(ranks, cap, ref):
     rows = 2 * cap + 1
-    for o in range(ranks):
-        here = o * cap
-        phase_ref[here : here + cap, :] = ref[o * rows : o * rows + cap, :]
-        cell_ref[here : here + cap, :] = ref[o * rows + cap : o * rows + 2 * cap, :]
-        info = ref[o * rows + 2 * cap : (o + 1) * rows, :]
-        info_ref[here : here + cap, :] = jnp.broadcast_to(info, (cap, LANES))
-        meta_ref[o : o + 1, :] = info
-
-
-def rank_slots(ranks, cap, meta_ref):
+    starts = range(0, ranks * rows, rows)
+    phase = jnp.concatenate([ref[s : s + cap, :] for s in starts], axis=0)
+    pixel = jnp.concatenate([ref[s + cap : s + 2 * cap, :] for s in starts], axis=0)
+    lines = [ref[s + 2 * cap : s + rows, :] for s in starts]
+    info = jnp.concatenate([jnp.broadcast_to(line, (cap, LANES)) for line in lines], axis=0)
+    return phase, pixel, info, jnp.concatenate(lines, axis=0)
+
+
+def rank_slots(ranks, cap, meta):
     lists = []
     spans = LANES // cap
     for k in range(ranks * cap // LANES):
-        names = meta_ref[k * spans : (k + 1) * spans, :]
+        names = meta[k * spans : (k + 1) * spans, :]
         lane = iota((spans, LANES), 1)
         spread = lane_gather(names, 2 * cap + (lane & (cap - 1)))
         mine = (lane >> log2(cap)) == iota((spans, LANES), 0)
@@ -204,7 +203,7 @@
     return rows
 
 
-def read_knots(ranks, cap, dets, nodes, meta_ref):
+def read_knots(ranks, cap, dets, nodes, meta):
     width = dets * nodes
     knots = ranks * nodes
     per_row = LANES // width
@@ -212,7 +211,7 @@
     for kind in range(2):
         lines = []
         for p in range(ranks // per_row):
-            names = meta_ref[p * per_row : (p + 1) * per_row, :]
+            names = meta[p * per_row : (p + 1) * per_row, :]
             lane = iota((per_row, LANES), 1)
             spread = lane_gather(names, (3 * cap + kind * width) + (lane & (width - 1)))
             here = (lane >> log2(width)) == iota((per_row, LANES), 0)
@@ -232,18 +231,17 @@
     return kinds
 
 
-def source_of(ranks, cap, dets, total, side, phase_ref, cell_ref, info_ref):
+def source_of(ranks, cap, dets, total, side, phase, pixel, info):
     slots = ranks * cap
     slot = iota((slots, LANES), 0) & (cap - 1)
     lane = iota((slots, LANES), 1)
-    listed = lane_gather(info_ref[...], jnp.minimum(lane, 2) * cap + slot)
+    listed = lane_gather(info, jnp.minimum(lane, 2) * cap + slot)
     listed = listed + jnp.where(lane == 1, (side * dets).astype(jnp.float32), 0.0)
-    pixel = cell_ref[...]
     cell = (pixel - jnp.floor(pixel * (1.0 / LANES)) * LANES).astype(jnp.bfloat16)
     whole = split3(listed)
     if max(total, ranks * OWNER_TILES) <= 65536:
         whole = whole[:2]
-    return jnp.concatenate(split3(phase_ref[...]) + (cell,) + whole, axis=1)
+    return jnp.concatenate(split3(phase) + (cell,) + whole, axis=1)
 
 
 def take_slots(at, rank, source, dets, side, tables):
@@ -344,16 +342,15 @@
 def own_kernel(
     ranks, cap, dets, nodes, spacing, own_ref,
     few_phase, few_cell, few_info, table_ref, cos_ref, sin_ref, stream_ref, basis_ref, bin_ref, packs_ref, count_ref,
-    phase_ref, cell_ref, info_ref, meta_ref,
 ):
     knots = ranks * nodes
     side = lax.axis_index("det")
-    unpack(ranks, cap, own_ref, phase_ref, cell_ref, info_ref, meta_ref)
-    rank, number = rank_slots(ranks, cap, meta_ref)
+    phase, pixel, info, meta = unpack(ranks, cap, own_ref)
+    rank, number = rank_slots(ranks, cap, meta)
     count_ref[...] = jnp.full((8, LANES), number, jnp.int32)
-    tables, left = read_knots(ranks, cap, dets, nodes, meta_ref)
+    tables, left = read_knots(ranks, cap, dets, nodes, meta)
     packs_ref[...] = jnp.concatenate(flatten(tables, knots) + flatten(left, knots), axis=0)
-    source = source_of(ranks, cap, dets, knots * spacing, side, phase_ref, cell_ref, info_ref)
+    source = source_of(ranks, cap, dets, knots * spacing, side, phase, pixel, info)
 
     def gather_block(block, carry):
         here = pl.ds(aligned(block * BLOCK, 16), BLOCK)
@@ -385,7 +382,7 @@
 ):
     few_phase, few_cell, few_info, table_ref, cos_ref, sin_ref, stream_ref, basis_ref, bin_ref = refs[9:18]
     out_ref, packs_ref, coeffs_ref = refs[18:21]
-    phase_ref, cell_ref, info_ref, meta_ref, total_ref, turned_ref, knots_ref, sems = refs[21:]
+    total_ref, turned_ref, knots_ref, sems = refs[21:]
     coeffs_copy = pltpu.make_async_copy(coeffs_hbm, coeffs_ref, sems.at[0])
     coeffs_copy.start()
     slots = ranks * cap
@@ -394,17 +391,17 @@
     group = lax.axis_index("det")
     side = 1 - group
 
-    unpack(ranks, cap, other_ref, phase_ref, cell_ref, info_ref, meta_ref)
-    rank, more = rank_slots(ranks, cap, meta_ref)
+    phase, pixel, info, meta = unpack(ranks, cap, other_ref)
+    rank, more = rank_slots(ranks, cap, meta)
     ready = jnp.max(count_ref[...])
     rank = jnp.where(rank >= 0, rank + ready, -1)
     number = ready + more
-    tables, left = read_knots(ranks, cap, dets, nodes, meta_ref)
+    tables, left = read_knots(ranks, cap, dets, nodes, meta)
     for kind, pages in enumerate((tables, left)):
         here = slice(kind * packed, (kind + 1) * packed)
         packs_ref[kind, pl.ds(group * packed, packed), :] = packs_own[here, :]
         packs_ref[kind, pl.ds(side * packed, packed), :] = jnp.concatenate(flatten(pages, knots), axis=0)
-    source = source_of(ranks, cap, dets, knots * spacing, side, phase_ref, cell_ref, info_ref)
+    source = source_of(ranks, cap, dets, knots * spacing, side, phase, pixel, info)
     blocks = block_count(number, 2 * slots)
     ready_blocks = block_count(ready, slots)
 
@@ -545,9 +542,11 @@
 ):
     nodes, dets = coeffs_ref.shape
     height = packs_ref.shape[1]
-    total = arrived_ref[0:height, :]
-    for o in range(1, arrived_ref.shape[0] // height):
-        total = total + arrived_ref[o * height : (o + 1) * height, :]
+    step = max(height, 8)
+    parts = [arrived_ref[r : r + step, :] for r in range(0, arrived_ref.shape[0], step)]
+    while len(parts) > 1:
+        parts = [a + b for a, b in zip(parts[0::2], parts[1::2], strict=True)]
+    total = sum((parts[0][r : r + height, :] for r in range(height, step, height)), parts[0][:height, :])
     search, left = packs_ref[0], packs_ref[1]
     image = total * (1.0 / spacing) + BASE_PRIOR * search
     norm_old = jnp.sum(left * left, keepdims=True)
@@ -626,7 +625,6 @@
         jax.ShapeDtypeStruct((5, room, LANES), f32),
         jax.ShapeDtypeStruct((room * CHANNELS, LANES), f32),
     )
-    arrival = [pltpu.VMEM((slots, LANES), f32)] * 3 + [pltpu.VMEM((ranks, LANES), f32)]
     sizes = (ranks, cap, dets, nodes, spacing)
     *state, packs, count = pl.pallas_call(
         functools.partial(own_kernel, *sizes),
@@ -636,7 +634,6 @@
         ),
         in_specs=[vmem],
         out_specs=(vmem,) * 11,
-        scratch_shapes=arrival,
         compiler_params=params,
         cost_estimate=pl.CostEstimate(flops=4_000_000_000, bytes_accessed=4_000_000, transcendentals=0),
         name="own",
@@ -650,7 +647,7 @@
         ),
         in_specs=[vmem, hbm] + [vmem] * 11,
         out_specs=(vmem,) * 12,
-        scratch_shapes=arrival + [
+        scratch_shapes=[
             pltpu.VMEM((CHANNELS, room, LANES), f32),
             pltpu.VMEM((2, 8, BLOCK), f32),
             pltpu.VMEM((pages, room, LANES), f32),

time: 35.7 us -> 35.5 us (level)
  blocking collectives: 28.4 us -> 27.9 us
    all_to_all x1, blocking collectives: 10.3 us -> 9.8 us  [body(): lax.all_to_all(partials.reshape(ranks * groups, 1, height * LANES), ('tm'...]
    pallas_call x1, Pallas kernels: 1.6 us -> 1.19 us  [body(): pl.pallas_call(functools.partial(own_kernel, *sizes), out_shape=shared +...]
    pallas_call x1, Pallas kernels: 2.66 us -> 3.02 us  [body(): pl.pallas_call(functools.partial(main_kernel, *sizes), out_shape=shared +...]
  transfers between devices with their start and end apart: 1 -> 1, of which waited for: 0 -> 1; matrix products, arithmetic and copies ran while one was open for 0% -> 0% of each run, Pallas kernels for 5% -> 3%
where the time goes in v10:
time: 35.5 us; the launch traced here: 35.2 us
  blocking collectives  27.9 us (79%)
  Pallas kernels  6.31 us (18%)
  between operations  0.66 us (2%)
    all_to_all x1, blocking collectives, body(): lax.all_to_all(outgoing.reshape(ranks, 1, rows * LANES), 'tm', split_axis...  18.1 us
    all_to_all x1, blocking collectives, body(): lax.all_to_all(partials.reshape(ranks * groups, 1, height * LANES), ('tm'...  9.8 us
    pallas_call x1, Pallas kernels, body(): pl.pallas_call(functools.partial(main_kernel, *sizes), out_shape=shared +...  3.02 us
    pallas_call x1, Pallas kernels, body(): pl.pallas_call(functools.partial(send_kernel, ranks, cap), out_shape=jax....  1.27 us
    pallas_call x1, Pallas kernels, body(): pl.pallas_call(functools.partial(own_kernel, *sizes), out_shape=shared +...  1.19 us
    pallas_call x1, Pallas kernels, body(): pl.pallas_call(functools.partial(finish_kernel, ranks, spacing), out_shap...  0.82 us
  transfers between devices with their start and end apart: 1, of which 1 were waited for; matrix products, arithmetic and copies ran while one was open for 0% of the time, Pallas kernels for 3%

profile of v10, /device:TPU:0, one launch (start us, length us, event | category | flops | bytes accessed | tf_op | source)
XLA Modules:
  0.0 35.2 jit_solution(7179773754950603403)
XLA Ops:
  0.6 1.3 %send.1 = f32[528,128]{1,0:T(8,128)S(1)} custom-call(s32[8,16]{1,0:T(8,128)} %patch_hbm.1, s32[1,8]{1,0:T(1,128)} %bitcast.20, f32[2,8]{1,0:T(2,128)} %bitcast.17, f32[2,8]{1,0:T(2,128)} %bitcast.18, s32[8,2048]{1,0:T(8,128)} %cell_hbm.1, f32[8,2048]{1,0:T(8,128)} %phase_hbm.1), custom_call_target="tpu_custom_call" | custom-call | tf_op jit(solution)/shard_map/send/pallas_call | solution.py:604
  1.9 18.1 %all_to_all.10 = f32[16,1,4224]{2,1,0:T(1,128)S(1)} all-to-all(f32[16,1,4224]{2,1,0:T(1,128)S(1)} %bitcast.12), channel_id=1, replica_groups=mesh['tm'=16,'det'=2] {'tm'}, dimensions={0} | all-to-all | bytes 540672 | tf_op jit(solution)/shard_map/all_to_all | solution.py:614
  20.0 0.0 collective-permute-start
  20.1 1.2 %own.1 = (f32[592,128]{1,0:T(8,128)S(1)}, f32[592,128]{1,0:T(8,128)S(1)}, f32[592,128]{1,0:T(8,128)S(1)}, f32[1,592,128]{2,1,0:T(8,128)S(1)}, f32[592,128]{1,0:T...) custom-call(f32[528,128]{1,0:T(8,128)S(1)} %bitcast.14), custom_call_target="tpu_custom_call" | custom-call | flops 4000000000 | bytes 4000000 | tf_op jit(solution)/shard_map/own/pallas_call | solution.py:629
  21.2 0.3 collective-permute-done
  21.6 3.0 %main.1 = (f32[592,128]{1,0:T(8,128)S(1)}, f32[592,128]{1,0:T(8,128)S(1)}, f32[592,128]{1,0:T(8,128)S(1)}, f32[1,592,128]{2,1,0:T(8,128)S(1)}, f32[592,128]{1,0:...) custom-call(f32[528,128]{1,0:T(8,128)S(1)} %bitcast.13, ...), custom_call_target="tpu_custom_call", output_to_operand_aliasing={{0}: (4, {}), {1}: (5, {}), {2}: (6, {}), {3}: (7, {}), {4}... | custom-call | tf_op jit(solution)/shard_map/main/pallas_call | solution.py:641
  24.6 9.8 %all_to_all.11 = f32[32,1,512]{2,1,0:T(1,128)S(1)} all-to-all(f32[32,1,512]{2,1,0:T(1,128)S(1)} %bitcast.16), channel_id=1, replica_groups=mesh['tm'=16,'det'=2] {'tm','det'}, dimensions={0} | all-to-all | bytes 131072 | tf_op jit(solution)/shard_map/all_to_all | solution.py:660
  34.4 0.8 %finish.1 = (f32[2,8]{1,0:T(2,128)}, f32[2,8]{1,0:T(2,128)}, f32[2,8]{1,0:T(2,128)}) custom-call(f32[128,128]{1,0:T(8,128)S(1)} %bitcast.15, f32[2,4,128]{2,1,0:T(4,128)S(1)} %get-tuple-element.32.packs_ref, f32[2,8]{1,0:T(2,128)S(1)} %get-tuple-element.33.coeffs_ref), custom_call_target="tpu_custom_call" | custom-call | tf_op jit(solution)/shard_map/finish/pallas_call | solution.py:664
Async XLA Ops:
  20.0 1.5 %collective-permute-start = (f32[16,1,4224]{2,1,0:T(1,128)S(1)}, f32[16,1,4224]{2,1,0:T(1,128)S(1)}, u32[]{:S(2)}, u32[]{:S(2)}) collective-permute-start(f32[16,1,4224]{2,1,0:T(1,128)S(1)} %all_to_all.10), channel_id=1, source_target_pairs={{0,1},{1,0},{2,3},{3,2},{4,5},{5,4},{6,7},{7,6},{8,9},{9,8},{10,11... | collective-permute-start | bytes 811016 | tf_op jit(solution)/shard_map/ppermute | solution.py:618

commit v11 on v10

--- a/solution.py
+++ b/solution.py
@@ -294,9 +294,8 @@
         sin_ref[pl.ds(at, COLLECT), :] = sine
         stream_ref[pl.ds(at, COLLECT), :] = stream
 
-    down = iota((LANES, 2 * LANES), 0).astype(jnp.float32).astype(jnp.bfloat16)
+    down = iota((LANES, LANES), 0).astype(jnp.float32).astype(jnp.bfloat16)
     channel = iota((CHANNELS, LANES), 0)
-    zeros = jnp.zeros((2 * CHANNELS, LANES), jnp.bfloat16)
 
     def collect(step):
         for k in range(COLLECT // 2):
@@ -316,20 +315,12 @@
                 stack = jnp.concatenate([high, rest], axis=0)
                 pieces.append(stack.astype(jnp.bfloat16))
                 cells.append(jnp.broadcast_to(few_cell[pl.ds(slot, 1), :].astype(jnp.bfloat16), (LANES, LANES)))
-            entry = jnp.concatenate(
-                [
-                    jnp.concatenate([pieces[0], zeros], axis=1),
-                    jnp.concatenate([zeros, pieces[1]], axis=1),
-                ],
-                axis=0,
-            )
-            hits = jnp.where(jnp.concatenate(cells, axis=1) == down, jnp.int8(1), jnp.int8(0))
-            sums = dot(entry, hits.T.astype(jnp.bfloat16))
+            hits = [jnp.where(cell == down, jnp.int8(1), jnp.int8(0)).T.astype(jnp.bfloat16) for cell in cells]
+            sums = dot(jnp.concatenate(pieces, axis=0), jnp.concatenate(hits, axis=1))
             for m in range(2):
                 base = 2 * CHANNELS * m
-                bin_ref[pl.ds((at + m) * CHANNELS, CHANNELS), :] = (
-                    sums[base : base + CHANNELS] + sums[base + CHANNELS : base + 2 * CHANNELS]
-                )
+                mine = sums[base : base + 2 * CHANNELS, m * LANES : (m + 1) * LANES]
+                bin_ref[pl.ds((at + m) * CHANNELS, CHANNELS), :] = mine[:CHANNELS] + mine[CHANNELS:]
 
     def both(step, carry):
         collect(step)

time: 35.5 us -> 35.6 us (level)
  Pallas kernels: 6.31 us -> 6.67 us
    pallas_call x1, Pallas kernels: 1.19 us -> 1.56 us  [body(): pl.pallas_call(functools.partial(own_kernel, *sizes), out_shape=shared +...]
  transfers between devices with their start and end apart: 1 -> 1, of which waited for: 1 -> 0; matrix products, arithmetic and copies ran while one was open for 0% -> 0% of each run, Pallas kernels for 3% -> 4%
where the time goes in v11:
time: 35.6 us; the launch traced here: 35.4 us
  blocking collectives  28 us (79%)
  Pallas kernels  6.67 us (19%)
  between operations  0.67 us (2%)
    all_to_all x1, blocking collectives, body(): lax.all_to_all(outgoing.reshape(ranks, 1, rows * LANES), 'tm', split_axis...  18.1 us
    all_to_all x1, blocking collectives, body(): lax.all_to_all(partials.reshape(ranks * groups, 1, height * LANES), ('tm'...  9.89 us
    pallas_call x1, Pallas kernels, body(): pl.pallas_call(functools.partial(main_kernel, *sizes), out_shape=shared +...  3.02 us
    pallas_call x1, Pallas kernels, body(): pl.pallas_call(functools.partial(own_kernel, *sizes), out_shape=shared +...  1.56 us
    pallas_call x1, Pallas kernels, body(): pl.pallas_call(functools.partial(send_kernel, ranks, cap), out_shape=jax....  1.27 us
    pallas_call x1, Pallas kernels, body(): pl.pallas_call(functools.partial(finish_kernel, ranks, spacing), out_shap...  0.82 us
  transfers between devices with their start and end apart: 1, of which 0 were waited for; matrix products, arithmetic and copies ran while one was open for 0% of the time, Pallas kernels for 4%

profile of v11, /device:TPU:0, one launch (start us, length us, event | category | flops | bytes accessed | tf_op | source)
XLA Modules:
  0.0 35.4 jit_solution(720239397977465251)
XLA Ops:
  0.6 1.3 %send.1 = f32[528,128]{1,0:T(8,128)S(1)} custom-call(s32[8,16]{1,0:T(8,128)} %patch_hbm.1, s32[1,8]{1,0:T(1,128)} %bitcast.20, f32[2,8]{1,0:T(2,128)} %bitcast.17, f32[2,8]{1,0:T(2,128)} %bitcast.18, s32[8,2048]{1,0:T(8,128)} %cell_hbm.1, f32[8,2048]{1,0:T(8,128)} %phase_hbm.1), custom_call_target="tpu_custom_call" | custom-call | tf_op jit(solution)/shard_map/send/pallas_call | solution.py:595
  1.9 18.1 %all_to_all.10 = f32[16,1,4224]{2,1,0:T(1,128)S(1)} all-to-all(f32[16,1,4224]{2,1,0:T(1,128)S(1)} %bitcast.12), channel_id=1, replica_groups=mesh['tm'=16,'det'=2] {'tm'}, dimensions={0} | all-to-all | bytes 540672 | tf_op jit(solution)/shard_map/all_to_all | solution.py:605
  20.0 0.0 collective-permute-start
  20.1 1.6 %own.1 = (f32[592,128]{1,0:T(8,128)S(1)}, f32[592,128]{1,0:T(8,128)S(1)}, f32[592,128]{1,0:T(8,128)S(1)}, f32[1,592,128]{2,1,0:T(8,128)S(1)}, f32[592,128]{1,0:T...) custom-call(f32[528,128]{1,0:T(8,128)S(1)} %bitcast.14), custom_call_target="tpu_custom_call" | custom-call | flops 4000000000 | bytes 4000000 | tf_op jit(solution)/shard_map/own/pallas_call | solution.py:620
  21.6 0.0 collective-permute-done
  21.6 3.0 %main.1 = (f32[592,128]{1,0:T(8,128)S(1)}, f32[592,128]{1,0:T(8,128)S(1)}, f32[592,128]{1,0:T(8,128)S(1)}, f32[1,592,128]{2,1,0:T(8,128)S(1)}, f32[592,128]{1,0:...) custom-call(f32[528,128]{1,0:T(8,128)S(1)} %bitcast.13, ...), custom_call_target="tpu_custom_call", output_to_operand_aliasing={{0}: (4, {}), {1}: (5, {}), {2}: (6, {}), {3}: (7, {}), {4}... | custom-call | tf_op jit(solution)/shard_map/main/pallas_call | solution.py:632
  24.7 9.9 %all_to_all.11 = f32[32,1,512]{2,1,0:T(1,128)S(1)} all-to-all(f32[32,1,512]{2,1,0:T(1,128)S(1)} %bitcast.16), channel_id=1, replica_groups=mesh['tm'=16,'det'=2] {'tm','det'}, dimensions={0} | all-to-all | bytes 131072 | tf_op jit(solution)/shard_map/all_to_all | solution.py:651
  34.5 0.8 %finish.1 = (f32[2,8]{1,0:T(2,128)}, f32[2,8]{1,0:T(2,128)}, f32[2,8]{1,0:T(2,128)}) custom-call(f32[128,128]{1,0:T(8,128)S(1)} %bitcast.15, f32[2,4,128]{2,1,0:T(4,128)S(1)} %get-tuple-element.32.packs_ref, f32[2,8]{1,0:T(2,128)S(1)} %get-tuple-element.33.coeffs_ref), custom_call_target="tpu_custom_call" | custom-call | tf_op jit(solution)/shard_map/finish/pallas_call | solution.py:655
Async XLA Ops:
  20.0 1.6 %collective-permute-start = (f32[16,1,4224]{2,1,0:T(1,128)S(1)}, f32[16,1,4224]{2,1,0:T(1,128)S(1)}, u32[]{:S(2)}, u32[]{:S(2)}) collective-permute-start(f32[16,1,4224]{2,1,0:T(1,128)S(1)} %all_to_all.10), channel_id=1, source_target_pairs={{0,1},{1,0},{2,3},{3,2},{4,5},{5,4},{6,7},{7,6},{8,9},{9,8},{10,11... | collective-permute-start | bytes 811016 | tf_op jit(solution)/shard_map/ppermute | solution.py:609

commit v12 on v9

--- a/solution.py
+++ b/solution.py
@@ -296,7 +296,7 @@
         sin_ref[pl.ds(at, COLLECT), :] = sine
         stream_ref[pl.ds(at, COLLECT), :] = stream
 
-    down = iota((LANES, 2 * LANES), 0).astype(jnp.float32).astype(jnp.bfloat16)
+    down = iota((LANES, 2 * LANES), 0).astype(jnp.int8)
     channel = iota((CHANNELS, LANES), 0)
     zeros = jnp.zeros((2 * CHANNELS, LANES), jnp.bfloat16)
 
@@ -317,7 +317,7 @@
                 rest = entry - high
                 stack = jnp.concatenate([high, rest], axis=0)
                 pieces.append(stack.astype(jnp.bfloat16))
-                cells.append(jnp.broadcast_to(few_cell[pl.ds(slot, 1), :].astype(jnp.bfloat16), (LANES, LANES)))
+                cells.append(jnp.broadcast_to(few_cell[pl.ds(slot, 1), :].astype(jnp.int32).astype(jnp.int8), (LANES, LANES)))
             entry = jnp.concatenate(
                 [
                     jnp.concatenate([pieces[0], zeros], axis=1),

time: 35.7 us -> 35.7 us (level)
  blocking collectives: 28.4 us -> 28 us
  Pallas kernels: 6.38 us -> 6.75 us
    all_to_all x1, blocking collectives: 10.3 us -> 9.88 us  [body(): lax.all_to_all(partials.reshape(ranks * groups, 1, height * LANES), ('tm'...]
    pallas_call x1, Pallas kernels: 2.66 us -> 3.03 us  [body(): pl.pallas_call(functools.partial(main_kernel, *sizes), out_shape=shared +...]
where the time goes in v12:
time: 35.7 us; the launch traced here: 35.4 us
  blocking collectives  28 us (78%)
  Pallas kernels  6.75 us (19%)
  between operations  0.67 us (2%)
    all_to_all x1, blocking collectives, body(): lax.all_to_all(outgoing.reshape(ranks, 1, rows * LANES), 'tm', split_axis...  18.1 us
    all_to_all x1, blocking collectives, body(): lax.all_to_all(partials.reshape(ranks * groups, 1, height * LANES), ('tm'...  9.88 us
    pallas_call x1, Pallas kernels, body(): pl.pallas_call(functools.partial(main_kernel, *sizes), out_shape=shared +...  3.03 us
    pallas_call x1, Pallas kernels, body(): pl.pallas_call(functools.partial(own_kernel, *sizes), out_shape=shared +...  1.6 us
    pallas_call x1, Pallas kernels, body(): pl.pallas_call(functools.partial(send_kernel, ranks, cap), out_shape=jax....  1.27 us
    pallas_call x1, Pallas kernels, body(): pl.pallas_call(functools.partial(finish_kernel, ranks, spacing), out_shap...  0.85 us
  transfers between devices with their start and end apart: 1, of which 0 were waited for; matrix products, arithmetic and copies ran while one was open for 0% of the time, Pallas kernels for 5%

profile of v12, /device:TPU:0, one launch (start us, length us, event | category | flops | bytes accessed | tf_op | source)
XLA Modules:
  0.0 35.4 jit_solution(1884399658197846251)
XLA Ops:
  0.6 1.3 %send.1 = f32[528,128]{1,0:T(8,128)S(1)} custom-call(s32[8,16]{1,0:T(8,128)} %patch_hbm.1, s32[1,8]{1,0:T(1,128)} %bitcast.20, f32[2,8]{1,0:T(2,128)} %bitcast.17, f32[2,8]{1,0:T(2,128)} %bitcast.18, s32[8,2048]{1,0:T(8,128)} %cell_hbm.1, f32[8,2048]{1,0:T(8,128)} %phase_hbm.1), custom_call_target="tpu_custom_call" | custom-call | tf_op jit(solution)/shard_map/send/pallas_call | solution.py:605
  1.9 18.1 %all_to_all.10 = f32[16,1,4224]{2,1,0:T(1,128)S(1)} all-to-all(f32[16,1,4224]{2,1,0:T(1,128)S(1)} %bitcast.12), channel_id=1, replica_groups=mesh['tm'=16,'det'=2] {'tm'}, dimensions={0} | all-to-all | bytes 540672 | tf_op jit(solution)/shard_map/all_to_all | solution.py:615
  20.0 0.0 collective-permute-start
  20.1 1.6 %own.1 = (f32[592,128]{1,0:T(8,128)S(1)}, f32[592,128]{1,0:T(8,128)S(1)}, f32[592,128]{1,0:T(8,128)S(1)}, f32[1,592,128]{2,1,0:T(8,128)S(1)}, f32[592,128]{1,0:T...) custom-call(f32[528,128]{1,0:T(8,128)S(1)} %bitcast.14), custom_call_target="tpu_custom_call" | custom-call | flops 4000000000 | bytes 4000000 | tf_op jit(solution)/shard_map/own/pallas_call | solution.py:631
  21.7 0.0 collective-permute-done
  21.7 3.0 %main.1 = (f32[592,128]{1,0:T(8,128)S(1)}, f32[592,128]{1,0:T(8,128)S(1)}, f32[592,128]{1,0:T(8,128)S(1)}, f32[1,592,128]{2,1,0:T(8,128)S(1)}, f32[592,128]{1,0:...) custom-call(f32[528,128]{1,0:T(8,128)S(1)} %bitcast.13, ...), custom_call_target="tpu_custom_call", output_to_operand_aliasing={{0}: (4, {}), {1}: (5, {}), {2}: (6, {}), {3}: (7, {}), {4}... | custom-call | tf_op jit(solution)/shard_map/main/pallas_call | solution.py:644
  24.7 9.9 %all_to_all.11 = f32[32,1,512]{2,1,0:T(1,128)S(1)} all-to-all(f32[32,1,512]{2,1,0:T(1,128)S(1)} %bitcast.16), channel_id=1, replica_groups=mesh['tm'=16,'det'=2] {'tm','det'}, dimensions={0} | all-to-all | bytes 131072 | tf_op jit(solution)/shard_map/all_to_all | solution.py:663
  34.6 0.8 %finish.1 = (f32[2,8]{1,0:T(2,128)}, f32[2,8]{1,0:T(2,128)}, f32[2,8]{1,0:T(2,128)}) custom-call(f32[128,128]{1,0:T(8,128)S(1)} %bitcast.15, f32[2,4,128]{2,1,0:T(4,128)S(1)} %get-tuple-element.32.packs_ref, f32[2,8]{1,0:T(2,128)S(1)} %get-tuple-element.33.coeffs_ref), custom_call_target="tpu_custom_call" | custom-call | tf_op jit(solution)/shard_map/finish/pallas_call | solution.py:667
Async XLA Ops:
  20.0 1.6 %collective-permute-start = (f32[16,1,4224]{2,1,0:T(1,128)S(1)}, f32[16,1,4224]{2,1,0:T(1,128)S(1)}, u32[]{:S(2)}, u32[]{:S(2)}) collective-permute-start(f32[16,1,4224]{2,1,0:T(1,128)S(1)} %all_to_all.10), channel_id=1, source_target_pairs={{0,1},{1,0},{2,3},{3,2},{4,5},{5,4},{6,7},{7,6},{8,9},{9,8},{10,11... | collective-permute-start | bytes 811016 | tf_op jit(solution)/shard_map/ppermute | solution.py:619
